TPU v7x, 128 devices: a whole 4x4x4 slice. The times are simulated.
128 devices in a mesh: tm: 8 (over x, y_hi), space: 16 (over y_lo, z, core).
Axes of the slice: x: 4, y: 4 (y_hi: 2, y_lo: 2; y = y_hi * 2 + y_lo), z: 4, core: 2. Of those that a mesh axis runs over, the one named last changes fastest.
Arguments:
- video: bfloat16 [32, 32, 24, 3072], P('tm', 'space'), may hold values from -6 to 6
- w_qkv: bfloat16 [3072, 16, 384], P(None, 'space'), may hold values from -0.109375 to 0.109375
- w_out: bfloat16 [16, 128, 3072], P('space'), may hold values from -0.5 to 0.5
- q_gain: float32 [128], replicated, may hold values from 1 to 8
- k_gain: float32 [128], replicated, may hold values from 1 to 8
- tile_perm: int32 [8, 3072], P('tm'), may hold values from 0 to 3071, as said below
- window: int32 [12, 6], replicated, may hold values from 0 to 11, as said below
Outputs:
- mixed: bfloat16 [8, 3072, 3072], P('tm', 'space')
Inputs may be any that keep to these rules, and one draw needn't show every extreme that they name: `tile_perm`: each row is a permutation of the slots of one frame group in which slots t*256 to t*256 + 255 hold exactly the tokens of tile t; tile t covers frames of the group, rows (t // 3) * 8 onward and columns (t % 3) * 8 onward, 8 and 8 of them. `window`: row t holds 6 different tiles, the first being t.
All inputs are finite; a program needn't handle non-finite values.
Results may differ from a plain program's by a relative error of at most 0.023.
The roundings to bfloat16 on the way count: a program that leaves them out, or rounds other values in their place, can miss the bound.
Values may be sent and summed in bfloat16 or wider, within the bound.
No kernel may reach another device: no remote copies, remote signals or barrier semaphores. Data moves between devices by JAX's collectives and lax.ppermute only.
A program may use at most 128 MiB of HBM per device.

v0:
```python
import jax
import jax.numpy as jnp
from jax import lax
from jax.sharding import PartitionSpec as P

TT = 4
TH = 8
TW = 8


def extended(cells, sides, width):
    for axis, dim in sides:
        count = lax.axis_size(axis)
        ends = count - 1
        head = lax.slice_in_dim(cells, 0, width, axis=dim)
        tail = lax.slice_in_dim(cells, cells.shape[dim] - width, cells.shape[dim], axis=dim)
        cells = jnp.concatenate(
            [
                lax.ppermute(tail, axis, [(i, (i + 1) % count) for i in range(ends)]),
                cells,
                lax.ppermute(head, axis, [((i + 1) % count, i) for i in range(ends)]),
            ],
            axis=dim,
        )
    return cells


def head_norm(values, gain):
    wide = values.astype(jnp.float32)
    scaled = wide * lax.rsqrt(jnp.mean(wide * wide, axis=-1, keepdims=True) + 1e-06)
    return (scaled * gain).astype(jnp.bfloat16)


def attend(queries, chosen, valid):
    heads_here = queries.shape[1]
    head_dim = queries.shape[2]
    span = chosen.shape[1] * chosen.shape[2]
    keys = chosen[:, :, :, :, 0, :].reshape(-1, heads_here, head_dim)
    values = chosen[:, :, :, :, 1, :].reshape(-1, heads_here, head_dim)
    scores = jnp.einsum(
        "qhd,khd->hqk", queries, keys, preferred_element_type=jnp.float32
    ) * head_dim ** (-0.5)
    live = jnp.repeat(valid, span)
    scores = jnp.where(live[None, None, :], scores, -jnp.inf)
    highest = jnp.max(scores, axis=-1, keepdims=True)
    weights = jnp.exp(scores - highest)
    probs = (weights / jnp.sum(weights, axis=-1, keepdims=True)).astype(jnp.bfloat16)
    result = jnp.einsum("hqk,khd->qhd", probs, values, preferred_element_type=jnp.float32)
    return result.astype(jnp.bfloat16)


def per_device(video, w_qkv, w_out, q_gain, k_gain, tile_perm, window):
    frames_here = video.shape[0]
    cols_here = video.shape[2]
    model_dim = video.shape[3]
    heads_here = w_qkv.shape[1]
    head_dim = w_out.shape[1]
    flat_w = w_qkv.reshape(model_dim, heads_here * 3 * head_dim)
    qkv = jnp.einsum(
        "frwd,dc->frwc",
        lax.all_gather(video, "space", axis=1, tiled=True),
        flat_w,
        preferred_element_type=jnp.float32,
    ).astype(jnp.bfloat16)
    group_tokens = frames_here * qkv.shape[1] * cols_here
    qkv = qkv.reshape(group_tokens, heads_here, 3, head_dim)
    ordered = jnp.take(qkv, tile_perm[0], axis=0)
    queries = head_norm(ordered[:, :, 0, :], q_gain)
    keys = head_norm(ordered[:, :, 1, :], k_gain)
    pairs = jnp.stack([keys, ordered[:, :, 2, :]], axis=2)
    beside_all = extended(pairs[None], (("tm", 0),), 1)
    tile_tokens = TT * TH * TW
    tile_count = group_tokens // tile_tokens
    beside_all = beside_all.reshape(3, tile_count, tile_tokens, heads_here, 2, head_dim)
    position = lax.axis_index("tm")
    valid = jnp.stack([position > 0, position >= 0, position < lax.axis_size("tm") - 1])
    query_tiles = queries.reshape(tile_count, tile_tokens, heads_here, head_dim)

    def one_tile(item):
        block, picks = item
        return attend(block, jnp.take(beside_all, picks, axis=1), valid)

    attn = lax.map(one_tile, (query_tiles, window)).reshape(group_tokens, heads_here, head_dim)
    flat_attn = attn.reshape(group_tokens, heads_here * head_dim)
    flat_out = w_out.reshape(heads_here * head_dim, model_dim)
    product = jnp.dot(flat_attn, flat_out, preferred_element_type=jnp.float32)
    summed = lax.psum_scatter(
        lax.optimization_barrier(product.astype(jnp.bfloat16))
        .astype(jnp.float32)
        .astype(jnp.bfloat16),
        "space",
        scatter_dimension=0,
        tiled=True,
    )
    return summed[None]


def solution(mesh):
    in_specs = (
        P("tm", "space", None, None),
        P(None, "space", None),
        P("space", None, None),
        P(),
        P(),
        P("tm", None),
        P(),
    )
    out_specs = P("tm", "space", None)
    return jax.shard_map(
        per_device, mesh=mesh, in_specs=in_specs, out_specs=out_specs, check_vma=False
    )
```

profile of v0, /device:TPU:0, one launch (start us, length us, event | category | flops | bytes accessed | tf_op | source)
XLA Modules:
  0.0 464.7 jit_solution(13269403749948973810)
XLA Ops:
  8.8 104.3 %all-gather.2.cloned.1.call-done = bf16[4,32,24,3072]{3,2,1,0:T(8,128)(2,1)} async-done(((bf16[4,2,24,3072]{3,2,1,0:T(8,128)(2,1)}), bf16[4,32,24,3072]{3,2,1,0:T(8,128)(2,1)}) %all-gather.2.cloned.1.call-update) | async-done | bytes 18874384 | tf_op jit(solution)/shard_map/all_gather | solution.py:61
  113.0 14.9 %fusion.11 = bf16[4,32,24,384]{3,2,1,0:T(8,128)(2,1)} fusion(bf16[4,32,24,3072]{3,2,1,0:T(8,128)(2,1)} %all-gather.2.cloned.1.call-done, bf16[3072,1,384]{2,0,1:T(8,128)(2,1)S(1)} %copy-done), kind=kOutput, calls=%fused_computation.26 | convolution fusion | flops 7248936960 | bytes 23592960 | tf_op jit(solution)/shard_map/frwd,dc->frwc/dot_general | solution.py:59
  128.0 7.0 %reshape.274 = bf16[3072,3,128]{2,1,0:T(4,128)(2,1)} reshape(bf16[4,32,24,384]{3,2,1,0:T(8,128)(2,1)} %fusion.11) | data formatting | bytes 4718592 | tf_op jit(solution)/shard_map/reshape | solution.py:66
  135.0 23.3 %gather_fusion.1 = bf16[3072,3,128]{2,1,0:T(4,128)(2,1)} fusion(bf16[3072,3,128]{2,1,0:T(4,128)(2,1)} %reshape.274, s32[3072]{0:T(1024)S(1)} %broadcast_clamp_fusion), kind=kCustom, calls=%fused_computation.1 | custom fusion | bytes 4730880 | tf_op jit(solution)/shard_map/jit(_take)/gather | solution.py:67
  158.3 3.7 bitcast_select_fusion.1
  162.9 1.3 slice_convert_fusion
  164.7 1.4 pad_maximum_fusion.1
  166.1 6.1 %collective-permute-start = (bf16[1,3072,1,2,128]{4,1,3,2,0:T(8,128)(2,1)}, bf16[1,3072,1,2,128]{4,1,3,2,0:T(8,128)(2,1)}, u32[]{:S(2)}, u32[]{:S(2)}) collective-permute-start(bf16[1,3072,1,2,128]{4,1,3,2,0:T(8,128)(2,1)} %get-tuple-element.89), channel_id=1, source_target_pairs={{0,16},{16,32},{32,48},{48,64},{64,80},{80,96},{96,112},{1,17},{17... | collective-permute-start | bytes 4718600 | tf_op jit(solution)/shard_map/ppermute | solution.py:19
  172.2 1.5 collective-permute-start.1
  173.9 1.9 multiply_convert_fusion
  175.7 63.3 %collective-permute-done = bf16[1,3072,1,2,128]{4,1,3,2,0:T(8,128)(2,1)} collective-permute-done((bf16[1,3072,1,2,128]{4,1,3,2,0:T(8,128)(2,1)}, bf16[1,3072,1,2,128]{4,1,3,2,0:T(8,128)(2,1)}, u32[]{:S(2)}, u32[]{:S(2)}) %collective-permute-start) | collective-permute-done | bytes 1572896 | tf_op jit(solution)/shard_map/ppermute | solution.py:19
  239.1 2.1 pad_maximum_fusion
  241.2 2.4 copy.41
  243.7 92.5 %while.10 = (s32[]{:T(128)}, bf16[12,256,1,128]{3,1,0,2:T(8,128)(2,1)}, s32[12,6]{1,0:T(8,128)S(1)}, bf16[3,12,256,1,2,128]{5,2,4,1,0,3:T(8,128)(2,1)}, pred[3]{...) while((s32[]{:T(128)}, bf16[12,256,1,128]{3,1,0,2:T(8,128)(2,1)}, ...), condition=%wide.region_5.6_spmd, body=%wide.region_2.0_spmd.sunk | while | flops 614629952 | bytes 35811552 | solution.py:83
  243.7 3.3 gather_fusion
  251.4 3.3 gather_fusion
  257.2 1.1 fusion.38
  259.1 3.3 gather_fusion
  264.9 1.1 fusion.38
  266.8 3.3 gather_fusion
  272.6 1.1 fusion.38
  274.5 3.3 gather_fusion
  280.3 1.1 fusion.38
  282.2 3.3 gather_fusion
  289.9 3.3 gather_fusion
  297.6 3.3 gather_fusion
  305.3 3.3 gather_fusion
  313.0 3.3 gather_fusion
  320.7 3.3 gather_fusion
  328.4 3.3 gather_fusion
  336.1 10.4 %convolution_convert_fusion = bf16[3072,3072]{1,0:T(8,128)(2,1)} fusion(bf16[3072,128]{1,0:T(8,128)(2,1)} %bitcast.88, bf16[1,128,3072]{2,1,0:T(8,128)(2,1)} %param.11), kind=kOutput, calls=%fused_computation.21 | convolution fusion | flops 2425356288 | bytes 20447232 | tf_op jit(solution)/shard_map/dot_general | solution.py:86
  346.6 111.2 %reduce-scatter.2.cloned.1.call-done = bf16[192,3072]{1,0:T(8,128)(2,1)} async-done(((bf16[3072,3072]{1,0:T(8,128)(2,1)}), bf16[192,3072]{1,0:T(8,128)(2,1)}) %reduce-scatter.2.cloned.1.call-update) | async-done | bytes 1179664 | tf_op jit(solution)/shard_map/reduce_scatter | solution.py:87
  (189 shorter events, 51.0 us)
Async XLA Ops:
  6.5 106.5 %copy-start = (bf16[3072,1,384]{2,0,1:T(8,128)(2,1)S(1)}, bf16[3072,1,384]{2,0,1:T(8,128)(2,1)}, u32[]{:S(2)}) copy-start(bf16[3072,1,384]{2,0,1:T(8,128)(2,1)} %param.10) | copy-start | bytes 7077892
  6.5 106.5 %all-gather.2.cloned.1.call-start = ((), (), s32[]{:S(2)}) async-start(), calls=%async_computation.1 | async-start | bytes 20054016 | tf_op jit(solution)/shard_map/all_gather | solution.py:61
  7.3 450.6 %reduce-scatter.2.cloned.1.call-start = ((), (), s32[]{:S(2)}) async-start(), calls=%async_computation.2 | async-start | bytes 20054016 | tf_op jit(solution)/shard_map/reduce_scatter | solution.py:87
  162.9 1.3 copy-start.3
  164.7 9.0 %copy-start.2 = (s32[12,6]{0,1:T(8,128)S(1)}, s32[12,6]{0,1:T(8,128)}, u32[]{:S(2)}) copy-start(s32[12,6]{0,1:T(8,128)} %param.15) | copy-start | bytes 868
  164.7 9.1 %copy-start.4 = (f32[128]{0:T(128)S(1)}, f32[128]{0:T(128)}, u32[]{:S(2)}) copy-start(f32[128]{0:T(128)} %param.12) | copy-start | bytes 1540
  166.1 73.0 %collective-permute-start = (bf16[1,3072,1,2,128]{4,1,3,2,0:T(8,128)(2,1)}, bf16[1,3072,1,2,128]{4,1,3,2,0:T(8,128)(2,1)}, u32[]{:S(2)}, u32[]{:S(2)}) collective-permute-start(bf16[1,3072,1,2,128]{4,1,3,2,0:T(8,128)(2,1)} %get-tuple-element.89), channel_id=1, source_target_pairs={{0,16},{16,32},{32,48},{48,64},{64,80},{80,96},{96,112},{1,17},{17... | collective-permute-start | bytes 4718600 | tf_op jit(solution)/shard_map/ppermute | solution.py:19
  172.2 66.9 %collective-permute-start.1 = (bf16[1,3072,1,2,128]{4,1,3,2,0:T(8,128)(2,1)}, bf16[1,3072,1,2,128]{4,1,3,2,0:T(8,128)(2,1)}, u32[]{:S(2)}, u32[]{:S(2)}) collective-permute-start(bf16[1,3072,1,2,128]{4,1,3,2,0:T(8,128)(2,1)} %get-tuple-element.89), channel_id=1, source_target_pairs={{16,0},{32,16},{48,32},{64,48},{80,64},{96,80},{112,96},{17,1},{33... | collective-permute-start | bytes 4718600 | tf_op jit(solution)/shard_map/ppermute | solution.py:21
  346.6 111.2 %copy-start.1 = (bf16[3072,1,384]{2,0,1:T(8,128)(2,1)S(1)}, bf16[3072,1,384]{2,0,1:T(8,128)(2,1)}, u32[]{:S(2)}) copy-start(bf16[3072,1,384]{2,0,1:T(8,128)(2,1)} %param.10) | copy-start | bytes 7077892
Sparse Core Ops, SparseCore 0:
  9.0 103.9 all-gather.1
  346.7 111.0 reduce-scatter.1
where the time goes:
time: 466 us; the launch traced here: 465 us
  waiting for transfers between devices  280 us (60%)
  local copies, waits for them, and re-layouts  87.4 us (19%)
  matrix products  49.4 us (11%)
  other arithmetic  26.5 us (6%)
  between operations  13.5 us (3%)
  starting transfers between devices  7.58 us (2%)
    reduce_scatter x1, waiting for transfers between devices, per_device(): lax.psum_scatter(lax.optimization_barrier(product.astype(jnp.bfloat16)).a...  111 us
    all_gather x1, waiting for transfers between devices, per_device(): lax.all_gather(video, 'space', axis=1, tiled=True)  104 us
    ppermute x1, waiting for transfers between devices, extended(): lax.ppermute(tail, axis, [(i, (i + 1) % count) for i in range(ends)])  63.3 us
    gather x12, local copies, waits for them, and re-layouts, one_tile(): return attend(block, jnp.take(beside_all, picks, axis=1), valid)  40 us
    gather x1, local copies, waits for them, and re-layouts, per_device(): ordered = jnp.take(qkv, tile_perm[0], axis=0)  23.3 us
    dot_general x1, matrix products, per_device(): jnp.einsum('frwd,dc->frwc', lax.all_gather(video, 'space', axis=1, tiled=...  14.9 us
    dot_general x12, matrix products, attend(): jnp.einsum('hqk,khd->qhd', probs, values, preferred_element_type=jnp.floa...  13.6 us
    dot_general x12, matrix products, attend(): jnp.einsum('qhd,khd->hqk', queries, keys, preferred_element_type=jnp.floa...  10.5 us
  transfers between devices with their start and end apart: 4, of which 3 were waited for; matrix products, arithmetic and copies ran while one was open for 1% of the time, Pallas kernels for 0%

commit v1 on v0

v1 whole, which is shorter than its diff:
```python
import jax
import jax.numpy as jnp
from jax import lax
from jax.experimental import pallas as pl
from jax.experimental.pallas import tpu as pltpu
from jax.sharding import Mesh
from jax.sharding import PartitionSpec as P

D = 3072
HD = 128
NT = 12
TILE = 256
WIN = 6
AXES = ("x", "yh", "yl", "z", "c")
SIZES = (4, 2, 2, 4, 2)
VMEM = 56 * 1024 * 1024


def move(value, target):
    pairs = []
    for x in range(4):
        for y in range(4):
            for z in range(4):
                for c in range(2):
                    goal = target(x, y, z, c)
                    if goal is None:
                        continue
                    a, b, d, e = goal
                    pairs.append(
                        (((x * 4 + y) * 4 + z) * 2 + c, ((a * 4 + b % 4) * 4 + d) * 2 + e)
                    )
    return lax.ppermute(value, AXES, pairs)


def across(k):
    return lambda x, y, z, c: (x, y, z ^ k, c)


def swap_core(x, y, z, c):
    return (x, y, z, 1 - c)


def up(x, y, z, c):
    return (x, y + 1, z, c)


def down(x, y, z, c):
    return (x, y - 1, z, c)


def regroup(k):
    return lambda x, y, z, c: (x, 2 * c + ((y & 1) ^ k), z, y >> 1)


def beside(x, y, z, c):
    if c == 1:
        return (x + 1, y, z, 0) if x < 3 else None
    return (x - 1, y, z, 1) if x > 0 else None


def normed(part, gain):
    wide = part.astype(jnp.float32)
    mean = jnp.mean(wide * wide, axis=-1, keepdims=True)
    return (wide * lax.rsqrt(mean + 1e-06) * gain).astype(jnp.bfloat16)


def project_body(rows, places, aliased, *refs):
    count = len(rows)
    xs = refs[:count]
    own_w, low_w, high_w, gain_q, gain_k = refs[count : count + 5]
    refs = refs[count + 5 + (4 if aliased else 0) :]
    outs = refs[:4]
    x_buf, w_buf, stage, x_sem, w_sem, out_sem = refs[4:]
    half = D // 2
    w_copies = [
        pltpu.make_async_copy(own_w, w_buf.at[:, 0:384], w_sem.at[0]),
        pltpu.make_async_copy(low_w, w_buf.at[0:half, 384:768], w_sem.at[1]),
        pltpu.make_async_copy(high_w, w_buf.at[half:D, 384:768], w_sem.at[2]),
    ]
    for copy in w_copies:
        copy.start()
    x_copies = []
    for i in range(count):
        copy = pltpu.make_async_copy(xs[i], x_buf.at[i, 0 : rows[i]], x_sem.at[i])
        copy.start()
        x_copies.append(copy)
    for copy in w_copies:
        copy.wait()
    out_copies = []
    for i in range(count):
        x_copies[i].wait()
        n = rows[i]
        lines = n // 24
        y = jnp.dot(x_buf[i, 0:n], w_buf[...], preferred_element_type=jnp.float32)
        y = y.astype(jnp.bfloat16)
        for h in range(2):
            q = normed(y[:, h * 384 : h * 384 + 128], gain_q[...])
            k = normed(y[:, h * 384 + 128 : h * 384 + 256], gain_k[...])
            v = y[:, h * 384 + 256 : h * 384 + 384]
            for value, base in ((q, 0), (k, 128), (v, 256)):
                tall = value.astype(jnp.float32).reshape(lines, 3, 8, 128)
                for tc in range(3):
                    stage[i, h, tc, 0 : lines * 8, base : base + 128] = (
                        tall[:, tc].reshape(lines * 8, 128).astype(jnp.bfloat16)
                    )
        row, blk, off = places[i]
        for h in range(2):
            for tc in range(3):
                for j, (lo, hi) in enumerate(((0, 128), (128, 384))):
                    copy = pltpu.make_async_copy(
                        stage.at[i, h, tc, 0 : lines * 8, lo:hi],
                        outs[2 * h + j].at[row, tc, blk, off : off + lines * 8],
                        out_sem.at[i],
                    )
                    copy.start()
                    out_copies.append(copy)
    for copy in out_copies:
        copy.wait()


def project(xs, places, own_w, low_w, high_w, gain_q, gain_k, previous=None):
    rows = [x.shape[0] for x in xs]
    count = len(xs)
    any_spec = pl.BlockSpec(memory_space=pl.ANY)
    vmem_spec = pl.BlockSpec(memory_space=pltpu.VMEM)
    shapes = []
    for _ in range(2):
        shapes.append(jax.ShapeDtypeStruct((2, 3, 4, 64, 128), jnp.bfloat16))
        shapes.append(jax.ShapeDtypeStruct((2, 3, 4, 64, 256), jnp.bfloat16))
    extra = [] if previous is None else list(previous)

    def body(*refs):
        project_body(rows, places, previous is not None, *refs)

    return pl.pallas_call(
        body,
        out_shape=shapes,
        in_specs=[any_spec] * (count + 3) + [vmem_spec] * 2 + [any_spec] * len(extra),
        out_specs=[any_spec] * 4,
        scratch_shapes=[
            pltpu.VMEM((count, max(rows), D), jnp.bfloat16),
            pltpu.VMEM((D, 768), jnp.bfloat16),
            pltpu.VMEM((count, 2, 3, 64, 384), jnp.bfloat16),
            pltpu.SemaphoreType.DMA((count,)),
            pltpu.SemaphoreType.DMA((3,)),
            pltpu.SemaphoreType.DMA((count,)),
        ],
        input_output_aliases={count + 5 + i: i for i in range(len(extra))},
        compiler_params=pltpu.CompilerParams(vmem_limit_bytes=VMEM),
        cost_estimate=pl.CostEstimate(
            flops=2 * sum(rows) * D * 768,
            bytes_accessed=sum(rows) * D * 2 + D * 768 * 2,
            transcendentals=0,
        ),
        name="project",
    )(*xs, own_w, low_w, high_w, gain_q, gain_k, *extra)


def attend_body(
    picks, facts, q0, q1, k00, k01, k10, k11, k20, k21, inner, out, q_buf, kv, scores, sem
):
    copies = []
    for i, (src, dst) in enumerate(
        (
            (q0, q_buf.at[0:6]),
            (q1, q_buf.at[6:12]),
            (k00, kv.at[0, 0:6]),
            (k01, kv.at[0, 6:12]),
            (k10, kv.at[1, 0:6]),
            (k11, kv.at[1, 6:12]),
            (k20, kv.at[2, 0:6]),
            (k21, kv.at[2, 6:12]),
        )
    ):
        copy = pltpu.make_async_copy(src, dst, sem.at[i])
        copy.start()
        copies.append(copy)
    for copy in copies:
        copy.wait()
    rel_row, rel_half, core, valid = facts[0], facts[1], facts[2], facts[3]
    scale = HD**-0.5 * 1.4426950408889634
    shift = jnp.where(valid > 0, 0.0, 1e30).astype(jnp.float32)

    def place(t):
        half = t // 6
        row = (t // 3) % 2
        return (half ^ rel_half) * 6 + (row ^ rel_row) * 3 + t % 3

    @pl.loop(0, NT)
    def _(t):
        q = q_buf[place(t)]
        where = [place(picks[t, j]) for j in range(WIN)]
        tops = []
        for g in range(3):
            top = None
            for j in range(WIN):
                s = lax.dot_general(
                    q,
                    kv[g, where[j], :, 0:HD],
                    (((1,), (1,)), ((), ())),
                    preferred_element_type=jnp.float32,
                )
                scores[g * WIN + j] = s
                high = jnp.maximum(s[:, 0:128], s[:, 128:256])
                top = high if top is None else jnp.maximum(top, high)
            tops.append(jnp.max(top, axis=-1, keepdims=True))
        tops[2] = tops[2] - shift
        m = jnp.maximum(jnp.maximum(tops[0], tops[1]), tops[2]) * scale
        m_far = m + shift
        total = jnp.zeros((TILE, 128), jnp.float32)
        acc = jnp.zeros((TILE, HD), jnp.float32)
        for g in range(3):
            base = m_far if g == 2 else m
            for j in range(WIN):
                p = jnp.exp2(scores[g * WIN + j] * scale - base)
                total = total + (p[:, 0:128] + p[:, 128:256])
                acc = acc + jnp.dot(
                    p.astype(jnp.bfloat16),
                    kv[g, where[j], :, HD : 2 * HD],
                    preferred_element_type=jnp.float32,
                )
        attn = (acc / jnp.sum(total, axis=-1, keepdims=True)).astype(jnp.bfloat16)
        columns = lax.broadcasted_iota(jnp.int32, (TILE, TILE), 1)
        pick = (inner[t] == columns).astype(jnp.float32).astype(jnp.bfloat16)
        ordered = jnp.dot(pick, attn, preferred_element_type=jnp.float32).astype(jnp.bfloat16)
        for i in range(4):
            piece = 4 * t + i
            owner = piece // 3
            out[(owner % 2) ^ core, owner // 2, piece % 3] = ordered[i * 64 : i * 64 + 64]


def attend(picks, facts, qs, kvs, inner):
    any_spec = pl.BlockSpec(memory_space=pl.ANY)
    vmem_spec = pl.BlockSpec(memory_space=pltpu.VMEM)
    smem_spec = pl.BlockSpec(memory_space=pltpu.SMEM)
    keys = 3 * WIN * TILE
    return pl.pallas_call(
        attend_body,
        out_shape=jax.ShapeDtypeStruct((2, 8, 3, 64, HD), jnp.bfloat16),
        in_specs=[smem_spec] * 2 + [any_spec] * 8 + [vmem_spec],
        out_specs=vmem_spec,
        scratch_shapes=[
            pltpu.VMEM((NT, TILE, HD), jnp.bfloat16),
            pltpu.VMEM((3, NT, TILE, 2 * HD), jnp.bfloat16),
            pltpu.VMEM((3 * WIN, TILE, TILE), jnp.float32),
            pltpu.SemaphoreType.DMA((8,)),
        ],
        compiler_params=pltpu.CompilerParams(vmem_limit_bytes=VMEM),
        cost_estimate=pl.CostEstimate(
            flops=4 * NT * TILE * keys * HD,
            bytes_accessed=6_000_000,
            transcendentals=NT * TILE * keys,
        ),
        name="attend",
    )(picks, facts, *qs, *kvs, inner)


def mix_body(attn, w, out):
    parts = [None] * 16
    for yh in range(2):
        for yl in range(2):
            for z in range(4):
                parts[yl * 8 + z * 2 + yh] = attn[(yh * 2 + yl) * 4 + z]
    flat = jnp.concatenate(parts, axis=-1)
    out[...] = jnp.dot(flat, w[...], preferred_element_type=jnp.float32).astype(jnp.bfloat16)


def mix(attn, w):
    step = 512
    return pl.pallas_call(
        mix_body,
        out_shape=jax.ShapeDtypeStruct((192, D), jnp.bfloat16),
        grid=(D // step,),
        in_specs=[
            pl.BlockSpec((16, 192, HD), lambda i: (0, 0, 0)),
            pl.BlockSpec((16 * HD, step), lambda i: (0, i)),
        ],
        out_specs=pl.BlockSpec((192, step), lambda i: (0, i)),
        compiler_params=pltpu.CompilerParams(vmem_limit_bytes=VMEM),
        cost_estimate=pl.CostEstimate(
            flops=2 * 192 * 2048 * D, bytes_accessed=14_000_000, transcendentals=0
        ),
        name="mix",
    )(attn, w)


def per_device(video, w_qkv, w_out, q_gain, k_gain, tile_perm, window):
    x_at, yh, yl, z, c = (lax.axis_index(a) for a in AXES)
    own = video.reshape(192, D)
    own_w = w_qkv.reshape(D, 384)
    gain_q = q_gain.reshape(1, HD)
    gain_k = k_gain.reshape(1, HD)

    near = move(own, across(1))
    rear = move(own, across(3))
    low_w = move(own_w[: D // 2], up)
    high_w = move(own_w[D // 2 :], down)
    own_other = move(own, swap_core)
    half = 96
    far_a = move(rear[:half], across(1))
    far_b = move(near[half:], across(3))
    near_other = move(near, swap_core)
    rear_other = move(rear, swap_core)
    far_a_other = move(far_a, swap_core)
    far_b_other = move(far_b, swap_core)

    first = project(
        [own, own_other, near, near_other, rear, rear_other],
        [(0, 0, 0), (0, 1, 0), (0, 2, 0), (0, 3, 0), (1, 2, 0), (1, 3, 0)],
        own_w, low_w, high_w, gain_q, gain_k,
    )
    q_a, kv_a, q_b, kv_b = project(
        [far_a, far_b, far_a_other, far_b_other],
        [(1, 0, 0), (1, 0, 32), (1, 1, 0), (1, 1, 32)],
        own_w, low_w, high_w, gain_q, gain_k, first,
    )
    kv0 = move(kv_a, regroup(0))
    kv1 = move(kv_b, regroup(1))
    q0 = move(q_a, regroup(0))
    q1 = move(q_b, regroup(1))
    kvs = [kv0, kv1, move(kv0, swap_core), move(kv1, swap_core), move(kv0, beside), move(kv1, beside)]

    raster = move(tile_perm.reshape(NT, TILE), regroup(0))
    frame, rest = raster // 768, raster % 768
    line, column = (rest // 24) % 8, rest % 8
    block = ((line // 4) ^ (z % 2)) * 2 + (((line // 2) % 2) ^ yh)
    inner = block * 64 + frame * 16 + (line % 2) * 8 + column
    valid = jnp.where(c == 0, x_at > 0, x_at < 3).astype(jnp.int32)
    facts = jnp.stack([z // 2, yl, c, valid]).astype(jnp.int32)
    attn = attend(
        window,
        facts,
        [q.reshape(6, TILE, HD) for q in (q0, q1)],
        [k.reshape(6, TILE, 2 * HD) for k in kvs],
        inner.reshape(NT, TILE, 1),
    )
    other = move(attn[1], swap_core)
    both = jnp.where(c == 0, jnp.stack([attn[0], other]), jnp.stack([other, attn[0]]))
    spread = lax.all_to_all(
        both.reshape(16, 192, HD), ("yh", "yl", "z"), 0, 0, tiled=True
    )
    w_all = lax.all_gather(w_out, ("yl", "z", "c"), axis=0, tiled=True)
    return mix(spread, w_all.reshape(16 * HD, D))[None]


def solution(mesh):
    fine = Mesh(mesh.devices.reshape(SIZES), AXES)
    tm = ("x", "yh")
    space = ("yl", "z", "c")
    in_specs = (
        P(tm, space, None, None),
        P(None, space, None),
        P(space, None, None),
        P(),
        P(),
        P(tm, None),
        P(),
    )
    return jax.shard_map(
        per_device, mesh=fine, in_specs=in_specs, out_specs=P(tm, space, None), check_vma=False
    )
```

time: 466 us -> 231 us (0.50)
  waiting for transfers between devices: 280 us -> 74.8 us
  local copies, waits for them, and re-layouts: 87.4 us -> 11.2 us
  Pallas kernels: 0 us -> 66.3 us
  matrix products: 49.4 us -> 0 us
  starting transfers between devices: 7.58 us -> 43.6 us
  other arithmetic: 26.5 us -> 1.53 us
  blocking collectives: 0 us -> 19.8 us
    reduce_scatter x1 -> x0, waiting for transfers between devices: 111 us -> none  [per_device(): lax.psum_scatter(lax.optimization_barrier(product.astype(jnp.bfloat16)).a...]
    all_gather x1, waiting for transfers between devices: 104 us -> 0.01 us  [per_device(): w_all = lax.all_gather(w_out, ('yl', 'z', 'c'), axis=0, tiled=True)]
    pallas_call x0 -> x4, Pallas kernels: none -> 66.3 us  [the longest x1 34 us: attend(): pl.pallas_call(attend_body, out_shape=jax.ShapeDtypeStruct((2, 8, 3, 64,...]
    gather x13 -> x0, local copies, waits for them, and re-layouts: 63.4 us -> none  [the longest x12 40 us: one_tile(): return attend(block, jnp.take(beside_all, picks, axis=1), valid)]
    dot_general x26 -> x0, matrix products: 49.4 us -> none  [the longest x1 14.9 us: per_device(): jnp.einsum('frwd,dc->frwc', lax.all_gather(video, 'space', axis=1, tiled=...]
    ppermute x2 -> x21, starting transfers between devices: 7.54 us -> 43.6 us  [move(): return lax.ppermute(value, AXES, pairs)]
    all_to_all x0 -> x1, blocking collectives: none -> 19.8 us  [per_device(): lax.all_to_all(both.reshape(16, 192, HD), ('yh', 'yl', 'z'), 0, 0, tiled=...]
    ppermute x2 -> x21, waiting for transfers between devices: 63.3 us -> 74.1 us  [move(): return lax.ppermute(value, AXES, pairs)]
  transfers between devices with their start and end apart: 4 -> 22, of which waited for: 3 -> 6; matrix products, arithmetic and copies ran while one was open for 1% -> 3% of each run, Pallas kernels for 0% -> 25%
where the time goes in v1:
time: 231 us
  waiting for transfers between devices  74.8 us (32%)
  Pallas kernels  66.3 us (29%)
  starting transfers between devices  43.6 us (19%)
  blocking collectives  19.8 us (9%)
  between operations  13.6 us (6%)
  local copies, waits for them, and re-layouts  11.2 us (5%)
    ppermute x21, waiting for transfers between devices, move(): return lax.ppermute(value, AXES, pairs)  74.1 us
    ppermute x21, starting transfers between devices, move(): return lax.ppermute(value, AXES, pairs)  43.6 us
    pallas_call x1, Pallas kernels, attend(): pl.pallas_call(attend_body, out_shape=jax.ShapeDtypeStruct((2, 8, 3, 64,...  34 us
    pallas_call x2, Pallas kernels, project(): pl.pallas_call(body, out_shape=shapes, in_specs=[any_spec] * (count + 3)...  23.7 us
    all_to_all x1, blocking collectives, per_device(): lax.all_to_all(both.reshape(16, 192, HD), ('yh', 'yl', 'z'), 0, 0, tiled=...  19.8 us
    pallas_call x1, Pallas kernels, mix(): pl.pallas_call(mix_body, out_shape=jax.ShapeDtypeStruct((192, D), jnp.bfl...  8.56 us
    unnamed x36, local copies, waits for them, and re-layouts  6.37 us
  transfers between devices with their start and end apart: 22, of which 6 were waited for; matrix products, arithmetic and copies ran while one was open for 3% of the time, Pallas kernels for 25%

profile of v1, /device:TPU:0, one launch (start us, length us, event | category | flops | bytes accessed | tf_op | source)
XLA Modules:
  0.0 230.8 jit_solution(16862353045114541385)
XLA Ops:
  6.5 0.7 all-gather.2.cloned.1.call-update
  7.3 4.2 %collective-permute-start = (bf16[192,3072]{1,0:T(8,128)(2,1)}, bf16[192,3072]{1,0:T(8,128)(2,1)S(1)}, u32[]{:S(2)}, u32[]{:S(2)}) collective-permute-start(bf16[192,3072]{1,0:T(8,128)(2,1)} %bitcast.37), channel_id=1, source_target_pairs={{0,6},{1,7},{2,4},{3,5},{4,2},{5,3},{6,0},{7,1},{8,14},{9,15},{10,... | collective-permute-start | bytes 3538952 | tf_op jit(solution)/shard_map/ppermute | solution.py:32
  11.5 1.9 slice_bitcast_fusion
  13.3 1.6 collective-permute-start.6
  15.0 1.7 collective-permute-start.7
  16.6 21.0 %collective-permute-done.refs_4_ = bf16[192,3072]{1,0:T(8,128)(2,1)S(1)} collective-permute-done((bf16[192,3072]{1,0:T(8,128)(2,1)}, bf16[192,3072]{1,0:T(8,128)(2,1)S(1)}, u32[]{:S(2)}, u32[]{:S(2)}) %collective-permute-start) | collective-permute-done | bytes 1179680 | tf_op jit(solution)/shard_map/ppermute | solution.py:32
  37.6 19.2 %collective-permute-done.2.refs_2_ = bf16[192,3072]{1,0:T(8,128)(2,1)S(1)} collective-permute-done((bf16[192,3072]{1,0:T(8,128)(2,1)}, bf16[192,3072]{1,0:T(8,128)(2,1)S(1)}, u32[]{:S(2)}, u32[]{:S(2)}) %collective-permute-start.2) | collective-permute-done | bytes 1179680 | tf_op jit(solution)/shard_map/ppermute | solution.py:32
  57.0 0.9 copy-done.7
  58.0 3.6 %collective-permute-done.6.refs_7_.refs_5_ = bf16[1536,384]{1,0:T(8,128)(2,1)S(1)} collective-permute-done((bf16[1536,384]{1,0:T(8,128)(2,1)S(1)}, bf16[1536,384]{1,0:T(8,128)(2,1)S(1)}, u32[]{:S(2)}, u32[]{:S(2)}) %collective-permute-start.6) | collective-permute-done | bytes 1179680 | tf_op jit(solution)/shard_map/ppermute | solution.py:32
  61.6 24.7 %collective-permute-done.1.refs_0_ = bf16[96,3072]{1,0:T(8,128)(2,1)S(1)} collective-permute-done((bf16[96,3072]{1,0:T(8,128)(2,1)S(1)}, bf16[96,3072]{1,0:T(8,128)(2,1)S(1)}, u32[]{:S(2)}, u32[]{:S(2)}) %collective-permute-start.1) | collective-permute-done | bytes 589856 | tf_op jit(solution)/shard_map/ppermute | solution.py:32
  86.8 1.0 copy-done.11
  87.9 1.1 copy-done.12
  88.9 14.8 %project.2 = (bf16[2,3,4,64,128]{4,3,2,1,0:T(8,128)(2,1)}, bf16[2,3,4,64,256]{4,3,2,1,0:T(8,128)(2,1)}, bf16[2,3,4,64,128]{4,3,2,1,0:T(8,128)(2,1)}, bf16[2,3,4,64,256]{4,3,2,1,0:T(8,128)(2,1)}) custom-call(bf16[192,3072]{1,0:T(8,128)(2,1)} %bitcast.40, bf16[192,3072]{1,0:T(8,128)(2,1)} %copy-done.10, bf16[192,3072]{1,0:T(8,128)(2,1)} %copy-done.7, ...), custom_call_target="tpu_custom_call" | custom-call | flops 5435817984 | bytes 11796480 | tf_op jit(solution)/shard_map/project/pallas_call | solution.py:135
  103.7 0.8 copy-done.4
  104.7 9.0 %project.3 = (bf16[2,3,4,64,128]{4,3,2,1,0:T(8,128)(2,1)}, bf16[2,3,4,64,256]{4,3,2,1,0:T(8,128)(2,1)}, bf16[2,3,4,64,128]{4,3,2,1,0:T(8,128)(2,1)}, bf16[2,3,4,64,256]{4,3,2,1,0:T(8,128)(2,1)}) custom-call(bf16[96,3072]{1,0:T(8,128)(2,1)} %copy-done.2, ...), custom_call_target="tpu_custom_call", output_to_operand_aliasing={{0}: (9, {}), {1}: (10, {}), {2}: (11, {}), {3}: (12, {})} | custom-call | flops 1811939328 | bytes 7077888 | tf_op jit(solution)/shard_map/project/pallas_call | solution.py:135
  113.7 1.8 collective-permute-start.13
  115.5 1.7 collective-permute-start.14
  119.0 4.5 %collective-permute-start.11 = (bf16[2,3,4,64,128]{4,3,2,1,0:T(8,128)(2,1)}, bf16[2,3,4,64,128]{4,3,2,1,0:T(8,128)(2,1)}, u32[]{:S(2)}, u32[]{:S(2)}) collective-permute-start(bf16[2,3,4,64,128]{4,3,2,1,0:T(8,128)(2,1)} %get-tuple-element.17), channel_id=1, source_target_pairs={{0,0},{1,16},{2,2},{3,18},{4,4},{5,20},{6,6},{7,22},{8,8},{9,24},{... | collective-permute-start | bytes 1179656 | tf_op jit(solution)/shard_map/ppermute | solution.py:32
  123.5 13.5 %collective-permute-start.15 = (bf16[2,3,4,64,256]{4,3,2,1,0:T(8,128)(2,1)S(1)}, bf16[2,3,4,64,256]{4,3,2,1,0:T(8,128)(2,1)S(1)}, u32[]{:S(2)}, u32[]{:S(2)}) collective-permute-start(bf16[2,3,4,64,256]{4,3,2,1,0:T(8,128)(2,1)S(1)} %collective-permute-done.13), channel_id=1, source_target_pairs={{0,1},{1,0},{2,3},{3,2},{4,5},{5,4},{6,7},{7,6},{8,9},{9,8},{10,11... | collective-permute-start | bytes 2359304 | tf_op jit(solution)/shard_map/ppermute | solution.py:32
  137.0 0.7 collective-permute-start.17
  137.7 5.4 %collective-permute-start.16 = (bf16[2,3,4,64,256]{4,3,2,1,0:T(8,128)(2,1)S(1)}, bf16[2,3,4,64,256]{4,3,2,1,0:T(8,128)(2,1)}, u32[]{:S(2)}, u32[]{:S(2)}) collective-permute-start(bf16[2,3,4,64,256]{4,3,2,1,0:T(8,128)(2,1)S(1)} %collective-permute-done.14), channel_id=1, source_target_pairs={{0,1},{1,0},{2,3},{3,2},{4,5},{5,4},{6,7},{7,6},{8,9},{9,8},{10,11... | collective-permute-start | bytes 2359304 | tf_op jit(solution)/shard_map/ppermute | solution.py:32
  143.1 1.6 collective-permute-start.18
  144.7 0.8 collective-permute-start.12
  146.9 1.7 copy.16.inner
  148.6 4.2 %collective-permute-done.12 = bf16[2,3,4,64,128]{4,3,2,1,0:T(8,128)(2,1)} collective-permute-done((bf16[2,3,4,64,128]{4,3,2,1,0:T(8,128)(2,1)}, bf16[2,3,4,64,128]{4,3,2,1,0:T(8,128)(2,1)}, u32[]{:S(2)}, u32[]{:S(2)}) %collective-permute-start.12) | collective-permute-done | bytes 393248 | tf_op jit(solution)/shard_map/ppermute | solution.py:32
  152.9 0.8 copy-done.15
  154.0 34.0 %attend.1 = bf16[2,8,3,64,128]{4,3,2,1,0:T(8,128)(2,1)} custom-call(s32[12,6]{1,0:T(8,128)} %copy.15.picks, s32[4]{0:T(128)} %pad_add_fusion.facts, bf16[6,256,128]{2,1,0:T(8,128)(2,1)} %bitcast.10.q0, bf16[6,256,128]{2,1,0:T(8,128)(2,1)} %bitcast.11.q1, bf16[6,256,256]{2,1,0:T(8,128)(2,1)} %bitcast.41, bf16[6,256,256]{2,1,0:T(8,128)(2,1)} %bitcast.42, ...), custom_call_target="tpu_custom_call" | custom-call | flops 7247757312 | bytes 6000000 | tf_op jit(solution)/shard_map/attend/pallas_call | solution.py:237
  188.0 1.2 fusion.19
  189.2 5.0 %collective-permute-start.20 = (bf16[8,3,64,128]{3,2,1,0:T(8,128)(2,1)S(1)}, bf16[8,3,64,128]{3,2,1,0:T(8,128)(2,1)S(1)}, u32[]{:S(2)}, u32[]{:S(2)}) collective-permute-start(bf16[8,3,64,128]{3,2,1,0:T(8,128)(2,1)S(1)} %get-tuple-element.24), channel_id=1, source_target_pairs={{0,1},{1,0},{2,3},{3,2},{4,5},{5,4},{6,7},{7,6},{8,9},{9,8},{10,11... | collective-permute-start | bytes 1179656 | tf_op jit(solution)/shard_map/ppermute | solution.py:32
  194.1 1.3 collective-permute-done.20
  195.6 19.8 %all_to_all.5.attn = bf16[16,192,128]{2,1,0:T(8,128)(2,1)} all-to-all(bf16[16,192,128]{2,1,0:T(8,128)(2,1)S(1)} %bitcast.31), channel_id=1, replica_groups=mesh['x'=4,'yh'=2,'yl'=2,'z'=4,'c'=2] {'yh','yl','z'}, dimensions={0} | all-to-all | bytes 1572864 | tf_op jit(solution)/shard_map/all_to_all | solution.py:339
  215.4 8.6 %mix.1 = bf16[192,3072]{1,0:T(8,128)(2,1)} custom-call(bf16[16,192,128]{2,1,0:T(8,128)(2,1)} %all_to_all.5.attn, bf16[2048,3072]{1,0:T(8,128)(2,1)} %bitcast.28), custom_call_target="tpu_custom_call" | custom-call | flops 2415919104 | bytes 14000000 | tf_op jit(solution)/shard_map/mix/pallas_call | solution.py:270
  (64 shorter events, 4.6 us)
Async XLA Ops:
  6.5 208.9 %all-gather.2.cloned.1.call-start = ((), (), s32[]{:S(2)}) async-start(), calls=%async_computation.1 | async-start | bytes 13369344 | tf_op jit(solution)/shard_map/all_gather | solution.py:342
  7.3 30.4 %collective-permute-start = (bf16[192,3072]{1,0:T(8,128)(2,1)}, bf16[192,3072]{1,0:T(8,128)(2,1)S(1)}, u32[]{:S(2)}, u32[]{:S(2)}) collective-permute-start(bf16[192,3072]{1,0:T(8,128)(2,1)} %bitcast.37), channel_id=1, source_target_pairs={{0,6},{1,7},{2,4},{3,5},{4,2},{5,3},{6,0},{7,1},{8,14},{9,15},{10,... | collective-permute-start | bytes 3538952 | tf_op jit(solution)/shard_map/ppermute | solution.py:32
  11.5 45.4 %collective-permute-start.2 = (bf16[192,3072]{1,0:T(8,128)(2,1)}, bf16[192,3072]{1,0:T(8,128)(2,1)S(1)}, u32[]{:S(2)}, u32[]{:S(2)}) collective-permute-start(bf16[192,3072]{1,0:T(8,128)(2,1)} %bitcast.38), channel_id=1, source_target_pairs={{0,2},{1,3},{2,0},{3,1},{4,6},{5,7},{6,4},{7,5},{8,10},{9,11},{10,... | collective-permute-start | bytes 3538952 | tf_op jit(solution)/shard_map/ppermute | solution.py:32
  11.5 46.4 %collective-permute-start.8 = (bf16[192,3072]{1,0:T(8,128)(2,1)}, bf16[192,3072]{1,0:T(8,128)(2,1)S(1)}, u32[]{:S(2)}, u32[]{:S(2)}) collective-permute-start(bf16[192,3072]{1,0:T(8,128)(2,1)} %bitcast.39), channel_id=1, source_target_pairs={{0,1},{1,0},{2,3},{3,2},{4,5},{5,4},{6,7},{7,6},{8,9},{9,8},{10,11... | collective-permute-start | bytes 3538952 | tf_op jit(solution)/shard_map/ppermute | solution.py:32
  13.3 48.2 %collective-permute-start.6 = (bf16[1536,384]{1,0:T(8,128)(2,1)S(1)}, bf16[1536,384]{1,0:T(8,128)(2,1)S(1)}, u32[]{:S(2)}, u32[]{:S(2)}) collective-permute-start(bf16[1536,384]{1,0:T(8,128)(2,1)S(1)} %get-tuple-element.22), channel_id=1, source_target_pairs={{0,8},{1,9},{2,10},{3,11},{4,12},{5,13},{6,14},{7,15},{8,16},{9,17... | collective-permute-start | bytes 3538952 | tf_op jit(solution)/shard_map/ppermute | solution.py:32
  15.0 71.8 %collective-permute-start.7 = (bf16[1536,384]{1,0:T(8,128)(2,1)S(1)}, bf16[1536,384]{1,0:T(8,128)(2,1)S(1)}, u32[]{:S(2)}, u32[]{:S(2)}) collective-permute-start(bf16[1536,384]{1,0:T(8,128)(2,1)S(1)} %get-tuple-element.21), channel_id=1, source_target_pairs={{0,24},{1,25},{2,26},{3,27},{4,28},{5,29},{6,30},{7,31},{8,0},{9,1... | collective-permute-start | bytes 3538952 | tf_op jit(solution)/shard_map/ppermute | solution.py:32
  37.6 19.3 %copy-start.6 = (bf16[192,3072]{1,0:T(8,128)(2,1)}, bf16[192,3072]{1,0:T(8,128)(2,1)S(1)}, u32[]{:S(2)}) copy-start(bf16[192,3072]{1,0:T(8,128)(2,1)S(1)} %collective-permute-done.refs_4_) | copy-start | bytes 3538948
  37.6 49.2 %collective-permute-start.10 = (bf16[192,3072]{1,0:T(8,128)(2,1)S(1)}, bf16[192,3072]{1,0:T(8,128)(2,1)S(1)}, u32[]{:S(2)}, u32[]{:S(2)}) collective-permute-start(bf16[192,3072]{1,0:T(8,128)(2,1)S(1)} %collective-permute-done.refs_4_), channel_id=1, source_target_pairs={{0,1},{1,0},{2,3},{3,2},{4,5},{5,4},{6,7},{7,6},{8,9},{9,8},{10,11... | collective-permute-start | bytes 3538952 | tf_op jit(solution)/shard_map/ppermute | solution.py:32
  56.9 30.0 %collective-permute-start.9 = (bf16[192,3072]{1,0:T(8,128)(2,1)S(1)}, bf16[192,3072]{1,0:T(8,128)(2,1)S(1)}, u32[]{:S(2)}, u32[]{:S(2)}) collective-permute-start(bf16[192,3072]{1,0:T(8,128)(2,1)S(1)} %collective-permute-done.2.refs_2_), channel_id=1, source_target_pairs={{0,1},{1,0},{2,3},{3,2},{4,5},{5,4},{6,7},{7,6},{8,9},{9,8},{10,11... | collective-permute-start | bytes 3538952 | tf_op jit(solution)/shard_map/ppermute | solution.py:32
  57.9 31.0 %copy-start.10 = (bf16[192,3072]{1,0:T(8,128)(2,1)}, bf16[192,3072]{1,0:T(8,128)(2,1)S(1)}, u32[]{:S(2)}) copy-start(bf16[192,3072]{1,0:T(8,128)(2,1)S(1)} %collective-permute-done.8.refs_1_) | copy-start | bytes 3538948
  57.9 28.4 %collective-permute-start.1 = (bf16[96,3072]{1,0:T(8,128)(2,1)S(1)}, bf16[96,3072]{1,0:T(8,128)(2,1)S(1)}, u32[]{:S(2)}, u32[]{:S(2)}) collective-permute-start(bf16[96,3072]{1,0:T(8,128)(2,1)S(1)} %slice.33), channel_id=1, source_target_pairs={{0,2},{1,3},{2,0},{3,1},{4,6},{5,7},{6,4},{7,5},{8,10},{9,11},{10,... | collective-permute-start | bytes 1769480 | tf_op jit(solution)/shard_map/ppermute | solution.py:32
  61.6 27.3 %copy-start = (bf16[1536,384]{1,0:T(8,128)(2,1)}, bf16[1536,384]{1,0:T(8,128)(2,1)S(1)}, u32[]{:S(2)}) copy-start(bf16[1536,384]{1,0:T(8,128)(2,1)S(1)} %collective-permute-done.6.refs_7_.refs_5_) | copy-start | bytes 3538948
  61.6 24.7 %collective-permute-start.3 = (bf16[96,3072]{1,0:T(8,128)(2,1)S(1)}, bf16[96,3072]{1,0:T(8,128)(2,1)S(1)}, u32[]{:S(2)}, u32[]{:S(2)}) collective-permute-start(bf16[96,3072]{1,0:T(8,128)(2,1)S(1)} %slice.34), channel_id=1, source_target_pairs={{0,6},{1,7},{2,4},{3,5},{4,2},{5,3},{6,0},{7,1},{8,14},{9,15},{10,... | collective-permute-start | bytes 1769480 | tf_op jit(solution)/shard_map/ppermute | solution.py:32
  86.3 17.4 %copy-start.2 = (bf16[96,3072]{1,0:T(8,128)(2,1)}, bf16[96,3072]{1,0:T(8,128)(2,1)S(1)}, u32[]{:S(2)}) copy-start(bf16[96,3072]{1,0:T(8,128)(2,1)S(1)} %collective-permute-done.1.refs_0_) | copy-start | bytes 1769476
  86.3 17.4 %collective-permute-start.4 = (bf16[96,3072]{1,0:T(8,128)(2,1)S(1)}, bf16[96,3072]{1,0:T(8,128)(2,1)S(1)}, u32[]{:S(2)}, u32[]{:S(2)}) collective-permute-start(bf16[96,3072]{1,0:T(8,128)(2,1)S(1)} %collective-permute-done.1.refs_0_), channel_id=1, source_target_pairs={{0,1},{1,0},{2,3},{3,2},{4,5},{5,4},{6,7},{7,6},{8,9},{9,8},{10,11... | collective-permute-start | bytes 1769480 | tf_op jit(solution)/shard_map/ppermute | solution.py:32
  86.3 17.4 %copy-start.3 = (bf16[96,3072]{1,0:T(8,128)(2,1)}, bf16[96,3072]{1,0:T(8,128)(2,1)S(1)}, u32[]{:S(2)}) copy-start(bf16[96,3072]{1,0:T(8,128)(2,1)S(1)} %collective-permute-done.3.refs_1_) | copy-start | bytes 1769476
  86.3 17.4 %collective-permute-start.5 = (bf16[96,3072]{1,0:T(8,128)(2,1)S(1)}, bf16[96,3072]{1,0:T(8,128)(2,1)S(1)}, u32[]{:S(2)}, u32[]{:S(2)}) collective-permute-start(bf16[96,3072]{1,0:T(8,128)(2,1)S(1)} %collective-permute-done.3.refs_1_), channel_id=1, source_target_pairs={{0,1},{1,0},{2,3},{3,2},{4,5},{5,4},{6,7},{7,6},{8,9},{9,8},{10,11... | collective-permute-start | bytes 1769480 | tf_op jit(solution)/shard_map/ppermute | solution.py:32
  86.8 2.1 copy-start.1
  104.7 13.0 %copy-start.8 = (s32[1,3072]{1,0:T(1,128)S(1)}, s32[1,3072]{1,0:T(1,128)}, u32[]{:S(2)}) copy-start(s32[1,3072]{1,0:T(1,128)} %param.12) | copy-start | bytes 36868
  104.7 40.8 %copy-start.9 = (s32[12,6]{0,1:T(8,128)S(1)}, s32[12,6]{0,1:T(8,128)}, u32[]{:S(2)}) copy-start(s32[12,6]{0,1:T(8,128)} %param.13) | copy-start | bytes 868
  113.7 9.9 %collective-permute-start.13 = (bf16[2,3,4,64,256]{4,3,2,1,0:T(8,128)(2,1)}, bf16[2,3,4,64,256]{4,3,2,1,0:T(8,128)(2,1)S(1)}, u32[]{:S(2)}, u32[]{:S(2)}) collective-permute-start(bf16[2,3,4,64,256]{4,3,2,1,0:T(8,128)(2,1)} %get-tuple-element.19), channel_id=1, source_target_pairs={{0,0},{1,16},{2,2},{3,18},{4,4},{5,20},{6,6},{7,22},{8,8},{9,24},{... | collective-permute-start | bytes 2359304 | tf_op jit(solution)/shard_map/ppermute | solution.py:32
  115.5 22.2 %collective-permute-start.14 = (bf16[2,3,4,64,256]{4,3,2,1,0:T(8,128)(2,1)}, bf16[2,3,4,64,256]{4,3,2,1,0:T(8,128)(2,1)S(1)}, u32[]{:S(2)}, u32[]{:S(2)}) collective-permute-start(bf16[2,3,4,64,256]{4,3,2,1,0:T(8,128)(2,1)} %get-tuple-element.20), channel_id=1, source_target_pairs={{0,8},{1,24},{2,10},{3,26},{4,12},{5,28},{6,14},{7,30},{8,0},{9,16... | collective-permute-start | bytes 2359304 | tf_op jit(solution)/shard_map/ppermute | solution.py:32
  118.4 24.8 %collective-permute-start.19 = (s32[12,256]{1,0:T(8,128)S(1)}, s32[12,256]{1,0:T(8,128)S(1)}, u32[]{:S(2)}, u32[]{:S(2)}) collective-permute-start(s32[12,256]{1,0:T(8,128)S(1)} %reshape.64), channel_id=1, source_target_pairs={{0,0},{1,16},{2,2},{3,18},{4,4},{5,20},{6,6},{7,22},{8,8},{9,24},{... | collective-permute-start | bytes 36872 | tf_op jit(solution)/shard_map/ppermute | solution.py:32
  119.0 25.7 %collective-permute-start.11 = (bf16[2,3,4,64,128]{4,3,2,1,0:T(8,128)(2,1)}, bf16[2,3,4,64,128]{4,3,2,1,0:T(8,128)(2,1)}, u32[]{:S(2)}, u32[]{:S(2)}) collective-permute-start(bf16[2,3,4,64,128]{4,3,2,1,0:T(8,128)(2,1)} %get-tuple-element.17), channel_id=1, source_target_pairs={{0,0},{1,16},{2,2},{3,18},{4,4},{5,20},{6,6},{7,22},{8,8},{9,24},{... | collective-permute-start | bytes 1179656 | tf_op jit(solution)/shard_map/ppermute | solution.py:32
  123.5 29.3 %copy-start.13 = (bf16[2,3,4,64,256]{4,3,2,1,0:T(8,128)(2,1)}, bf16[2,3,4,64,256]{4,3,2,1,0:T(8,128)(2,1)S(1)}, u32[]{:S(2)}) copy-start(bf16[2,3,4,64,256]{4,3,2,1,0:T(8,128)(2,1)S(1)} %collective-permute-done.13) | copy-start | bytes 2359300
  123.5 29.2 %collective-permute-start.15 = (bf16[2,3,4,64,256]{4,3,2,1,0:T(8,128)(2,1)S(1)}, bf16[2,3,4,64,256]{4,3,2,1,0:T(8,128)(2,1)S(1)}, u32[]{:S(2)}, u32[]{:S(2)}) collective-permute-start(bf16[2,3,4,64,256]{4,3,2,1,0:T(8,128)(2,1)S(1)} %collective-permute-done.13), channel_id=1, source_target_pairs={{0,1},{1,0},{2,3},{3,2},{4,5},{5,4},{6,7},{7,6},{8,9},{9,8},{10,11... | collective-permute-start | bytes 2359304 | tf_op jit(solution)/shard_map/ppermute | solution.py:32
  137.0 15.8 %collective-permute-start.17 = (bf16[2,3,4,64,256]{4,3,2,1,0:T(8,128)(2,1)S(1)}, bf16[2,3,4,64,256]{4,3,2,1,0:T(8,128)(2,1)S(1)}, u32[]{:S(2)}, u32[]{:S(2)}) collective-permute-start(bf16[2,3,4,64,256]{4,3,2,1,0:T(8,128)(2,1)S(1)} %collective-permute-done.13), channel_id=1, source_target_pairs={{1,32},{3,34},{5,36},{7,38},{9,40},{11,42},{13,44},{15,46},{17,48}... | collective-permute-start | bytes 2359304 | tf_op jit(solution)/shard_map/ppermute | solution.py:32
  137.7 15.1 %copy-start.14 = (bf16[2,3,4,64,256]{4,3,2,1,0:T(8,128)(2,1)}, bf16[2,3,4,64,256]{4,3,2,1,0:T(8,128)(2,1)S(1)}, u32[]{:S(2)}) copy-start(bf16[2,3,4,64,256]{4,3,2,1,0:T(8,128)(2,1)S(1)} %collective-permute-done.14) | copy-start | bytes 2359300
  137.7 15.1 %collective-permute-start.16 = (bf16[2,3,4,64,256]{4,3,2,1,0:T(8,128)(2,1)S(1)}, bf16[2,3,4,64,256]{4,3,2,1,0:T(8,128)(2,1)}, u32[]{:S(2)}, u32[]{:S(2)}) collective-permute-start(bf16[2,3,4,64,256]{4,3,2,1,0:T(8,128)(2,1)S(1)} %collective-permute-done.14), channel_id=1, source_target_pairs={{0,1},{1,0},{2,3},{3,2},{4,5},{5,4},{6,7},{7,6},{8,9},{9,8},{10,11... | collective-permute-start | bytes 2359304 | tf_op jit(solution)/shard_map/ppermute | solution.py:32
  143.1 9.7 %collective-permute-start.18 = (bf16[2,3,4,64,256]{4,3,2,1,0:T(8,128)(2,1)S(1)}, bf16[2,3,4,64,256]{4,3,2,1,0:T(8,128)(2,1)}, u32[]{:S(2)}, u32[]{:S(2)}) collective-permute-start(bf16[2,3,4,64,256]{4,3,2,1,0:T(8,128)(2,1)S(1)} %collective-permute-done.14), channel_id=1, source_target_pairs={{1,32},{3,34},{5,36},{7,38},{9,40},{11,42},{13,44},{15,46},{17,48}... | collective-permute-start | bytes 2359304 | tf_op jit(solution)/shard_map/ppermute | solution.py:32
  144.7 8.1 %collective-permute-start.12 = (bf16[2,3,4,64,128]{4,3,2,1,0:T(8,128)(2,1)}, bf16[2,3,4,64,128]{4,3,2,1,0:T(8,128)(2,1)}, u32[]{:S(2)}, u32[]{:S(2)}) collective-permute-start(bf16[2,3,4,64,128]{4,3,2,1,0:T(8,128)(2,1)} %get-tuple-element.18), channel_id=1, source_target_pairs={{0,8},{1,24},{2,10},{3,26},{4,12},{5,28},{6,14},{7,30},{8,0},{9,16... | collective-permute-start | bytes 1179656 | tf_op jit(solution)/shard_map/ppermute | solution.py:32
  189.2 6.3 %collective-permute-start.20 = (bf16[8,3,64,128]{3,2,1,0:T(8,128)(2,1)S(1)}, bf16[8,3,64,128]{3,2,1,0:T(8,128)(2,1)S(1)}, u32[]{:S(2)}, u32[]{:S(2)}) collective-permute-start(bf16[8,3,64,128]{3,2,1,0:T(8,128)(2,1)S(1)} %get-tuple-element.24), channel_id=1, source_target_pairs={{0,1},{1,0},{2,3},{3,2},{4,5},{5,4},{6,7},{7,6},{8,9},{9,8},{10,11... | collective-permute-start | bytes 1179656 | tf_op jit(solution)/shard_map/ppermute | solution.py:32
  (7 other events, 7.0 us)
Sparse Core Ops, SparseCore 0:
  9.1 103.4 all-gather.1

commit v2 on v1

v2 whole, which is shorter than its diff:
```python
import jax
import jax.numpy as jnp
from jax import lax
from jax.experimental import pallas as pl
from jax.experimental.pallas import tpu as pltpu
from jax.sharding import Mesh
from jax.sharding import PartitionSpec as P

D = 3072
HD = 128
NT = 12
TILE = 256
WIN = 6
AXES = ("x", "yh", "yl", "z", "c")
SIZES = (4, 2, 2, 4, 2)
VMEM = 60 * 1024 * 1024


def move(value, target):
    pairs = []
    for x in range(4):
        for y in range(4):
            for z in range(4):
                for c in range(2):
                    goal = target(x, y, z, c)
                    if goal is None:
                        continue
                    a, b, d, e = goal
                    pairs.append(
                        (((x * 4 + y) * 4 + z) * 2 + c, ((a * 4 + b % 4) * 4 + d) * 2 + e)
                    )
    return lax.ppermute(value, AXES, pairs)


def after(value, *others):
    return lax.optimization_barrier((value,) + others)[0]


def across(k):
    return lambda x, y, z, c: (x, y, z ^ k, c)


def swap_core(x, y, z, c):
    return (x, y, z, 1 - c)


def up(x, y, z, c):
    return (x, y + 1, z, c)


def down(x, y, z, c):
    return (x, y - 1, z, c)


def regroup(k):
    return lambda x, y, z, c: (x, 2 * c + ((y & 1) ^ k), z, y >> 1)


def beside(x, y, z, c):
    if c == 1:
        return (x + 1, y, z, 0) if x < 3 else None
    return (x - 1, y, z, 1) if x > 0 else None


def normed(part, gain):
    wide = part.astype(jnp.float32)
    mean = jnp.mean(wide * wide, axis=-1, keepdims=True)
    return (wide * lax.rsqrt(mean + 1e-06) * gain).astype(jnp.bfloat16)


def project_body(rows, places, *refs):
    count = len(rows)
    xs = refs[:count]
    own_w, low_w, high_w, gain_q, gain_k, out0, out1 = refs[count : count + 7]
    outs = (out0, out1)
    x_buf, w_buf, stage, x_sem, w_sem, out_sem = refs[count + 7 :]
    half = D // 2
    starts = [sum(rows[:i]) for i in range(count)]
    w_copies = [
        pltpu.make_async_copy(own_w, w_buf.at[:, 0:384], w_sem.at[0]),
        pltpu.make_async_copy(low_w, w_buf.at[0:half, 384:768], w_sem.at[1]),
        pltpu.make_async_copy(high_w, w_buf.at[half:D, 384:768], w_sem.at[2]),
    ]
    for copy in w_copies:
        copy.start()
    x_copies = []
    for i in range(count):
        copy = pltpu.make_async_copy(
            xs[i], x_buf.at[starts[i] : starts[i] + rows[i]], x_sem.at[i]
        )
        copy.start()
        x_copies.append(copy)
    for copy in w_copies:
        copy.wait()
    out_copies = []
    at = 0
    while at < count:
        members = [at]
        while sum(rows[i] for i in members) < 384:
            members.append(members[-1] + 1)
        at = members[-1] + 1
        for i in members:
            x_copies[i].wait()
        base, n = starts[members[0]], 384
        y = jnp.dot(x_buf[base : base + n], w_buf[...], preferred_element_type=jnp.float32)
        y = y.astype(jnp.bfloat16)
        for h in range(2):
            for part in range(3):
                left = h * 384 + part * 128
                value = y[:, left : left + 128]
                if part < 2:
                    value = normed(value, (gain_q, gain_k)[part][...])
                tall = value.astype(jnp.float32).reshape(n // 24, 3, 8, 128)
                for i in members:
                    line, lines = (starts[i] - base) // 24, rows[i] // 24
                    for tc in range(3):
                        stage[i, h, tc, 0 : lines * 8, part * 128 : part * 128 + 128] = (
                            tall[line : line + lines, tc]
                            .reshape(lines * 8, 128)
                            .astype(jnp.bfloat16)
                        )
        for i in members:
            blk, off = places[i]
            tall_rows = rows[i] // 3
            for h in range(2):
                copy = pltpu.make_async_copy(
                    stage.at[i, h, :, 0:tall_rows],
                    outs[h].at[:, blk, off : off + tall_rows],
                    out_sem.at[i, h],
                )
                copy.start()
                out_copies.append(copy)
    for copy in out_copies:
        copy.wait()


def project(xs, places, own_w, low_w, high_w, gain_q, gain_k):
    rows = [x.shape[0] for x in xs]
    count = len(xs)
    any_spec = pl.BlockSpec(memory_space=pl.ANY)
    vmem_spec = pl.BlockSpec(memory_space=pltpu.VMEM)

    def body(*refs):
        project_body(rows, places, *refs)

    return pl.pallas_call(
        body,
        out_shape=[jax.ShapeDtypeStruct((3, 4, 64, 384), jnp.bfloat16)] * 2,
        in_specs=[any_spec] * (count + 3) + [vmem_spec] * 2,
        out_specs=[any_spec] * 2,
        scratch_shapes=[
            pltpu.VMEM((sum(rows), D), jnp.bfloat16),
            pltpu.VMEM((D, 768), jnp.bfloat16),
            pltpu.VMEM((count, 2, 3, 64, 384), jnp.bfloat16),
            pltpu.SemaphoreType.DMA((count,)),
            pltpu.SemaphoreType.DMA((3,)),
            pltpu.SemaphoreType.DMA((count, 2)),
        ],
        compiler_params=pltpu.CompilerParams(vmem_limit_bytes=VMEM),
        cost_estimate=pl.CostEstimate(
            flops=2 * sum(rows) * D * 768,
            bytes_accessed=sum(rows) * D * 2 + D * 768 * 2,
            transcendentals=0,
        ),
        name="project",
    )(*xs, own_w, low_w, high_w, gain_q, gain_k)


def attend_body(
    near, far, s_near, s_far, x_near, x_far, picks_hbm, perm, out,
    q_buf, kv, v_t, even, odd, picks, sem,
):
    copies = []

    def fetch(src, dst):
        copy = pltpu.make_async_copy(src, dst, sem.at[len(copies)])
        copy.start()
        copies.append(copy)

    fetch(picks_hbm, picks)
    for h in range(2):
        for chunk, blocks, row, off in (
            (near, (0, 3), 0, 0), (far, (0, 1), 0, 3), (near, (3, 4), 1, 0), (far, (1, 4), 1, 1),
        ):
            tiles = pl.ds(h * 6 + row * 3, 3)
            there = pl.ds(off, blocks[1] - blocks[0])
            src = chunk[h].at[:, blocks[0] : blocks[1]]
            fetch(src.at[:, :, :, 0:HD], q_buf.at[tiles, there])
            fetch(src.at[:, :, :, HD : 3 * HD], kv.at[0, tiles, there])
    for g, (a, b) in ((1, (s_near, s_far)), (2, (x_near, x_far))):
        for h in range(2):
            for chunk, blocks, row, off in (
                (a, (0, 3), 0, 0), (b, (0, 1), 0, 3), (a, (3, 4), 1, 0), (b, (1, 4), 1, 1),
            ):
                fetch(
                    chunk.at[h, :, blocks[0] : blocks[1]],
                    kv.at[g, pl.ds(h * 6 + row * 3, 3), pl.ds(off, blocks[1] - blocks[0])],
                )
    for copy in copies:
        copy.wait()
    for g in range(3):

        @pl.loop(0, NT)
        def _(t):
            v_t[g, t] = kv[g, t, :, :, HD : 2 * HD].reshape(TILE, HD).T

    x_at, z = lax.axis_index("x"), lax.axis_index("z")
    rel_half, rel_core, core = lax.axis_index("yl"), lax.axis_index("yh"), lax.axis_index("c")
    rel_row, rel_z = z // 2, z % 2
    valid = jnp.where(core == 0, x_at, 3 - x_at)
    scale = HD**-0.5 * 1.4426950408889634
    shift = jnp.where(valid > 0, 0.0, 1e30).astype(jnp.float32)
    chunks = 3 * WIN

    def place(t):
        half = t // 6
        row = (t // 3) % 2
        return (half ^ rel_half) * 6 + (row ^ rel_row) * 3 + t % 3

    def places(t):
        return [place(picks[t, j]) for j in range(WIN)]

    def score(q, where, buf, n, tops):
        g, j = divmod(n, WIN)
        s = lax.dot_general(
            kv[g, where[j], :, :, 0:HD].reshape(TILE, HD),
            q,
            (((1,), (1,)), ((), ())),
            preferred_element_type=jnp.float32,
        )
        buf[n] = s
        high = jnp.max(s.reshape(TILE // 8, 8, TILE), axis=0)
        i = 1 if g == 2 else 0
        tops[i] = high if tops[i] is None else jnp.maximum(tops[i], high)

    def step(t, cur, nxt, tops):
        where = places(t)
        later = jnp.minimum(t + 1, NT - 1)
        where_next = places(later)
        q_next = q_buf[place(later)].reshape(TILE, HD)
        m = jnp.max(jnp.maximum(tops[0], tops[1] - shift), axis=0, keepdims=True) * scale
        m_far = m + shift
        tops_next = [None, None]
        total = jnp.zeros((8, TILE), jnp.float32)
        acc = jnp.zeros((HD, TILE), jnp.float32)
        for n in range(chunks):
            g, j = divmod(n, WIN)
            score(q_next, where_next, nxt, n, tops_next)
            p = jnp.exp2(cur[n] * scale - (m_far if g == 2 else m))
            total = total + jnp.sum(p.reshape(TILE // 8, 8, TILE), axis=0)
            acc = acc + jnp.dot(
                v_t[g, where[j]], p.astype(jnp.bfloat16), preferred_element_type=jnp.float32
            )
        attn = (acc / jnp.sum(total, axis=0, keepdims=True)).astype(jnp.bfloat16)
        raster = perm[pl.ds(t, 1), :]
        frame = (
            (raster >= 768).astype(jnp.int32)
            + (raster >= 1536).astype(jnp.int32)
            + (raster >= 2304).astype(jnp.int32)
        )
        rest = raster - 768 * frame
        line = (rest * 2731) >> 16
        column = (rest - 24 * line) & 7
        rank = (((line >> 2) & 1) ^ rel_z) * 2 + (((line >> 1) & 1) ^ rel_core)
        second = jnp.where(rank == 2, 0, jnp.where(rank == 3, 3, rank + 1))
        block = jnp.where((((t // 3) % 2) ^ rel_row) == 1, second, rank)
        inner = block * 64 + frame * 16 + (line & 1) * 8 + column
        pick = (lax.broadcasted_iota(jnp.int32, (TILE, TILE), 0) == inner).astype(jnp.float32)
        ordered = jnp.dot(
            attn, pick.astype(jnp.bfloat16), preferred_element_type=jnp.float32
        ).T.astype(jnp.bfloat16)
        for i in range(4):
            piece = 4 * t + i
            owner = piece // 3
            out[(owner % 2) ^ core, owner // 2, piece % 3] = ordered[i * 64 : i * 64 + 64]
        return tuple(tops_next)

    tops = [None, None]
    first = places(0)
    for n in range(chunks):
        score(q_buf[place(0)].reshape(TILE, HD), first, even, n, tops)

    def two(i, tops):
        tops = step(2 * i, even, odd, tops)
        return step(2 * i + 1, odd, even, tops)

    lax.fori_loop(0, NT // 2, two, tuple(tops))


def attend(near, far, s_near, s_far, x_near, x_far, picks, perm):
    any_spec = pl.BlockSpec(memory_space=pl.ANY)
    vmem_spec = pl.BlockSpec(memory_space=pltpu.VMEM)
    keys = 3 * WIN * TILE

    def body(n0, n1, f0, f1, *refs):
        attend_body((n0, n1), (f0, f1), *refs)

    return pl.pallas_call(
        body,
        out_shape=jax.ShapeDtypeStruct((2, 8, 3, 64, HD), jnp.bfloat16),
        in_specs=[any_spec] * 9 + [vmem_spec],
        out_specs=vmem_spec,
        scratch_shapes=[
            pltpu.VMEM((NT, 4, 64, HD), jnp.bfloat16),
            pltpu.VMEM((3, NT, 4, 64, 2 * HD), jnp.bfloat16),
            pltpu.VMEM((3, NT, HD, TILE), jnp.bfloat16),
            pltpu.VMEM((3 * WIN, TILE, TILE), jnp.float32),
            pltpu.VMEM((3 * WIN, TILE, TILE), jnp.float32),
            pltpu.SMEM((NT, WIN), jnp.int32),
            pltpu.SemaphoreType.DMA((40,)),
        ],
        compiler_params=pltpu.CompilerParams(vmem_limit_bytes=VMEM),
        cost_estimate=pl.CostEstimate(
            flops=4 * NT * TILE * keys * HD,
            bytes_accessed=6_000_000,
            transcendentals=NT * TILE * keys,
        ),
        name="attend",
    )(*near, *far, s_near, s_far, x_near, x_far, picks, perm)


def mix_body(attn, *refs):
    out = refs[8]
    core, half, z = lax.axis_index("c"), lax.axis_index("yl"), lax.axis_index("z")
    total = None
    for i in range(8):
        side, pair = i // 4, i % 4
        kind = core ^ side
        heads = [
            attn[kind, (half ^ (pair // 2)) * 4 + (z ^ k)] for k in ((0, 1), (3, 2))[pair % 2]
        ]
        flat = jnp.concatenate(heads, axis=-1)
        part = jnp.dot(flat, refs[i][...], preferred_element_type=jnp.float32)
        total = part if total is None else total + part
    out[...] = total.astype(jnp.bfloat16)


def mix(attn, w_here, w_there):
    step = 512
    return pl.pallas_call(
        mix_body,
        out_shape=jax.ShapeDtypeStruct((192, D), jnp.bfloat16),
        grid=(D // step,),
        in_specs=[pl.BlockSpec((2, 8, 192, HD), lambda i: (0, 0, 0, 0))]
        + [pl.BlockSpec((2 * HD, step), lambda i: (0, i))] * 8,
        out_specs=pl.BlockSpec((192, step), lambda i: (0, i)),
        compiler_params=pltpu.CompilerParams(vmem_limit_bytes=VMEM),
        cost_estimate=pl.CostEstimate(
            flops=2 * 192 * 2048 * D, bytes_accessed=14_000_000, transcendentals=0
        ),
        name="mix",
    )(attn.reshape(2, 8, 192, HD), *w_here, *w_there)


def per_device(video, w_qkv, w_out, q_gain, k_gain, tile_perm, window):
    c = lax.axis_index("c")
    own = video.reshape(192, D)
    own_w = w_qkv.reshape(D, 384)
    gain_q = q_gain.reshape(1, HD)
    gain_k = k_gain.reshape(1, HD)

    near = move(own, across(1))
    rear = move(own, across(3))
    own_other = move(own, swap_core)
    low_w = move(own_w[: D // 2], up)
    high_w = move(own_w[D // 2 :], down)
    near, rear, own_other, low_w, high_w, tile_perm, w_out = lax.optimization_barrier(
        (near, rear, own_other, low_w, high_w, tile_perm, w_out)
    )

    far_a = move(rear[:96], across(1))
    far_b = move(near[96:], across(3))
    near_other = move(near, swap_core)
    rear_other = move(rear, swap_core)
    raster = move(tile_perm.reshape(NT, TILE), regroup(0))
    close = project(
        [own, own_other, near, rear],
        [(0, 0), (1, 0), (2, 0), (3, 0)],
        own_w, low_w, high_w, gain_q, gain_k,
    )

    near0 = move(close[0], regroup(0))
    near1 = move(close[1], regroup(1))
    far_a, far_b = after(far_a, close[0]), after(far_b, close[0])
    far_a_other = move(far_a, swap_core)
    far_b_other = move(far_b, swap_core)
    w_own = after(w_out, far_a_other, far_b_other)
    w_near = move(w_own, across(1))
    w_rear = move(w_own, across(3))
    w_far = move(w_own, across(2))
    distant = project(
        [near_other, rear_other, far_a, far_b, far_a_other, far_b_other],
        [(0, 0), (3, 0), (1, 0), (1, 32), (2, 0), (2, 32)],
        own_w, low_w, high_w, gain_q, gain_k,
    )
    near0, near1 = after(near0, distant[0]), after(near1, distant[0])
    near_kv = jnp.stack([near0[..., HD:], near1[..., HD:]])
    s_near = move(near_kv, swap_core)
    x_near = move(near_kv, beside)
    far0 = move(distant[0], regroup(0))
    far1 = move(distant[1], regroup(1))
    far_kv = jnp.stack([far0[..., HD:], far1[..., HD:]])
    s_far = move(far_kv, swap_core)
    x_far = move(far_kv, beside)
    w_near, w_rear = after(w_near, far0, far1), after(w_rear, far0, far1)
    w_one = jnp.concatenate([w_own, w_near]).reshape(2 * HD, D)
    w_two = jnp.concatenate([w_rear, w_far]).reshape(2 * HD, D)
    w_three = move(w_one, up)
    w_four = move(w_two, down)
    w_here = [w_one, w_two, w_three, w_four]
    w_there = [move(w_one, swap_core), move(w_two, swap_core)]
    attn = attend((near0, near1), (far0, far1), s_near, s_far, x_near, x_far, window, raster)
    other = move(attn[1], swap_core)
    both = jnp.where(c == 0, jnp.stack([attn[0], other]), jnp.stack([other, attn[0]]))
    spread = lax.all_to_all(
        both.reshape(16, 192, HD), ("yh", "yl", "z"), 0, 0, tiled=True
    )
    w_there += [move(after(w_three, attn), swap_core), move(after(w_four, attn), swap_core)]
    return mix(spread, w_here, w_there)[None]


def solution(mesh):
    fine = Mesh(mesh.devices.reshape(SIZES), AXES)
    tm = ("x", "yh")
    space = ("yl", "z", "c")
    in_specs = (
        P(tm, space, None, None),
        P(None, space, None),
        P(space, None, None),
        P(),
        P(),
        P(tm, None),
        P(),
    )
    return jax.shard_map(
        per_device, mesh=fine, in_specs=in_specs, out_specs=P(tm, space, None), check_vma=False
    )
```

time: 231 us -> 194 us (0.84)
  blocking collectives: 19.8 us -> 0 us
  between operations: 13.6 us -> 0.29 us
  Pallas kernels: 66.3 us -> 57.8 us
  starting transfers between devices: 43.6 us -> 49.2 us
  local copies, waits for them, and re-layouts: 11.2 us -> 6.3 us
  other arithmetic: 1.53 us -> 4.99 us
    all_to_all x1 -> x0, blocking collectives: 19.8 us -> none  [per_device(): lax.all_to_all(both.reshape(16, 192, HD), ('yh', 'yl', 'z'), 0, 0, tiled=...]
    all_to_all x0 -> x1, waiting for transfers between devices: none -> 15.2 us  [per_device(): lax.all_to_all(both.reshape(16, 192, HD), ('yh', 'yl', 'z'), 0, 0, tiled=...]
    ppermute x21 -> x30, waiting for transfers between devices: 74.1 us -> 59.4 us  [move(): return lax.ppermute(value, AXES, pairs)]
    pallas_call x3, Pallas kernels: 57.7 us -> 49 us  [the longest x1 27.9 us: attend(): pl.pallas_call(body, out_shape=jax.ShapeDtypeStruct((2, 8, 3, 64, HD), jn...]
    unnamed x36 -> x29, local copies, waits for them, and re-layouts: 6.37 us -> 0.74 us
    all_to_all x0 -> x1, starting transfers between devices: none -> 4.29 us  [per_device(): lax.all_to_all(both.reshape(16, 192, HD), ('yh', 'yl', 'z'), 0, 0, tiled=...]
    ppermute x21 -> x30, starting transfers between devices: 43.6 us -> 44.9 us  [move(): return lax.ppermute(value, AXES, pairs)]
  transfers between devices with their start and end apart: 22 -> 31, of which waited for: 6 -> 12; matrix products, arithmetic and copies ran while one was open for 3% -> 6% of each run, Pallas kernels for 25% -> 25%
where the time goes in v2:
time: 194 us; the launch traced here: 193 us
  waiting for transfers between devices  74.6 us (38%)
  Pallas kernels  57.8 us (30%)
  starting transfers between devices  49.2 us (25%)
  local copies, waits for them, and re-layouts  6.3 us (3%)
  other arithmetic  4.99 us (3%)
    ppermute x30, waiting for transfers between devices, move(): return lax.ppermute(value, AXES, pairs)  59.4 us
    ppermute x30, starting transfers between devices, move(): return lax.ppermute(value, AXES, pairs)  44.9 us
    pallas_call x1, Pallas kernels, attend(): pl.pallas_call(body, out_shape=jax.ShapeDtypeStruct((2, 8, 3, 64, HD), jn...  27.9 us
    pallas_call x2, Pallas kernels, project(): pl.pallas_call(body, out_shape=[jax.ShapeDtypeStruct((3, 4, 64, 384), jnp...  21.1 us
    all_to_all x1, waiting for transfers between devices, per_device(): lax.all_to_all(both.reshape(16, 192, HD), ('yh', 'yl', 'z'), 0, 0, tiled=...  15.2 us
    pallas_call x1, Pallas kernels, mix(): pl.pallas_call(mix_body, out_shape=jax.ShapeDtypeStruct((192, D), jnp.bfl...  8.77 us
    all_to_all x1, starting transfers between devices, per_device(): lax.all_to_all(both.reshape(16, 192, HD), ('yh', 'yl', 'z'), 0, 0, tiled=...  4.29 us
  transfers between devices with their start and end apart: 31, of which 12 were waited for; matrix products, arithmetic and copies ran while one was open for 6% of the time, Pallas kernels for 25%

profile of v2, /device:TPU:0, one launch (start us, length us, event | category | flops | bytes accessed | tf_op | source)
XLA Modules:
  0.0 193.1 jit_solution(227651450471392183)
XLA Ops:
  0.0 4.1 %collective-permute-start.1 = (bf16[192,3072]{1,0:T(8,128)(2,1)}, bf16[192,3072]{1,0:T(8,128)(2,1)S(1)}, u32[]{:S(2)}, u32[]{:S(2)}) collective-permute-start(bf16[192,3072]{1,0:T(8,128)(2,1)} %bitcast.34), channel_id=1, source_target_pairs={{0,6},{1,7},{2,4},{3,5},{4,2},{5,3},{6,0},{7,1},{8,14},{9,15},{10,... | collective-permute-start | bytes 3538952 | tf_op jit(solution)/shard_map/ppermute | solution.py:32
  4.1 1.9 slice_bitcast_fusion
  6.0 3.1 %collective-permute-start.4 = (bf16[1536,384]{1,0:T(8,128)(2,1)S(1)}, bf16[1536,384]{1,0:T(8,128)(2,1)S(1)}, u32[]{:S(2)}, u32[]{:S(2)}) collective-permute-start(bf16[1536,384]{1,0:T(8,128)(2,1)S(1)} %get-tuple-element.45), channel_id=1, source_target_pairs={{0,24},{1,25},{2,26},{3,27},{4,28},{5,29},{6,30},{7,31},{8,0},{9,1... | collective-permute-start | bytes 3538952 | tf_op jit(solution)/shard_map/ppermute | solution.py:32
  9.1 21.9 %collective-permute-done.1.refs_3_ = bf16[192,3072]{1,0:T(8,128)(2,1)S(1)} collective-permute-done((bf16[192,3072]{1,0:T(8,128)(2,1)}, bf16[192,3072]{1,0:T(8,128)(2,1)S(1)}, u32[]{:S(2)}, u32[]{:S(2)}) %collective-permute-start.1) | collective-permute-done | bytes 1179680 | tf_op jit(solution)/shard_map/ppermute | solution.py:32
  31.0 1.6 collective-permute-done.refs_2_
  32.5 2.2 %collective-permute-done.4.refs_6_.refs_8_ = bf16[1536,384]{1,0:T(8,128)(2,1)S(1)} collective-permute-done((bf16[1536,384]{1,0:T(8,128)(2,1)S(1)}, bf16[1536,384]{1,0:T(8,128)(2,1)S(1)}, u32[]{:S(2)}, u32[]{:S(2)}) %collective-permute-start.4) | collective-permute-done | bytes 1179680 | tf_op jit(solution)/shard_map/ppermute | solution.py:32
  34.7 3.5 %collective-permute-done.3.refs_5_.refs_7_ = bf16[1536,384]{1,0:T(8,128)(2,1)} collective-permute-done((bf16[1536,384]{1,0:T(8,128)(2,1)S(1)}, bf16[1536,384]{1,0:T(8,128)(2,1)}, u32[]{:S(2)}, u32[]{:S(2)}) %collective-permute-start.3) | collective-permute-done | bytes 1179680 | tf_op jit(solution)/shard_map/ppermute | solution.py:32
  38.3 1.8 collective-permute-start.8
  40.1 1.1 slice.42
  42.1 10.5 %project.2 = (bf16[3,4,64,384]{3,2,1,0:T(8,128)(2,1)}, bf16[3,4,64,384]{3,2,1,0:T(8,128)(2,1)}) custom-call(bf16[192,3072]{1,0:T(8,128)(2,1)} %bitcast.36, bf16[192,3072]{1,0:T(8,128)(2,1)} %copy-done.11, bf16[192,3072]{1,0:T(8,128)(2,1)} %collective-permute-done.refs_2_, bf16[192,3072]{1,0:T(8,128)(2,1)} %copy-done.3, bf16[3072,384]{1,0:T(8,128)(2,1)} %bitcast.31, ...), custom_call_target="tpu_custom_call" | custom-call | flops 3623878656 | bytes 9437184 | tf_op jit(solution)/shard_map/project/pallas_call | solution.py:146
  52.7 3.6 %collective-permute-done.9.refs_3_ = bf16[96,3072]{1,0:T(8,128)(2,1)} collective-permute-done((bf16[96,3072]{1,0:T(8,128)(2,1)S(1)}, bf16[96,3072]{1,0:T(8,128)(2,1)}, u32[]{:S(2)}, u32[]{:S(2)}) %collective-permute-start.9) | collective-permute-done | bytes 589856 | tf_op jit(solution)/shard_map/ppermute | solution.py:32
  56.4 1.9 collective-permute-start.5
  58.7 10.7 %project.3 = (bf16[3,4,64,384]{3,2,1,0:T(8,128)(2,1)}, bf16[3,4,64,384]{3,2,1,0:T(8,128)(2,1)}) custom-call(bf16[192,3072]{1,0:T(8,128)(2,1)} %collective-permute-done.6.refs_0_, bf16[192,3072]{1,0:T(8,128)(2,1)} %collective-permute-done.7.refs_1_, bf16[96,3072]{1,0:T(8,128)(2,1)} %copy-done.12, bf16[96,3072]{1,0:T(8,128)(2,1)} %collective-permute-done.9.refs_3_, ...), custom_call_target="tpu_custom_call" | custom-call | flops 3623878656 | bytes 9437184 | tf_op jit(solution)/shard_map/project/pallas_call | solution.py:146
  69.4 1.6 collective-permute-start.14
  73.6 1.7 collective-permute-start.13
  75.4 0.9 pad_maximum_fusion.2
  76.4 3.3 %collective-permute-done.14.f1 = bf16[3,4,64,384]{3,2,1,0:T(8,128)(2,1)S(1)} collective-permute-done((bf16[3,4,64,384]{3,2,1,0:T(8,128)(2,1)}, bf16[3,4,64,384]{3,2,1,0:T(8,128)(2,1)S(1)}, u32[]{:S(2)}, u32[]{:S(2)}) %collective-permute-start.14) | collective-permute-done | bytes 589856 | tf_op jit(solution)/shard_map/ppermute | solution.py:32
  80.6 1.6 collective-permute-start.17
  82.2 7.9 %collective-permute-done.22 = bf16[1,128,3072]{2,1,0:T(8,128)(2,1)S(1)} collective-permute-done((bf16[1,128,3072]{2,1,0:T(8,128)(2,1)S(1)}, bf16[1,128,3072]{2,1,0:T(8,128)(2,1)S(1)}, u32[]{:S(2)}, u32[]{:S(2)}) %collective-permute-start.22) | collective-permute-done | bytes 786464 | tf_op jit(solution)/shard_map/ppermute | solution.py:32
  90.1 7.5 %collective-permute-start.15 = (bf16[2,3,4,64,256]{4,3,2,1,0:T(8,128)(2,1)}, bf16[2,3,4,64,256]{4,3,2,1,0:T(8,128)(2,1)}, u32[]{:S(2)}, u32[]{:S(2)}) collective-permute-start(bf16[2,3,4,64,256]{4,3,2,1,0:T(8,128)(2,1)} %pad_maximum_fusion.2), channel_id=1, source_target_pairs={{0,1},{1,0},{2,3},{3,2},{4,5},{5,4},{6,7},{7,6},{8,9},{9,8},{10,11... | collective-permute-start | bytes 2359304 | tf_op jit(solution)/shard_map/ppermute | solution.py:32
  97.9 10.8 %collective-permute-done.23 = bf16[1,128,3072]{2,1,0:T(8,128)(2,1)S(1)} collective-permute-done((bf16[1,128,3072]{2,1,0:T(8,128)(2,1)S(1)}, bf16[1,128,3072]{2,1,0:T(8,128)(2,1)S(1)}, u32[]{:S(2)}, u32[]{:S(2)}) %collective-permute-start.23) | collective-permute-done | bytes 786464 | tf_op jit(solution)/shard_map/ppermute | solution.py:32
  108.9 3.5 %collective-permute-start.25 = (bf16[256,3072]{1,0:T(8,128)(2,1)S(1)}, bf16[256,3072]{1,0:T(8,128)(2,1)}, u32[]{:S(2)}, u32[]{:S(2)}) collective-permute-start(bf16[256,3072]{1,0:T(8,128)(2,1)S(1)} %bitcast.27), channel_id=1, source_target_pairs={{0,24},{1,25},{2,26},{3,27},{4,28},{5,29},{6,30},{7,31},{8,0},{9,1... | collective-permute-start | bytes 4718600 | tf_op jit(solution)/shard_map/ppermute | solution.py:32
  113.3 1.6 collective-permute-start.18
  114.9 2.0 %collective-permute-start.16 = (bf16[2,3,4,64,256]{4,3,2,1,0:T(8,128)(2,1)}, bf16[2,3,4,64,256]{4,3,2,1,0:T(8,128)(2,1)}, u32[]{:S(2)}, u32[]{:S(2)}) collective-permute-start(bf16[2,3,4,64,256]{4,3,2,1,0:T(8,128)(2,1)} %pad_maximum_fusion.3), channel_id=1, source_target_pairs={{0,1},{1,0},{2,3},{3,2},{4,5},{5,4},{6,7},{7,6},{8,9},{9,8},{10,11... | collective-permute-start | bytes 2359304 | tf_op jit(solution)/shard_map/ppermute | solution.py:32
  117.7 10.5 %collective-permute-start.27 = (bf16[256,3072]{1,0:T(8,128)(2,1)S(1)}, bf16[256,3072]{1,0:T(8,128)(2,1)}, u32[]{:S(2)}, u32[]{:S(2)}) collective-permute-start(bf16[256,3072]{1,0:T(8,128)(2,1)S(1)} %bitcast.28), channel_id=1, source_target_pairs={{0,1},{1,0},{2,3},{3,2},{4,5},{5,4},{6,7},{7,6},{8,9},{9,8},{10,11... | collective-permute-start | bytes 4718600 | tf_op jit(solution)/shard_map/ppermute | solution.py:32
  128.1 27.9 %attend.1 = bf16[2,8,3,64,128]{4,3,2,1,0:T(8,128)(2,1)} custom-call(bf16[3,4,64,384]{3,2,1,0:T(8,128)(2,1)} %copy-done.7, bf16[3,4,64,384]{3,2,1,0:T(8,128)(2,1)} %copy-done.6, bf16[3,4,64,384]{3,2,1,0:T(8,128)(2,1)} %copy-done.5, bf16[3,4,64,384]{3,2,1,0:T(8,128)(2,1)} %copy-done.4, bf16[2,3,4,64,256]{4,3,2,1,0:T(8,128)(2,1)} %collective-permute-done.15.refs_0_, ...), custom_call_target="tpu_custom_call" | custom-call | flops 7247757312 | bytes 6000000 | tf_op jit(solution)/shard_map/attend/pallas_call | solution.py:298
  156.7 1.9 %fusion = (bf16[1,8,3,64,128]{4,3,2,1,0:T(8,128)(2,1)S(1)}, bf16[8,3,64,128]{3,2,1,0:T(8,128)(2,1)}) fusion(bf16[2,8,3,64,128]{4,3,2,1,0:T(8,128)(2,1)} %attend.1), kind=kLoop, calls=%fused_computation.12 | loop fusion | bytes 1572864 | tf_op jit(solution)/shard_map/slice | solution.py:414
  158.7 4.0 %collective-permute-done.20 = bf16[8,3,64,128]{3,2,1,0:T(8,128)(2,1)} collective-permute-done((bf16[8,3,64,128]{3,2,1,0:T(8,128)(2,1)}, bf16[8,3,64,128]{3,2,1,0:T(8,128)(2,1)}, u32[]{:S(2)}, u32[]{:S(2)}) %collective-permute-start.20) | collective-permute-done | bytes 393248 | tf_op jit(solution)/shard_map/ppermute | solution.py:32
  162.7 2.1 %maximum_select_fusion = bf16[2,8,3,64,128]{4,3,2,1,0:T(8,128)(2,1)} fusion(bf16[1,8,3,64,128]{4,3,2,1,0:T(8,128)(2,1)} %bitcast.11, bf16[1,8,3,64,128]{4,3,2,1,0:T(8,128)(2,1)S(1)} %get-tuple-element.47, pred[]{:T(512)S(6)} %eq.3), kind=kLoop, calls=%fused_computation.6 | loop fusion | flops 1179648 | bytes 1572865 | tf_op jit(solution)/shard_map/jit(_where)/select_n | solution.py:414
  164.9 4.3 %all-to-all-start = ((bf16[16,192,128]{2,1,0:T(8,128)(2,1)}), bf16[16,192,128]{2,1,0:T(8,128)(2,1)}, u32[]{:S(2)}, u32[]{:S(2)}) async-start(bf16[16,192,128]{2,1,0:T(8,128)(2,1)} %bitcast.30), calls=%async_computation | async-start | bytes 1572864 | tf_op jit(solution)/shard_map/all_to_all | solution.py:415
  169.2 15.2 %all-to-all-done = bf16[16,192,128]{2,1,0:T(8,128)(2,1)} async-done(((bf16[16,192,128]{2,1,0:T(8,128)(2,1)}), bf16[16,192,128]{2,1,0:T(8,128)(2,1)}, u32[]{:S(2)}, u32[]{:S(2)}) %all-to-all-start) | async-done | bytes 786464 | tf_op jit(solution)/shard_map/all_to_all | solution.py:415
  184.4 8.8 %mix.1 = bf16[192,3072]{1,0:T(8,128)(2,1)} custom-call(bf16[2,8,192,128]{3,2,1,0:T(8,128)(2,1)} %bitcast.13.attn, bf16[256,3072]{1,0:T(8,128)(2,1)} %bitcast.26, bf16[256,3072]{1,0:T(8,128)(2,1)} %bitcast.29, bf16[256,3072]{1,0:T(8,128)(2,1)} %collective-permute-done.24.refs_2_, bf16[256,3072]{1,0:T(8,128)(2,1)} %collective-permute-done.25.refs_3_, ...), custom_call_target="tpu_custom_call" | custom-call | flops 2415919104 | bytes 14000000 | tf_op jit(solution)/shard_map/mix/pallas_call | solution.py:340
  (78 shorter events, 8.0 us)
Async XLA Ops:
  0.0 9.1 %collective-permute-start.2 = (bf16[192,3072]{1,0:T(8,128)(2,1)}, bf16[192,3072]{1,0:T(8,128)(2,1)S(1)}, u32[]{:S(2)}, u32[]{:S(2)}) collective-permute-start(bf16[192,3072]{1,0:T(8,128)(2,1)} %bitcast.33), channel_id=1, source_target_pairs={{0,1},{1,0},{2,3},{3,2},{4,5},{5,4},{6,7},{7,6},{8,9},{9,8},{10,11... | collective-permute-start | bytes 3538952 | tf_op jit(solution)/shard_map/ppermute | solution.py:32
  0.0 31.0 %collective-permute-start.1 = (bf16[192,3072]{1,0:T(8,128)(2,1)}, bf16[192,3072]{1,0:T(8,128)(2,1)S(1)}, u32[]{:S(2)}, u32[]{:S(2)}) collective-permute-start(bf16[192,3072]{1,0:T(8,128)(2,1)} %bitcast.34), channel_id=1, source_target_pairs={{0,6},{1,7},{2,4},{3,5},{4,2},{5,3},{6,0},{7,1},{8,14},{9,15},{10,... | collective-permute-start | bytes 3538952 | tf_op jit(solution)/shard_map/ppermute | solution.py:32
  4.1 28.4 %collective-permute-start = (bf16[192,3072]{1,0:T(8,128)(2,1)}, bf16[192,3072]{1,0:T(8,128)(2,1)}, u32[]{:S(2)}, u32[]{:S(2)}) collective-permute-start(bf16[192,3072]{1,0:T(8,128)(2,1)} %bitcast.35), channel_id=1, source_target_pairs={{0,2},{1,3},{2,0},{3,1},{4,6},{5,7},{6,4},{7,5},{8,10},{9,11},{10,... | collective-permute-start | bytes 3538952 | tf_op jit(solution)/shard_map/ppermute | solution.py:32
  6.0 28.7 %collective-permute-start.4 = (bf16[1536,384]{1,0:T(8,128)(2,1)S(1)}, bf16[1536,384]{1,0:T(8,128)(2,1)S(1)}, u32[]{:S(2)}, u32[]{:S(2)}) collective-permute-start(bf16[1536,384]{1,0:T(8,128)(2,1)S(1)} %get-tuple-element.45), channel_id=1, source_target_pairs={{0,24},{1,25},{2,26},{3,27},{4,28},{5,29},{6,30},{7,31},{8,0},{9,1... | collective-permute-start | bytes 3538952 | tf_op jit(solution)/shard_map/ppermute | solution.py:32
  9.1 29.1 %collective-permute-start.3 = (bf16[1536,384]{1,0:T(8,128)(2,1)S(1)}, bf16[1536,384]{1,0:T(8,128)(2,1)}, u32[]{:S(2)}, u32[]{:S(2)}) collective-permute-start(bf16[1536,384]{1,0:T(8,128)(2,1)S(1)} %get-tuple-element.46), channel_id=1, source_target_pairs={{0,8},{1,9},{2,10},{3,11},{4,12},{5,13},{6,14},{7,15},{8,16},{9,17... | collective-permute-start | bytes 3538952 | tf_op jit(solution)/shard_map/ppermute | solution.py:32
  38.3 14.4 %collective-permute-start.8 = (bf16[96,3072]{1,0:T(8,128)(2,1)S(1)}, bf16[96,3072]{1,0:T(8,128)(2,1)S(1)}, u32[]{:S(2)}, u32[]{:S(2)}) collective-permute-start(bf16[96,3072]{1,0:T(8,128)(2,1)S(1)} %slice.41), channel_id=1, source_target_pairs={{0,2},{1,3},{2,0},{3,1},{4,6},{5,7},{6,4},{7,5},{8,10},{9,11},{10,... | collective-permute-start | bytes 1769480 | tf_op jit(solution)/shard_map/ppermute | solution.py:32
  41.2 15.1 %collective-permute-start.9 = (bf16[96,3072]{1,0:T(8,128)(2,1)S(1)}, bf16[96,3072]{1,0:T(8,128)(2,1)}, u32[]{:S(2)}, u32[]{:S(2)}) collective-permute-start(bf16[96,3072]{1,0:T(8,128)(2,1)S(1)} %slice.42), channel_id=1, source_target_pairs={{0,6},{1,7},{2,4},{3,5},{4,2},{5,3},{6,0},{7,1},{8,14},{9,15},{10,... | collective-permute-start | bytes 1769480 | tf_op jit(solution)/shard_map/ppermute | solution.py:32
  41.6 17.1 %collective-permute-start.6 = (bf16[192,3072]{1,0:T(8,128)(2,1)}, bf16[192,3072]{1,0:T(8,128)(2,1)}, u32[]{:S(2)}, u32[]{:S(2)}) collective-permute-start(bf16[192,3072]{1,0:T(8,128)(2,1)} %collective-permute-done.refs_2_), channel_id=1, source_target_pairs={{0,1},{1,0},{2,3},{3,2},{4,5},{5,4},{6,7},{7,6},{8,9},{9,8},{10,11... | collective-permute-start | bytes 3538952 | tf_op jit(solution)/shard_map/ppermute | solution.py:32
  41.6 17.1 %collective-permute-start.7 = (bf16[192,3072]{1,0:T(8,128)(2,1)S(1)}, bf16[192,3072]{1,0:T(8,128)(2,1)}, u32[]{:S(2)}, u32[]{:S(2)}) collective-permute-start(bf16[192,3072]{1,0:T(8,128)(2,1)S(1)} %collective-permute-done.1.refs_3_), channel_id=1, source_target_pairs={{0,1},{1,0},{2,3},{3,2},{4,5},{5,4},{6,7},{7,6},{8,9},{9,8},{10,11... | collective-permute-start | bytes 3538952 | tf_op jit(solution)/shard_map/ppermute | solution.py:32
  52.7 3.7 %collective-permute-start.10 = (bf16[96,3072]{1,0:T(8,128)(2,1)S(1)}, bf16[96,3072]{1,0:T(8,128)(2,1)}, u32[]{:S(2)}, u32[]{:S(2)}) collective-permute-start(bf16[96,3072]{1,0:T(8,128)(2,1)S(1)} %collective-permute-done.8.refs_2_), channel_id=1, source_target_pairs={{0,1},{1,0},{2,3},{3,2},{4,5},{5,4},{6,7},{7,6},{8,9},{9,8},{10,11... | collective-permute-start | bytes 1769480 | tf_op jit(solution)/shard_map/ppermute | solution.py:32
  56.3 2.3 %collective-permute-start.11 = (bf16[96,3072]{1,0:T(8,128)(2,1)}, bf16[96,3072]{1,0:T(8,128)(2,1)}, u32[]{:S(2)}, u32[]{:S(2)}) collective-permute-start(bf16[96,3072]{1,0:T(8,128)(2,1)} %collective-permute-done.9.refs_3_), channel_id=1, source_target_pairs={{0,1},{1,0},{2,3},{3,2},{4,5},{5,4},{6,7},{7,6},{8,9},{9,8},{10,11... | collective-permute-start | bytes 1769480 | tf_op jit(solution)/shard_map/ppermute | solution.py:32
  56.3 17.3 %collective-permute-start.12 = (bf16[3,4,64,384]{3,2,1,0:T(8,128)(2,1)}, bf16[3,4,64,384]{3,2,1,0:T(8,128)(2,1)S(1)}, u32[]{:S(2)}, u32[]{:S(2)}) collective-permute-start(bf16[3,4,64,384]{3,2,1,0:T(8,128)(2,1)} %get-tuple-element.35), channel_id=1, source_target_pairs={{0,8},{1,24},{2,10},{3,26},{4,12},{5,28},{6,14},{7,30},{8,0},{9,16... | collective-permute-start | bytes 1769480 | tf_op jit(solution)/shard_map/ppermute | solution.py:32
  56.4 17.2 %collective-permute-start.5 = (bf16[3,4,64,384]{3,2,1,0:T(8,128)(2,1)}, bf16[3,4,64,384]{3,2,1,0:T(8,128)(2,1)S(1)}, u32[]{:S(2)}, u32[]{:S(2)}) collective-permute-start(bf16[3,4,64,384]{3,2,1,0:T(8,128)(2,1)} %get-tuple-element.30), channel_id=1, source_target_pairs={{0,0},{1,16},{2,2},{3,18},{4,4},{5,20},{6,6},{7,22},{8,8},{9,24},{... | collective-permute-start | bytes 1769480 | tf_op jit(solution)/shard_map/ppermute | solution.py:32
  69.4 10.3 %collective-permute-start.14 = (bf16[3,4,64,384]{3,2,1,0:T(8,128)(2,1)}, bf16[3,4,64,384]{3,2,1,0:T(8,128)(2,1)S(1)}, u32[]{:S(2)}, u32[]{:S(2)}) collective-permute-start(bf16[3,4,64,384]{3,2,1,0:T(8,128)(2,1)} %get-tuple-element.37), channel_id=1, source_target_pairs={{0,8},{1,24},{2,10},{3,26},{4,12},{5,28},{6,14},{7,30},{8,0},{9,16... | collective-permute-start | bytes 1769480 | tf_op jit(solution)/shard_map/ppermute | solution.py:32
  72.1 41.2 %collective-permute-start.19 = (s32[12,256]{1,0:T(8,128)S(1)}, s32[12,256]{1,0:T(8,128)S(1)}, u32[]{:S(2)}, u32[]{:S(2)}) collective-permute-start(s32[12,256]{1,0:T(8,128)S(1)} %reshape.35), channel_id=1, source_target_pairs={{0,0},{1,16},{2,2},{3,18},{4,4},{5,20},{6,6},{7,22},{8,8},{9,24},{... | collective-permute-start | bytes 36872 | tf_op jit(solution)/shard_map/ppermute | solution.py:32
  72.8 17.3 %collective-permute-start.22 = (bf16[1,128,3072]{2,1,0:T(8,128)(2,1)S(1)}, bf16[1,128,3072]{2,1,0:T(8,128)(2,1)S(1)}, u32[]{:S(2)}, u32[]{:S(2)}) collective-permute-start(bf16[1,128,3072]{2,1,0:T(8,128)(2,1)S(1)} %copy-done.2), channel_id=1, source_target_pairs={{0,6},{1,7},{2,4},{3,5},{4,2},{5,3},{6,0},{7,1},{8,14},{9,15},{10,... | collective-permute-start | bytes 2359304 | tf_op jit(solution)/shard_map/ppermute | solution.py:32
  73.6 24.0 %collective-permute-start.21 = (bf16[1,128,3072]{2,1,0:T(8,128)(2,1)S(1)}, bf16[1,128,3072]{2,1,0:T(8,128)(2,1)S(1)}, u32[]{:S(2)}, u32[]{:S(2)}) collective-permute-start(bf16[1,128,3072]{2,1,0:T(8,128)(2,1)S(1)} %copy-done.2), channel_id=1, source_target_pairs={{0,2},{1,3},{2,0},{3,1},{4,6},{5,7},{6,4},{7,5},{8,10},{9,11},{10,... | collective-permute-start | bytes 2359304 | tf_op jit(solution)/shard_map/ppermute | solution.py:32
  73.6 7.0 %collective-permute-start.13 = (bf16[3,4,64,384]{3,2,1,0:T(8,128)(2,1)}, bf16[3,4,64,384]{3,2,1,0:T(8,128)(2,1)S(1)}, u32[]{:S(2)}, u32[]{:S(2)}) collective-permute-start(bf16[3,4,64,384]{3,2,1,0:T(8,128)(2,1)} %get-tuple-element.33), channel_id=1, source_target_pairs={{0,0},{1,16},{2,2},{3,18},{4,4},{5,20},{6,6},{7,22},{8,8},{9,24},{... | collective-permute-start | bytes 1769480 | tf_op jit(solution)/shard_map/ppermute | solution.py:32
  79.7 29.0 %collective-permute-start.23 = (bf16[1,128,3072]{2,1,0:T(8,128)(2,1)S(1)}, bf16[1,128,3072]{2,1,0:T(8,128)(2,1)S(1)}, u32[]{:S(2)}, u32[]{:S(2)}) collective-permute-start(bf16[1,128,3072]{2,1,0:T(8,128)(2,1)S(1)} %copy-done.2), channel_id=1, source_target_pairs={{0,4},{1,5},{2,6},{3,7},{4,0},{5,1},{6,2},{7,3},{8,12},{9,13},{10,... | collective-permute-start | bytes 2359304 | tf_op jit(solution)/shard_map/ppermute | solution.py:32
  80.6 34.3 %collective-permute-start.17 = (bf16[2,3,4,64,256]{4,3,2,1,0:T(8,128)(2,1)}, bf16[2,3,4,64,256]{4,3,2,1,0:T(8,128)(2,1)}, u32[]{:S(2)}, u32[]{:S(2)}) collective-permute-start(bf16[2,3,4,64,256]{4,3,2,1,0:T(8,128)(2,1)} %pad_maximum_fusion.2), channel_id=1, source_target_pairs={{1,32},{3,34},{5,36},{7,38},{9,40},{11,42},{13,44},{15,46},{17,48}... | collective-permute-start | bytes 2359304 | tf_op jit(solution)/shard_map/ppermute | solution.py:32
  90.1 27.5 %collective-permute-start.15 = (bf16[2,3,4,64,256]{4,3,2,1,0:T(8,128)(2,1)}, bf16[2,3,4,64,256]{4,3,2,1,0:T(8,128)(2,1)}, u32[]{:S(2)}, u32[]{:S(2)}) collective-permute-start(bf16[2,3,4,64,256]{4,3,2,1,0:T(8,128)(2,1)} %pad_maximum_fusion.2), channel_id=1, source_target_pairs={{0,1},{1,0},{2,3},{3,2},{4,5},{5,4},{6,7},{7,6},{8,9},{9,8},{10,11... | collective-permute-start | bytes 2359304 | tf_op jit(solution)/shard_map/ppermute | solution.py:32
  97.8 58.3 %collective-permute-start.24 = (bf16[256,3072]{1,0:T(8,128)(2,1)S(1)}, bf16[256,3072]{1,0:T(8,128)(2,1)}, u32[]{:S(2)}, u32[]{:S(2)}) collective-permute-start(bf16[256,3072]{1,0:T(8,128)(2,1)S(1)} %bitcast.24), channel_id=1, source_target_pairs={{0,8},{1,9},{2,10},{3,11},{4,12},{5,13},{6,14},{7,15},{8,16},{9,17... | collective-permute-start | bytes 4718600 | tf_op jit(solution)/shard_map/ppermute | solution.py:32
  108.9 47.2 %copy-start.1 = (bf16[2,128,3072]{2,1,0:T(8,128)(2,1)}, bf16[2,128,3072]{2,1,0:T(8,128)(2,1)S(1)}, u32[]{:S(2)}) copy-start(bf16[2,128,3072]{2,1,0:T(8,128)(2,1)S(1)} %pad_maximum_fusion.1) | copy-start | bytes 4718596
  108.9 47.3 %collective-permute-start.25 = (bf16[256,3072]{1,0:T(8,128)(2,1)S(1)}, bf16[256,3072]{1,0:T(8,128)(2,1)}, u32[]{:S(2)}, u32[]{:S(2)}) collective-permute-start(bf16[256,3072]{1,0:T(8,128)(2,1)S(1)} %bitcast.27), channel_id=1, source_target_pairs={{0,24},{1,25},{2,26},{3,27},{4,28},{5,29},{6,30},{7,31},{8,0},{9,1... | collective-permute-start | bytes 4718600 | tf_op jit(solution)/shard_map/ppermute | solution.py:32
  113.3 4.3 %collective-permute-start.18 = (bf16[2,3,4,64,256]{4,3,2,1,0:T(8,128)(2,1)}, bf16[2,3,4,64,256]{4,3,2,1,0:T(8,128)(2,1)}, u32[]{:S(2)}, u32[]{:S(2)}) collective-permute-start(bf16[2,3,4,64,256]{4,3,2,1,0:T(8,128)(2,1)} %pad_maximum_fusion.3), channel_id=1, source_target_pairs={{1,32},{3,34},{5,36},{7,38},{9,40},{11,42},{13,44},{15,46},{17,48}... | collective-permute-start | bytes 2359304 | tf_op jit(solution)/shard_map/ppermute | solution.py:32
  114.9 13.2 %collective-permute-start.16 = (bf16[2,3,4,64,256]{4,3,2,1,0:T(8,128)(2,1)}, bf16[2,3,4,64,256]{4,3,2,1,0:T(8,128)(2,1)}, u32[]{:S(2)}, u32[]{:S(2)}) collective-permute-start(bf16[2,3,4,64,256]{4,3,2,1,0:T(8,128)(2,1)} %pad_maximum_fusion.3), channel_id=1, source_target_pairs={{0,1},{1,0},{2,3},{3,2},{4,5},{5,4},{6,7},{7,6},{8,9},{9,8},{10,11... | collective-permute-start | bytes 2359304 | tf_op jit(solution)/shard_map/ppermute | solution.py:32
  117.6 51.5 %collective-permute-start.26 = (bf16[256,3072]{1,0:T(8,128)(2,1)S(1)}, bf16[256,3072]{1,0:T(8,128)(2,1)}, u32[]{:S(2)}, u32[]{:S(2)}) collective-permute-start(bf16[256,3072]{1,0:T(8,128)(2,1)S(1)} %bitcast.25), channel_id=1, source_target_pairs={{0,1},{1,0},{2,3},{3,2},{4,5},{5,4},{6,7},{7,6},{8,9},{9,8},{10,11... | collective-permute-start | bytes 4718600 | tf_op jit(solution)/shard_map/ppermute | solution.py:32
  117.7 51.5 %collective-permute-start.27 = (bf16[256,3072]{1,0:T(8,128)(2,1)S(1)}, bf16[256,3072]{1,0:T(8,128)(2,1)}, u32[]{:S(2)}, u32[]{:S(2)}) collective-permute-start(bf16[256,3072]{1,0:T(8,128)(2,1)S(1)} %bitcast.28), channel_id=1, source_target_pairs={{0,1},{1,0},{2,3},{3,2},{4,5},{5,4},{6,7},{7,6},{8,9},{9,8},{10,11... | collective-permute-start | bytes 4718600 | tf_op jit(solution)/shard_map/ppermute | solution.py:32
  156.1 28.3 %collective-permute-start.28 = (bf16[256,3072]{1,0:T(8,128)(2,1)}, bf16[256,3072]{1,0:T(8,128)(2,1)}, u32[]{:S(2)}, u32[]{:S(2)}) collective-permute-start(bf16[256,3072]{1,0:T(8,128)(2,1)} %collective-permute-done.24.refs_2_), channel_id=1, source_target_pairs={{0,1},{1,0},{2,3},{3,2},{4,5},{5,4},{6,7},{7,6},{8,9},{9,8},{10,11... | collective-permute-start | bytes 4718600 | tf_op jit(solution)/shard_map/ppermute | solution.py:32
  156.2 28.2 %collective-permute-start.29 = (bf16[256,3072]{1,0:T(8,128)(2,1)}, bf16[256,3072]{1,0:T(8,128)(2,1)}, u32[]{:S(2)}, u32[]{:S(2)}) collective-permute-start(bf16[256,3072]{1,0:T(8,128)(2,1)} %collective-permute-done.25.refs_3_), channel_id=1, source_target_pairs={{0,1},{1,0},{2,3},{3,2},{4,5},{5,4},{6,7},{7,6},{8,9},{9,8},{10,11... | collective-permute-start | bytes 4718600 | tf_op jit(solution)/shard_map/ppermute | solution.py:32
  158.6 4.1 %collective-permute-start.20 = (bf16[8,3,64,128]{3,2,1,0:T(8,128)(2,1)}, bf16[8,3,64,128]{3,2,1,0:T(8,128)(2,1)}, u32[]{:S(2)}, u32[]{:S(2)}) collective-permute-start(bf16[8,3,64,128]{3,2,1,0:T(8,128)(2,1)} %get-tuple-element.48), channel_id=1, source_target_pairs={{0,1},{1,0},{2,3},{3,2},{4,5},{5,4},{6,7},{7,6},{8,9},{9,8},{10,11... | collective-permute-start | bytes 1179656 | tf_op jit(solution)/shard_map/ppermute | solution.py:32
  164.9 19.5 %all-to-all-start = ((bf16[16,192,128]{2,1,0:T(8,128)(2,1)}), bf16[16,192,128]{2,1,0:T(8,128)(2,1)}, u32[]{:S(2)}, u32[]{:S(2)}) async-start(bf16[16,192,128]{2,1,0:T(8,128)(2,1)} %bitcast.30), calls=%async_computation | async-start | bytes 1572864 | tf_op jit(solution)/shard_map/all_to_all | solution.py:415
  (13 other events, 186.4 us)

commit v3 on v2

--- a/solution.py
+++ b/solution.py
@@ -14,6 +14,11 @@
 AXES = ("x", "yh", "yl", "z", "c")
 SIZES = (4, 2, 2, 4, 2)
 VMEM = 60 * 1024 * 1024
+MIXERS = [
+    [((x * 4 + (yh ^ c) * 2 + yl) * 4 + z) * 2 + c for yh in range(2) for yl in range(2) for z in range(4)]
+    for x in range(4)
+    for c in range(2)
+]
 
 
 def move(value, target):
@@ -167,7 +172,7 @@
 
 
 def attend_body(
-    near, far, s_near, s_far, x_near, x_far, picks_hbm, perm, out,
+    near, far, s_near, s_far, x_near, x_far, picks_hbm, perm, keep, send,
     q_buf, kv, v_t, even, odd, picks, sem,
 ):
     copies = []
@@ -196,9 +201,9 @@
                     chunk.at[h, :, blocks[0] : blocks[1]],
                     kv.at[g, pl.ds(h * 6 + row * 3, 3), pl.ds(off, blocks[1] - blocks[0])],
                 )
-    for copy in copies:
-        copy.wait()
-    for g in range(3):
+    for g, upto in ((0, 17), (1, 25), (2, 33)):
+        for copy in copies[(0, 17, 25)[g] : upto]:
+            copy.wait()
 
         @pl.loop(0, NT)
         def _(t):
@@ -252,7 +257,7 @@
                 v_t[g, where[j]], p.astype(jnp.bfloat16), preferred_element_type=jnp.float32
             )
         attn = (acc / jnp.sum(total, axis=0, keepdims=True)).astype(jnp.bfloat16)
-        raster = perm[pl.ds(t, 1), :]
+        raster = perm[:, pl.ds(pl.multiple_of(t * TILE, TILE), TILE)]
         frame = (
             (raster >= 768).astype(jnp.int32)
             + (raster >= 1536).astype(jnp.int32)
@@ -272,7 +277,16 @@
         for i in range(4):
             piece = 4 * t + i
             owner = piece // 3
-            out[(owner % 2) ^ core, owner // 2, piece % 3] = ordered[i * 64 : i * 64 + 64]
+            rows = ordered[i * 64 : i * 64 + 64]
+
+            @pl.when((owner % 2) == core)
+            def _():
+                keep[owner // 2, piece % 3] = rows
+
+            @pl.when((owner % 2) != core)
+            def _():
+                send[owner // 2, piece % 3] = rows
+
         return tuple(tops_next)
 
     tops = [None, None]
@@ -290,16 +304,15 @@
 def attend(near, far, s_near, s_far, x_near, x_far, picks, perm):
     any_spec = pl.BlockSpec(memory_space=pl.ANY)
     vmem_spec = pl.BlockSpec(memory_space=pltpu.VMEM)
-    keys = 3 * WIN * TILE
 
     def body(n0, n1, f0, f1, *refs):
         attend_body((n0, n1), (f0, f1), *refs)
 
     return pl.pallas_call(
         body,
-        out_shape=jax.ShapeDtypeStruct((2, 8, 3, 64, HD), jnp.bfloat16),
+        out_shape=[jax.ShapeDtypeStruct((8, 3, 64, HD), jnp.bfloat16)] * 2,
         in_specs=[any_spec] * 9 + [vmem_spec],
-        out_specs=vmem_spec,
+        out_specs=[vmem_spec] * 2,
         scratch_shapes=[
             pltpu.VMEM((NT, 4, 64, HD), jnp.bfloat16),
             pltpu.VMEM((3, NT, 4, 64, 2 * HD), jnp.bfloat16),
@@ -311,9 +324,7 @@
         ],
         compiler_params=pltpu.CompilerParams(vmem_limit_bytes=VMEM),
         cost_estimate=pl.CostEstimate(
-            flops=4 * NT * TILE * keys * HD,
-            bytes_accessed=6_000_000,
-            transcendentals=NT * TILE * keys,
+            flops=32_000_000_000, bytes_accessed=6_000_000, transcendentals=0
         ),
         name="attend",
     )(*near, *far, s_near, s_far, x_near, x_far, picks, perm)
@@ -321,13 +332,12 @@
 
 def mix_body(attn, *refs):
     out = refs[8]
-    core, half, z = lax.axis_index("c"), lax.axis_index("yl"), lax.axis_index("z")
+    half, z = lax.axis_index("yl"), lax.axis_index("z")
     total = None
     for i in range(8):
         side, pair = i // 4, i % 4
-        kind = core ^ side
         heads = [
-            attn[kind, (half ^ (pair // 2)) * 4 + (z ^ k)] for k in ((0, 1), (3, 2))[pair % 2]
+            attn[side, (half ^ (pair // 2)) * 4 + (z ^ k)] for k in ((0, 1), (3, 2))[pair % 2]
         ]
         flat = jnp.concatenate(heads, axis=-1)
         part = jnp.dot(flat, refs[i][...], preferred_element_type=jnp.float32)
@@ -364,15 +374,15 @@
     own_other = move(own, swap_core)
     low_w = move(own_w[: D // 2], up)
     high_w = move(own_w[D // 2 :], down)
-    near, rear, own_other, low_w, high_w, tile_perm, w_out = lax.optimization_barrier(
-        (near, rear, own_other, low_w, high_w, tile_perm, w_out)
+    raster = move(tile_perm, regroup(0))
+    near, rear, own_other, low_w, high_w, raster, w_out = lax.optimization_barrier(
+        (near, rear, own_other, low_w, high_w, raster, w_out)
     )
 
     far_a = move(rear[:96], across(1))
     far_b = move(near[96:], across(3))
     near_other = move(near, swap_core)
     rear_other = move(rear, swap_core)
-    raster = move(tile_perm.reshape(NT, TILE), regroup(0))
     close = project(
         [own, own_other, near, rear],
         [(0, 0), (1, 0), (2, 0), (3, 0)],
@@ -387,7 +397,6 @@
     w_own = after(w_out, far_a_other, far_b_other)
     w_near = move(w_own, across(1))
     w_rear = move(w_own, across(3))
-    w_far = move(w_own, across(2))
     distant = project(
         [near_other, rear_other, far_a, far_b, far_a_other, far_b_other],
         [(0, 0), (3, 0), (1, 0), (1, 32), (2, 0), (2, 32)],
@@ -397,25 +406,26 @@
     near_kv = jnp.stack([near0[..., HD:], near1[..., HD:]])
     s_near = move(near_kv, swap_core)
     x_near = move(near_kv, beside)
-    far0 = move(distant[0], regroup(0))
-    far1 = move(distant[1], regroup(1))
+    w_far = move(after(w_own, distant[0]), across(2))
+    far0 = move(after(distant[0], w_near, w_rear), regroup(0))
+    far1 = move(after(distant[1], w_near, w_rear), regroup(1))
     far_kv = jnp.stack([far0[..., HD:], far1[..., HD:]])
     s_far = move(far_kv, swap_core)
     x_far = move(far_kv, beside)
-    w_near, w_rear = after(w_near, far0, far1), after(w_rear, far0, far1)
+    w_near, w_rear, w_far = (after(w, far0, far1) for w in (w_near, w_rear, w_far))
     w_one = jnp.concatenate([w_own, w_near]).reshape(2 * HD, D)
     w_two = jnp.concatenate([w_rear, w_far]).reshape(2 * HD, D)
     w_three = move(w_one, up)
     w_four = move(w_two, down)
     w_here = [w_one, w_two, w_three, w_four]
     w_there = [move(w_one, swap_core), move(w_two, swap_core)]
-    attn = attend((near0, near1), (far0, far1), s_near, s_far, x_near, x_far, window, raster)
-    other = move(attn[1], swap_core)
-    both = jnp.where(c == 0, jnp.stack([attn[0], other]), jnp.stack([other, attn[0]]))
+    keep, send = attend((near0, near1), (far0, far1), s_near, s_far, x_near, x_far, window, raster)
+    received = move(send, swap_core)
+    both = jnp.concatenate([keep, received])
     spread = lax.all_to_all(
-        both.reshape(16, 192, HD), ("yh", "yl", "z"), 0, 0, tiled=True
-    )
-    w_there += [move(after(w_three, attn), swap_core), move(after(w_four, attn), swap_core)]
+        both.reshape(16, 192, HD), AXES, 0, 0, axis_index_groups=MIXERS, tiled=True
+    )
+    w_there += [move(after(w_three, received), swap_core), move(after(w_four, received), swap_core)]
     return mix(spread, w_here, w_there)[None]
 
 

time: 194 us -> 178 us (0.918)
  waiting for transfers between devices: 74.6 us -> 57.4 us
    ppermute x30, waiting for transfers between devices: 59.4 us -> 43.1 us  [move(): return lax.ppermute(value, AXES, pairs)]
    unnamed x29 -> x31, local copies, waits for them, and re-layouts: 0.74 us -> 3.42 us
    select_n x1 -> x0, other arithmetic: 2.13 us -> none  [per_device(): jnp.where(c == 0, jnp.stack([attn[0], other]), jnp.stack([other, attn[0]]))]
    concatenate x0 -> x1, other arithmetic: none -> 1.94 us  [per_device(): both = jnp.concatenate([keep, received])]
  transfers between devices with their start and end apart: 31 -> 31, of which waited for: 12 -> 10; matrix products, arithmetic and copies ran while one was open for 6% -> 5% of each run, Pallas kernels for 25% -> 27%
where the time goes in v3:
time: 178 us; the launch traced here: 177 us
  waiting for transfers between devices  57.4 us (32%)
  Pallas kernels  56.8 us (32%)
  starting transfers between devices  50.3 us (28%)
  local copies, waits for them, and re-layouts  7.66 us (4%)
  other arithmetic  4.25 us (2%)
    ppermute x30, starting transfers between devices, move(): return lax.ppermute(value, AXES, pairs)  46 us
    ppermute x30, waiting for transfers between devices, move(): return lax.ppermute(value, AXES, pairs)  43.1 us
    pallas_call x1, Pallas kernels, attend(): pl.pallas_call(body, out_shape=[jax.ShapeDtypeStruct((8, 3, 64, HD), jnp....  27 us
    pallas_call x2, Pallas kernels, project(): pl.pallas_call(body, out_shape=[jax.ShapeDtypeStruct((3, 4, 64, 384), jnp...  21.1 us
    all_to_all x1, waiting for transfers between devices, per_device(): lax.all_to_all(both.reshape(16, 192, HD), AXES, 0, 0, axis_index_groups=M...  14.2 us
    pallas_call x1, Pallas kernels, mix(): pl.pallas_call(mix_body, out_shape=jax.ShapeDtypeStruct((192, D), jnp.bfl...  8.77 us
    all_to_all x1, starting transfers between devices, per_device(): lax.all_to_all(both.reshape(16, 192, HD), AXES, 0, 0, axis_index_groups=M...  4.28 us
  transfers between devices with their start and end apart: 31, of which 10 were waited for; matrix products, arithmetic and copies ran while one was open for 5% of the time, Pallas kernels for 27%

profile of v3, /device:TPU:0, one launch (start us, length us, event | category | flops | bytes accessed | tf_op | source)
XLA Modules:
  0.0 176.6 jit_solution(2843970290886235616)
XLA Ops:
  0.0 4.1 %collective-permute-start.1 = (bf16[192,3072]{1,0:T(8,128)(2,1)}, bf16[192,3072]{1,0:T(8,128)(2,1)S(1)}, u32[]{:S(2)}, u32[]{:S(2)}) collective-permute-start(bf16[192,3072]{1,0:T(8,128)(2,1)} %bitcast.31), channel_id=1, source_target_pairs={{0,6},{1,7},{2,4},{3,5},{4,2},{5,3},{6,0},{7,1},{8,14},{9,15},{10,... | collective-permute-start | bytes 3538952 | tf_op jit(solution)/shard_map/ppermute | solution.py:37
  4.1 1.4 collective-permute-start.5
  5.5 1.9 %slice_bitcast_fusion = (bf16[1536,384]{1,0:T(8,128)(2,1)S(1)}, bf16[1536,384]{1,0:T(8,128)(2,1)S(1)}) fusion(bf16[3072,1,384]{2,0,1:T(8,128)(2,1)} %param.8), kind=kLoop, calls=%fused_computation.2 | loop fusion | bytes 4718592 | tf_op jit(solution)/shard_map/slice | solution.py:376
  7.3 4.7 %collective-permute-start.4 = (bf16[1536,384]{1,0:T(8,128)(2,1)S(1)}, bf16[1536,384]{1,0:T(8,128)(2,1)S(1)}, u32[]{:S(2)}, u32[]{:S(2)}) collective-permute-start(bf16[1536,384]{1,0:T(8,128)(2,1)S(1)} %get-tuple-element.57), channel_id=1, source_target_pairs={{0,24},{1,25},{2,26},{3,27},{4,28},{5,29},{6,30},{7,31},{8,0},{9,1... | collective-permute-start | bytes 3538952 | tf_op jit(solution)/shard_map/ppermute | solution.py:37
  12.1 18.9 %collective-permute-done.1.refs_3_ = bf16[192,3072]{1,0:T(8,128)(2,1)S(1)} collective-permute-done((bf16[192,3072]{1,0:T(8,128)(2,1)}, bf16[192,3072]{1,0:T(8,128)(2,1)S(1)}, u32[]{:S(2)}, u32[]{:S(2)}) %collective-permute-start.1) | collective-permute-done | bytes 1179680 | tf_op jit(solution)/shard_map/ppermute | solution.py:37
  31.0 1.6 collective-permute-done.refs_2_
  32.5 4.4 %collective-permute-done.4.refs_6_.refs_8_ = bf16[1536,384]{1,0:T(8,128)(2,1)S(1)} collective-permute-done((bf16[1536,384]{1,0:T(8,128)(2,1)S(1)}, bf16[1536,384]{1,0:T(8,128)(2,1)S(1)}, u32[]{:S(2)}, u32[]{:S(2)}) %collective-permute-start.4) | collective-permute-done | bytes 1179680 | tf_op jit(solution)/shard_map/ppermute | solution.py:37
  38.0 2.6 %collective-permute-done.3.refs_5_.refs_7_ = bf16[1536,384]{1,0:T(8,128)(2,1)} collective-permute-done((bf16[1536,384]{1,0:T(8,128)(2,1)S(1)}, bf16[1536,384]{1,0:T(8,128)(2,1)}, u32[]{:S(2)}, u32[]{:S(2)}) %collective-permute-start.3) | collective-permute-done | bytes 1179680 | tf_op jit(solution)/shard_map/ppermute | solution.py:37
  40.6 2.1 %collective-permute-start.9 = (bf16[96,3072]{1,0:T(8,128)(2,1)S(1)}, bf16[96,3072]{1,0:T(8,128)(2,1)}, u32[]{:S(2)}, u32[]{:S(2)}) collective-permute-start(bf16[96,3072]{1,0:T(8,128)(2,1)S(1)} %slice.34), channel_id=1, source_target_pairs={{0,2},{1,3},{2,0},{3,1},{4,6},{5,7},{6,4},{7,5},{8,10},{9,11},{10,... | collective-permute-start | bytes 1769480 | tf_op jit(solution)/shard_map/ppermute | solution.py:37
  42.7 1.1 slice.35
  44.5 10.5 %project.2 = (bf16[3,4,64,384]{3,2,1,0:T(8,128)(2,1)}, bf16[3,4,64,384]{3,2,1,0:T(8,128)(2,1)}) custom-call(bf16[192,3072]{1,0:T(8,128)(2,1)} %bitcast.33, bf16[192,3072]{1,0:T(8,128)(2,1)} %copy-done.11, bf16[192,3072]{1,0:T(8,128)(2,1)} %collective-permute-done.refs_2_, bf16[192,3072]{1,0:T(8,128)(2,1)} %copy-done.6, bf16[3072,384]{1,0:T(8,128)(2,1)} %bitcast.28, ...), custom_call_target="tpu_custom_call" | custom-call | flops 3623878656 | bytes 9437184 | tf_op jit(solution)/shard_map/project/pallas_call | solution.py:151
  55.2 3.7 %collective-permute-done.10.refs_3_ = bf16[96,3072]{1,0:T(8,128)(2,1)} collective-permute-done((bf16[96,3072]{1,0:T(8,128)(2,1)S(1)}, bf16[96,3072]{1,0:T(8,128)(2,1)}, u32[]{:S(2)}, u32[]{:S(2)}) %collective-permute-start.10) | collective-permute-done | bytes 589856 | tf_op jit(solution)/shard_map/ppermute | solution.py:37
  59.7 1.4 collective-permute-done.12.refs_5_
  62.2 1.5 collective-permute-start.13
  63.7 5.9 %collective-permute-start.6 = (bf16[3,4,64,384]{3,2,1,0:T(8,128)(2,1)}, bf16[3,4,64,384]{3,2,1,0:T(8,128)(2,1)}, u32[]{:S(2)}, u32[]{:S(2)}) collective-permute-start(bf16[3,4,64,384]{3,2,1,0:T(8,128)(2,1)} %get-tuple-element.36), channel_id=1, source_target_pairs={{0,0},{1,16},{2,2},{3,18},{4,4},{5,20},{6,6},{7,22},{8,8},{9,24},{... | collective-permute-start | bytes 1769480 | tf_op jit(solution)/shard_map/ppermute | solution.py:37
  69.7 10.6 %project.3 = (bf16[3,4,64,384]{3,2,1,0:T(8,128)(2,1)}, bf16[3,4,64,384]{3,2,1,0:T(8,128)(2,1)}) custom-call(bf16[192,3072]{1,0:T(8,128)(2,1)} %collective-permute-done.7.refs_0_, bf16[192,3072]{1,0:T(8,128)(2,1)} %collective-permute-done.8.refs_1_, bf16[96,3072]{1,0:T(8,128)(2,1)} %collective-permute-done.9.refs_2_, ...), custom_call_target="tpu_custom_call" | custom-call | flops 3623878656 | bytes 9437184 | tf_op jit(solution)/shard_map/project/pallas_call | solution.py:151
  80.3 2.4 %collective-permute-done.15 = bf16[1,128,3072]{2,1,0:T(8,128)(2,1)S(1)} collective-permute-done((bf16[1,128,3072]{2,1,0:T(8,128)(2,1)S(1)}, bf16[1,128,3072]{2,1,0:T(8,128)(2,1)S(1)}, u32[]{:S(2)}, u32[]{:S(2)}) %collective-permute-start.15) | collective-permute-done | bytes 786464 | tf_op jit(solution)/shard_map/ppermute | solution.py:37
  82.7 1.9 %collective-permute-start.16 = (bf16[3,4,64,384]{3,2,1,0:T(8,128)(2,1)}, bf16[3,4,64,384]{3,2,1,0:T(8,128)(2,1)S(1)}, u32[]{:S(2)}, u32[]{:S(2)}) collective-permute-start(bf16[3,4,64,384]{3,2,1,0:T(8,128)(2,1)} %get-tuple-element.45), channel_id=1, source_target_pairs={{0,0},{1,16},{2,2},{3,18},{4,4},{5,20},{6,6},{7,22},{8,8},{9,24},{... | collective-permute-start | bytes 1769480 | tf_op jit(solution)/shard_map/ppermute | solution.py:37
  84.6 1.8 %collective-permute-start.23 = (bf16[1,128,3072]{2,1,0:T(8,128)(2,1)S(1)}, bf16[1,128,3072]{2,1,0:T(8,128)(2,1)S(1)}, u32[]{:S(2)}, u32[]{:S(2)}) collective-permute-start(bf16[1,128,3072]{2,1,0:T(8,128)(2,1)S(1)} %copy-done.2), channel_id=1, source_target_pairs={{0,4},{1,5},{2,6},{3,7},{4,0},{5,1},{6,2},{7,3},{8,12},{9,13},{10,... | collective-permute-start | bytes 2359304 | tf_op jit(solution)/shard_map/ppermute | solution.py:37
  87.4 1.2 slice_bitcast_fusion.4
  89.5 1.8 collective-permute-start.20
  91.3 2.4 %collective-permute-start.18 = (bf16[2,3,4,64,256]{4,3,2,1,0:T(8,128)(2,1)}, bf16[2,3,4,64,256]{4,3,2,1,0:T(8,128)(2,1)}, u32[]{:S(2)}, u32[]{:S(2)}) collective-permute-start(bf16[2,3,4,64,256]{4,3,2,1,0:T(8,128)(2,1)} %pad_maximum_fusion.2), channel_id=1, source_target_pairs={{0,1},{1,0},{2,3},{3,2},{4,5},{5,4},{6,7},{7,6},{8,9},{9,8},{10,11... | collective-permute-start | bytes 2359304 | tf_op jit(solution)/shard_map/ppermute | solution.py:37
  93.7 7.1 %collective-permute-done.17.f1 = bf16[3,4,64,384]{3,2,1,0:T(8,128)(2,1)S(1)} collective-permute-done((bf16[3,4,64,384]{3,2,1,0:T(8,128)(2,1)}, bf16[3,4,64,384]{3,2,1,0:T(8,128)(2,1)S(1)}, u32[]{:S(2)}, u32[]{:S(2)}) %collective-permute-start.17) | collective-permute-done | bytes 589856 | tf_op jit(solution)/shard_map/ppermute | solution.py:37
  101.9 1.5 collective-permute-start.21
  103.4 3.0 %collective-permute-start.19 = (bf16[2,3,4,64,256]{4,3,2,1,0:T(8,128)(2,1)}, bf16[2,3,4,64,256]{4,3,2,1,0:T(8,128)(2,1)}, u32[]{:S(2)}, u32[]{:S(2)}) collective-permute-start(bf16[2,3,4,64,256]{4,3,2,1,0:T(8,128)(2,1)} %pad_maximum_fusion.3), channel_id=1, source_target_pairs={{0,1},{1,0},{2,3},{3,2},{4,5},{5,4},{6,7},{7,6},{8,9},{9,8},{10,11... | collective-permute-start | bytes 2359304 | tf_op jit(solution)/shard_map/ppermute | solution.py:37
  107.3 2.2 %collective-permute-start.25 = (bf16[256,3072]{1,0:T(8,128)(2,1)S(1)}, bf16[256,3072]{1,0:T(8,128)(2,1)}, u32[]{:S(2)}, u32[]{:S(2)}) collective-permute-start(bf16[256,3072]{1,0:T(8,128)(2,1)S(1)} %bitcast.21), channel_id=1, source_target_pairs={{0,24},{1,25},{2,26},{3,27},{4,28},{5,29},{6,30},{7,31},{8,0},{9,1... | collective-permute-start | bytes 4718600 | tf_op jit(solution)/shard_map/ppermute | solution.py:37
  109.8 27.0 %attend.1 = (bf16[8,3,64,128]{3,2,1,0:T(8,128)(2,1)}, bf16[8,3,64,128]{3,2,1,0:T(8,128)(2,1)}) custom-call(bf16[3,4,64,384]{3,2,1,0:T(8,128)(2,1)} %collective-permute-done.6.n0, bf16[3,4,64,384]{3,2,1,0:T(8,128)(2,1)} %collective-permute-done.13.n1, bf16[3,4,64,384]{3,2,1,0:T(8,128)(2,1)} %copy-done.7, bf16[3,4,64,384]{3,2,1,0:T(8,128)(2,1)} %copy-done.8, ...), custom_call_target="tpu_custom_call" | custom-call | flops 32000000000 | bytes 6000000 | tf_op jit(solution)/shard_map/attend/pallas_call | solution.py:311
  136.7 8.6 %collective-permute-start.22 = (bf16[8,3,64,128]{3,2,1,0:T(8,128)(2,1)}, bf16[8,3,64,128]{3,2,1,0:T(8,128)(2,1)S(1)}, u32[]{:S(2)}, u32[]{:S(2)}) collective-permute-start(bf16[8,3,64,128]{3,2,1,0:T(8,128)(2,1)} %get-tuple-element.50), channel_id=1, source_target_pairs={{0,1},{1,0},{2,3},{3,2},{4,5},{5,4},{6,7},{7,6},{8,9},{9,8},{10,11... | collective-permute-start | bytes 1179656 | tf_op jit(solution)/shard_map/ppermute | solution.py:37
  147.4 1.9 %pad_maximum_fusion.4 = bf16[16,3,64,128]{3,2,1,0:T(8,128)(2,1)} fusion(bf16[8,3,64,128]{3,2,1,0:T(8,128)(2,1)S(1)} %collective-permute-done.22, bf16[8,3,64,128]{3,2,1,0:T(8,128)(2,1)} %get-tuple-element.49), kind=kLoop, calls=%fused_computation.6 | loop fusion | flops 393216 | bytes 1572864 | tf_op jit(solution)/shard_map/concatenate | solution.py:424
  149.3 4.3 %all-to-all-start = ((bf16[16,192,128]{2,1,0:T(8,128)(2,1)}), bf16[16,192,128]{2,1,0:T(8,128)(2,1)}, u32[]{:S(2)}, u32[]{:S(2)}) async-start(bf16[16,192,128]{2,1,0:T(8,128)(2,1)} %bitcast.27), calls=%async_computation | async-start | bytes 1572864 | tf_op jit(solution)/shard_map/all_to_all | solution.py:425
  153.6 14.2 %all-to-all-done = bf16[16,192,128]{2,1,0:T(8,128)(2,1)} async-done(((bf16[16,192,128]{2,1,0:T(8,128)(2,1)}), bf16[16,192,128]{2,1,0:T(8,128)(2,1)}, u32[]{:S(2)}, u32[]{:S(2)}) %all-to-all-start) | async-done | bytes 786464 | tf_op jit(solution)/shard_map/all_to_all | solution.py:425
  167.9 8.8 %mix.1 = bf16[192,3072]{1,0:T(8,128)(2,1)} custom-call(bf16[2,8,192,128]{3,2,1,0:T(8,128)(2,1)} %bitcast.11.attn, bf16[256,3072]{1,0:T(8,128)(2,1)} %bitcast.26, bf16[256,3072]{1,0:T(8,128)(2,1)} %bitcast.23, bf16[256,3072]{1,0:T(8,128)(2,1)} %collective-permute-done.24.refs_2_, bf16[256,3072]{1,0:T(8,128)(2,1)} %collective-permute-done.25.refs_3_, ...), custom_call_target="tpu_custom_call" | custom-call | flops 2415919104 | bytes 14000000 | tf_op jit(solution)/shard_map/mix/pallas_call | solution.py:350
  (76 shorter events, 10.2 us)
Async XLA Ops:
  0.0 12.1 %collective-permute-start.2 = (bf16[192,3072]{1,0:T(8,128)(2,1)}, bf16[192,3072]{1,0:T(8,128)(2,1)S(1)}, u32[]{:S(2)}, u32[]{:S(2)}) collective-permute-start(bf16[192,3072]{1,0:T(8,128)(2,1)} %bitcast.30), channel_id=1, source_target_pairs={{0,1},{1,0},{2,3},{3,2},{4,5},{5,4},{6,7},{7,6},{8,9},{9,8},{10,11... | collective-permute-start | bytes 3538952 | tf_op jit(solution)/shard_map/ppermute | solution.py:37
  0.0 31.0 %collective-permute-start.1 = (bf16[192,3072]{1,0:T(8,128)(2,1)}, bf16[192,3072]{1,0:T(8,128)(2,1)S(1)}, u32[]{:S(2)}, u32[]{:S(2)}) collective-permute-start(bf16[192,3072]{1,0:T(8,128)(2,1)} %bitcast.31), channel_id=1, source_target_pairs={{0,6},{1,7},{2,4},{3,5},{4,2},{5,3},{6,0},{7,1},{8,14},{9,15},{10,... | collective-permute-start | bytes 3538952 | tf_op jit(solution)/shard_map/ppermute | solution.py:37
  4.1 28.4 %collective-permute-start = (bf16[192,3072]{1,0:T(8,128)(2,1)}, bf16[192,3072]{1,0:T(8,128)(2,1)}, u32[]{:S(2)}, u32[]{:S(2)}) collective-permute-start(bf16[192,3072]{1,0:T(8,128)(2,1)} %bitcast.32), channel_id=1, source_target_pairs={{0,2},{1,3},{2,0},{3,1},{4,6},{5,7},{6,4},{7,5},{8,10},{9,11},{10,... | collective-permute-start | bytes 3538952 | tf_op jit(solution)/shard_map/ppermute | solution.py:37
  4.1 7.9 %collective-permute-start.5 = (s32[1,3072]{1,0:T(1,128)}, s32[1,3072]{1,0:T(1,128)S(1)}, u32[]{:S(2)}, u32[]{:S(2)}) collective-permute-start(s32[1,3072]{1,0:T(1,128)} %param.12), channel_id=1, source_target_pairs={{0,0},{1,16},{2,2},{3,18},{4,4},{5,20},{6,6},{7,22},{8,8},{9,24},{... | collective-permute-start | bytes 36872 | tf_op jit(solution)/shard_map/ppermute | solution.py:37
  7.3 29.6 %collective-permute-start.4 = (bf16[1536,384]{1,0:T(8,128)(2,1)S(1)}, bf16[1536,384]{1,0:T(8,128)(2,1)S(1)}, u32[]{:S(2)}, u32[]{:S(2)}) collective-permute-start(bf16[1536,384]{1,0:T(8,128)(2,1)S(1)} %get-tuple-element.57), channel_id=1, source_target_pairs={{0,24},{1,25},{2,26},{3,27},{4,28},{5,29},{6,30},{7,31},{8,0},{9,1... | collective-permute-start | bytes 3538952 | tf_op jit(solution)/shard_map/ppermute | solution.py:37
  12.1 43.0 %copy-start.14 = (s32[1,3072]{1,0:T(1,128)}, s32[1,3072]{1,0:T(1,128)S(1)}, u32[]{:S(2)}) copy-start(s32[1,3072]{1,0:T(1,128)S(1)} %collective-permute-done.5.refs_5_) | copy-start | bytes 36868
  12.1 28.5 %collective-permute-start.3 = (bf16[1536,384]{1,0:T(8,128)(2,1)S(1)}, bf16[1536,384]{1,0:T(8,128)(2,1)}, u32[]{:S(2)}, u32[]{:S(2)}) collective-permute-start(bf16[1536,384]{1,0:T(8,128)(2,1)S(1)} %get-tuple-element.58), channel_id=1, source_target_pairs={{0,8},{1,9},{2,10},{3,11},{4,12},{5,13},{6,14},{7,15},{8,16},{9,17... | collective-permute-start | bytes 3538952 | tf_op jit(solution)/shard_map/ppermute | solution.py:37
  40.6 14.4 %collective-permute-start.9 = (bf16[96,3072]{1,0:T(8,128)(2,1)S(1)}, bf16[96,3072]{1,0:T(8,128)(2,1)}, u32[]{:S(2)}, u32[]{:S(2)}) collective-permute-start(bf16[96,3072]{1,0:T(8,128)(2,1)S(1)} %slice.34), channel_id=1, source_target_pairs={{0,2},{1,3},{2,0},{3,1},{4,6},{5,7},{6,4},{7,5},{8,10},{9,11},{10,... | collective-permute-start | bytes 1769480 | tf_op jit(solution)/shard_map/ppermute | solution.py:37
  43.8 15.0 %collective-permute-start.10 = (bf16[96,3072]{1,0:T(8,128)(2,1)S(1)}, bf16[96,3072]{1,0:T(8,128)(2,1)}, u32[]{:S(2)}, u32[]{:S(2)}) collective-permute-start(bf16[96,3072]{1,0:T(8,128)(2,1)S(1)} %slice.35), channel_id=1, source_target_pairs={{0,6},{1,7},{2,4},{3,5},{4,2},{5,3},{6,0},{7,1},{8,14},{9,15},{10,... | collective-permute-start | bytes 1769480 | tf_op jit(solution)/shard_map/ppermute | solution.py:37
  44.0 19.7 %collective-permute-start.7 = (bf16[192,3072]{1,0:T(8,128)(2,1)}, bf16[192,3072]{1,0:T(8,128)(2,1)}, u32[]{:S(2)}, u32[]{:S(2)}) collective-permute-start(bf16[192,3072]{1,0:T(8,128)(2,1)} %collective-permute-done.refs_2_), channel_id=1, source_target_pairs={{0,1},{1,0},{2,3},{3,2},{4,5},{5,4},{6,7},{7,6},{8,9},{9,8},{10,11... | collective-permute-start | bytes 3538952 | tf_op jit(solution)/shard_map/ppermute | solution.py:37
  44.0 25.7 %collective-permute-start.8 = (bf16[192,3072]{1,0:T(8,128)(2,1)S(1)}, bf16[192,3072]{1,0:T(8,128)(2,1)}, u32[]{:S(2)}, u32[]{:S(2)}) collective-permute-start(bf16[192,3072]{1,0:T(8,128)(2,1)S(1)} %collective-permute-done.1.refs_3_), channel_id=1, source_target_pairs={{0,1},{1,0},{2,3},{3,2},{4,5},{5,4},{6,7},{7,6},{8,9},{9,8},{10,11... | collective-permute-start | bytes 3538952 | tf_op jit(solution)/shard_map/ppermute | solution.py:37
  55.0 3.8 %collective-permute-start.11 = (bf16[96,3072]{1,0:T(8,128)(2,1)}, bf16[96,3072]{1,0:T(8,128)(2,1)S(1)}, u32[]{:S(2)}, u32[]{:S(2)}) collective-permute-start(bf16[96,3072]{1,0:T(8,128)(2,1)} %collective-permute-done.9.refs_2_), channel_id=1, source_target_pairs={{0,1},{1,0},{2,3},{3,2},{4,5},{5,4},{6,7},{7,6},{8,9},{9,8},{10,11... | collective-permute-start | bytes 1769480 | tf_op jit(solution)/shard_map/ppermute | solution.py:37
  58.9 2.2 %collective-permute-start.12 = (bf16[96,3072]{1,0:T(8,128)(2,1)}, bf16[96,3072]{1,0:T(8,128)(2,1)S(1)}, u32[]{:S(2)}, u32[]{:S(2)}) collective-permute-start(bf16[96,3072]{1,0:T(8,128)(2,1)} %collective-permute-done.10.refs_3_), channel_id=1, source_target_pairs={{0,1},{1,0},{2,3},{3,2},{4,5},{5,4},{6,7},{7,6},{8,9},{9,8},{10,11... | collective-permute-start | bytes 1769480 | tf_op jit(solution)/shard_map/ppermute | solution.py:37
  61.9 20.8 %collective-permute-start.15 = (bf16[1,128,3072]{2,1,0:T(8,128)(2,1)S(1)}, bf16[1,128,3072]{2,1,0:T(8,128)(2,1)S(1)}, u32[]{:S(2)}, u32[]{:S(2)}) collective-permute-start(bf16[1,128,3072]{2,1,0:T(8,128)(2,1)S(1)} %copy-done.2), channel_id=1, source_target_pairs={{0,6},{1,7},{2,4},{3,5},{4,2},{5,3},{6,0},{7,1},{8,14},{9,15},{10,... | collective-permute-start | bytes 2359304 | tf_op jit(solution)/shard_map/ppermute | solution.py:37
  62.2 20.5 %collective-permute-start.14 = (bf16[1,128,3072]{2,1,0:T(8,128)(2,1)S(1)}, bf16[1,128,3072]{2,1,0:T(8,128)(2,1)S(1)}, u32[]{:S(2)}, u32[]{:S(2)}) collective-permute-start(bf16[1,128,3072]{2,1,0:T(8,128)(2,1)S(1)} %copy-done.2), channel_id=1, source_target_pairs={{0,2},{1,3},{2,0},{3,1},{4,6},{5,7},{6,4},{7,5},{8,10},{9,11},{10,... | collective-permute-start | bytes 2359304 | tf_op jit(solution)/shard_map/ppermute | solution.py:37
  62.2 22.4 %collective-permute-start.13 = (bf16[3,4,64,384]{3,2,1,0:T(8,128)(2,1)}, bf16[3,4,64,384]{3,2,1,0:T(8,128)(2,1)}, u32[]{:S(2)}, u32[]{:S(2)}) collective-permute-start(bf16[3,4,64,384]{3,2,1,0:T(8,128)(2,1)} %get-tuple-element.41), channel_id=1, source_target_pairs={{0,8},{1,24},{2,10},{3,26},{4,12},{5,28},{6,14},{7,30},{8,0},{9,16... | collective-permute-start | bytes 1769480 | tf_op jit(solution)/shard_map/ppermute | solution.py:37
  63.7 20.9 %collective-permute-start.6 = (bf16[3,4,64,384]{3,2,1,0:T(8,128)(2,1)}, bf16[3,4,64,384]{3,2,1,0:T(8,128)(2,1)}, u32[]{:S(2)}, u32[]{:S(2)}) collective-permute-start(bf16[3,4,64,384]{3,2,1,0:T(8,128)(2,1)} %get-tuple-element.36), channel_id=1, source_target_pairs={{0,0},{1,16},{2,2},{3,18},{4,4},{5,20},{6,6},{7,22},{8,8},{9,24},{... | collective-permute-start | bytes 1769480 | tf_op jit(solution)/shard_map/ppermute | solution.py:37
  82.7 10.9 %collective-permute-start.16 = (bf16[3,4,64,384]{3,2,1,0:T(8,128)(2,1)}, bf16[3,4,64,384]{3,2,1,0:T(8,128)(2,1)S(1)}, u32[]{:S(2)}, u32[]{:S(2)}) collective-permute-start(bf16[3,4,64,384]{3,2,1,0:T(8,128)(2,1)} %get-tuple-element.45), channel_id=1, source_target_pairs={{0,0},{1,16},{2,2},{3,18},{4,4},{5,20},{6,6},{7,22},{8,8},{9,24},{... | collective-permute-start | bytes 1769480 | tf_op jit(solution)/shard_map/ppermute | solution.py:37
  84.6 22.5 %collective-permute-start.23 = (bf16[1,128,3072]{2,1,0:T(8,128)(2,1)S(1)}, bf16[1,128,3072]{2,1,0:T(8,128)(2,1)S(1)}, u32[]{:S(2)}, u32[]{:S(2)}) collective-permute-start(bf16[1,128,3072]{2,1,0:T(8,128)(2,1)S(1)} %copy-done.2), channel_id=1, source_target_pairs={{0,4},{1,5},{2,6},{3,7},{4,0},{5,1},{6,2},{7,3},{8,12},{9,13},{10,... | collective-permute-start | bytes 2359304 | tf_op jit(solution)/shard_map/ppermute | solution.py:37
  86.4 14.4 %collective-permute-start.17 = (bf16[3,4,64,384]{3,2,1,0:T(8,128)(2,1)}, bf16[3,4,64,384]{3,2,1,0:T(8,128)(2,1)S(1)}, u32[]{:S(2)}, u32[]{:S(2)}) collective-permute-start(bf16[3,4,64,384]{3,2,1,0:T(8,128)(2,1)} %get-tuple-element.47), channel_id=1, source_target_pairs={{0,8},{1,24},{2,10},{3,26},{4,12},{5,28},{6,14},{7,30},{8,0},{9,16... | collective-permute-start | bytes 1769480 | tf_op jit(solution)/shard_map/ppermute | solution.py:37
  89.5 20.1 %collective-permute-start.20 = (bf16[2,3,4,64,256]{4,3,2,1,0:T(8,128)(2,1)}, bf16[2,3,4,64,256]{4,3,2,1,0:T(8,128)(2,1)}, u32[]{:S(2)}, u32[]{:S(2)}) collective-permute-start(bf16[2,3,4,64,256]{4,3,2,1,0:T(8,128)(2,1)} %pad_maximum_fusion.2), channel_id=1, source_target_pairs={{1,32},{3,34},{5,36},{7,38},{9,40},{11,42},{13,44},{15,46},{17,48}... | collective-permute-start | bytes 2359304 | tf_op jit(solution)/shard_map/ppermute | solution.py:37
  91.3 18.5 %collective-permute-start.18 = (bf16[2,3,4,64,256]{4,3,2,1,0:T(8,128)(2,1)}, bf16[2,3,4,64,256]{4,3,2,1,0:T(8,128)(2,1)}, u32[]{:S(2)}, u32[]{:S(2)}) collective-permute-start(bf16[2,3,4,64,256]{4,3,2,1,0:T(8,128)(2,1)} %pad_maximum_fusion.2), channel_id=1, source_target_pairs={{0,1},{1,0},{2,3},{3,2},{4,5},{5,4},{6,7},{7,6},{8,9},{9,8},{10,11... | collective-permute-start | bytes 2359304 | tf_op jit(solution)/shard_map/ppermute | solution.py:37
  101.9 7.9 %collective-permute-start.21 = (bf16[2,3,4,64,256]{4,3,2,1,0:T(8,128)(2,1)}, bf16[2,3,4,64,256]{4,3,2,1,0:T(8,128)(2,1)}, u32[]{:S(2)}, u32[]{:S(2)}) collective-permute-start(bf16[2,3,4,64,256]{4,3,2,1,0:T(8,128)(2,1)} %pad_maximum_fusion.3), channel_id=1, source_target_pairs={{1,32},{3,34},{5,36},{7,38},{9,40},{11,42},{13,44},{15,46},{17,48}... | collective-permute-start | bytes 2359304 | tf_op jit(solution)/shard_map/ppermute | solution.py:37
  103.4 6.3 %collective-permute-start.19 = (bf16[2,3,4,64,256]{4,3,2,1,0:T(8,128)(2,1)}, bf16[2,3,4,64,256]{4,3,2,1,0:T(8,128)(2,1)}, u32[]{:S(2)}, u32[]{:S(2)}) collective-permute-start(bf16[2,3,4,64,256]{4,3,2,1,0:T(8,128)(2,1)} %pad_maximum_fusion.3), channel_id=1, source_target_pairs={{0,1},{1,0},{2,3},{3,2},{4,5},{5,4},{6,7},{7,6},{8,9},{9,8},{10,11... | collective-permute-start | bytes 2359304 | tf_op jit(solution)/shard_map/ppermute | solution.py:37
  107.3 39.6 %collective-permute-start.25 = (bf16[256,3072]{1,0:T(8,128)(2,1)S(1)}, bf16[256,3072]{1,0:T(8,128)(2,1)}, u32[]{:S(2)}, u32[]{:S(2)}) collective-permute-start(bf16[256,3072]{1,0:T(8,128)(2,1)S(1)} %bitcast.21), channel_id=1, source_target_pairs={{0,24},{1,25},{2,26},{3,27},{4,28},{5,29},{6,30},{7,31},{8,0},{9,1... | collective-permute-start | bytes 4718600 | tf_op jit(solution)/shard_map/ppermute | solution.py:37
  109.6 37.6 %collective-permute-start.24 = (bf16[256,3072]{1,0:T(8,128)(2,1)S(1)}, bf16[256,3072]{1,0:T(8,128)(2,1)}, u32[]{:S(2)}, u32[]{:S(2)}) collective-permute-start(bf16[256,3072]{1,0:T(8,128)(2,1)S(1)} %bitcast.24), channel_id=1, source_target_pairs={{0,8},{1,9},{2,10},{3,11},{4,12},{5,13},{6,14},{7,15},{8,16},{9,17... | collective-permute-start | bytes 4718600 | tf_op jit(solution)/shard_map/ppermute | solution.py:37
  136.7 10.1 %collective-permute-start.22 = (bf16[8,3,64,128]{3,2,1,0:T(8,128)(2,1)}, bf16[8,3,64,128]{3,2,1,0:T(8,128)(2,1)S(1)}, u32[]{:S(2)}, u32[]{:S(2)}) collective-permute-start(bf16[8,3,64,128]{3,2,1,0:T(8,128)(2,1)} %get-tuple-element.50), channel_id=1, source_target_pairs={{0,1},{1,0},{2,3},{3,2},{4,5},{5,4},{6,7},{7,6},{8,9},{9,8},{10,11... | collective-permute-start | bytes 1179656 | tf_op jit(solution)/shard_map/ppermute | solution.py:37
  145.3 8.3 %collective-permute-start.27 = (bf16[256,3072]{1,0:T(8,128)(2,1)S(1)}, bf16[256,3072]{1,0:T(8,128)(2,1)}, u32[]{:S(2)}, u32[]{:S(2)}) collective-permute-start(bf16[256,3072]{1,0:T(8,128)(2,1)S(1)} %bitcast.22), channel_id=1, source_target_pairs={{0,1},{1,0},{2,3},{3,2},{4,5},{5,4},{6,7},{7,6},{8,9},{9,8},{10,11... | collective-permute-start | bytes 4718600 | tf_op jit(solution)/shard_map/ppermute | solution.py:37
  145.4 8.2 %collective-permute-start.26 = (bf16[256,3072]{1,0:T(8,128)(2,1)S(1)}, bf16[256,3072]{1,0:T(8,128)(2,1)}, u32[]{:S(2)}, u32[]{:S(2)}) collective-permute-start(bf16[256,3072]{1,0:T(8,128)(2,1)S(1)} %bitcast.25), channel_id=1, source_target_pairs={{0,1},{1,0},{2,3},{3,2},{4,5},{5,4},{6,7},{7,6},{8,9},{9,8},{10,11... | collective-permute-start | bytes 4718600 | tf_op jit(solution)/shard_map/ppermute | solution.py:37
  146.9 21.0 %collective-permute-start.29 = (bf16[256,3072]{1,0:T(8,128)(2,1)}, bf16[256,3072]{1,0:T(8,128)(2,1)}, u32[]{:S(2)}, u32[]{:S(2)}) collective-permute-start(bf16[256,3072]{1,0:T(8,128)(2,1)} %collective-permute-done.25.refs_3_), channel_id=1, source_target_pairs={{0,1},{1,0},{2,3},{3,2},{4,5},{5,4},{6,7},{7,6},{8,9},{9,8},{10,11... | collective-permute-start | bytes 4718600 | tf_op jit(solution)/shard_map/ppermute | solution.py:37
  147.3 20.6 %collective-permute-start.28 = (bf16[256,3072]{1,0:T(8,128)(2,1)}, bf16[256,3072]{1,0:T(8,128)(2,1)}, u32[]{:S(2)}, u32[]{:S(2)}) collective-permute-start(bf16[256,3072]{1,0:T(8,128)(2,1)} %collective-permute-done.24.refs_2_), channel_id=1, source_target_pairs={{0,1},{1,0},{2,3},{3,2},{4,5},{5,4},{6,7},{7,6},{8,9},{9,8},{10,11... | collective-permute-start | bytes 4718600 | tf_op jit(solution)/shard_map/ppermute | solution.py:37
  149.3 18.5 %all-to-all-start = ((bf16[16,192,128]{2,1,0:T(8,128)(2,1)}), bf16[16,192,128]{2,1,0:T(8,128)(2,1)}, u32[]{:S(2)}, u32[]{:S(2)}) async-start(bf16[16,192,128]{2,1,0:T(8,128)(2,1)} %bitcast.27), calls=%async_computation | async-start | bytes 1572864 | tf_op jit(solution)/shard_map/all_to_all | solution.py:425
  (14 other events, 179.3 us)

commit v4 on v3

--- a/solution.py
+++ b/solution.py
@@ -13,7 +13,7 @@
 WIN = 6
 AXES = ("x", "yh", "yl", "z", "c")
 SIZES = (4, 2, 2, 4, 2)
-VMEM = 60 * 1024 * 1024
+VMEM = 63 * 1024 * 1024
 MIXERS = [
     [((x * 4 + (yh ^ c) * 2 + yl) * 4 + z) * 2 + c for yh in range(2) for yl in range(2) for z in range(4)]
     for x in range(4)

time: 178 us -> 186 us (1.045)
  waiting for transfers between devices: 57.4 us -> 65.7 us
  starting transfers between devices: 50.3 us -> 44.2 us
  local copies, waits for them, and re-layouts: 7.66 us -> 10.9 us
  other arithmetic: 4.25 us -> 6.99 us
    ppermute x30, waiting for transfers between devices: 43.1 us -> 49.7 us  [move(): return lax.ppermute(value, AXES, pairs)]
    ppermute x30, starting transfers between devices: 46 us -> 40.5 us  [move(): return lax.ppermute(value, AXES, pairs)]
    concatenate x1, other arithmetic: 0.15 us -> 2.46 us  [per_device(): w_two = jnp.concatenate([w_rear, w_far]).reshape(2 * HD, D)]
    concatenate x1, other arithmetic: 0.15 us -> 2.44 us  [per_device(): w_one = jnp.concatenate([w_own, w_near]).reshape(2 * HD, D)]
    slice x1, local copies, waits for them, and re-layouts: 0.04 us -> 1.96 us  [per_device(): far_a = move(rear[:96], across(1))]
    unnamed x31 -> x23, local copies, waits for them, and re-layouts: 3.42 us -> 3.86 us
  transfers between devices with their start and end apart: 31 -> 31, of which waited for: 10 -> 11; matrix products, arithmetic and copies ran while one was open for 5% -> 7% of each run, Pallas kernels for 27% -> 26%
where the time goes in v4:
time: 186 us; the launch traced here: 185 us
  waiting for transfers between devices  65.7 us (35%)
  Pallas kernels  56.8 us (31%)
  starting transfers between devices  44.2 us (24%)
  local copies, waits for them, and re-layouts  10.9 us (6%)
  other arithmetic  6.99 us (4%)
    ppermute x30, waiting for transfers between devices, move(): return lax.ppermute(value, AXES, pairs)  49.7 us
    ppermute x30, starting transfers between devices, move(): return lax.ppermute(value, AXES, pairs)  40.5 us
    pallas_call x1, Pallas kernels, attend(): pl.pallas_call(body, out_shape=[jax.ShapeDtypeStruct((8, 3, 64, HD), jnp....  27 us
    pallas_call x2, Pallas kernels, project(): pl.pallas_call(body, out_shape=[jax.ShapeDtypeStruct((3, 4, 64, 384), jnp...  21.1 us
    all_to_all x1, waiting for transfers between devices, per_device(): lax.all_to_all(both.reshape(16, 192, HD), AXES, 0, 0, axis_index_groups=M...  15.9 us
    pallas_call x1, Pallas kernels, mix(): pl.pallas_call(mix_body, out_shape=jax.ShapeDtypeStruct((192, D), jnp.bfl...  8.76 us
    unnamed x23, local copies, waits for them, and re-layouts  3.86 us
  transfers between devices with their start and end apart: 31, of which 11 were waited for; matrix products, arithmetic and copies ran while one was open for 7% of the time, Pallas kernels for 26%

profile of v4, /device:TPU:0, one launch (start us, length us, event | category | flops | bytes accessed | tf_op | source)
XLA Modules:
  0.0 184.7 jit_solution(4939374001349859412)
XLA Ops:
  0.0 4.1 %collective-permute-start.1 = (bf16[192,3072]{1,0:T(8,128)(2,1)}, bf16[192,3072]{1,0:T(8,128)(2,1)}, u32[]{:S(2)}, u32[]{:S(2)}) collective-permute-start(bf16[192,3072]{1,0:T(8,128)(2,1)} %bitcast.25), channel_id=1, source_target_pairs={{0,6},{1,7},{2,4},{3,5},{4,2},{5,3},{6,0},{7,1},{8,14},{9,15},{10,... | collective-permute-start | bytes 3538952 | tf_op jit(solution)/shard_map/ppermute | solution.py:37
  5.5 1.9 %slice_bitcast_fusion = (bf16[1536,384]{1,0:T(8,128)(2,1)S(1)}, bf16[1536,384]{1,0:T(8,128)(2,1)S(1)}) fusion(bf16[3072,1,384]{2,0,1:T(8,128)(2,1)} %param.8), kind=kLoop, calls=%fused_computation.2 | loop fusion | bytes 4718592 | tf_op jit(solution)/shard_map/slice | solution.py:376
  7.3 4.7 %collective-permute-start.4 = (bf16[1536,384]{1,0:T(8,128)(2,1)S(1)}, bf16[1536,384]{1,0:T(8,128)(2,1)S(1)}, u32[]{:S(2)}, u32[]{:S(2)}) collective-permute-start(bf16[1536,384]{1,0:T(8,128)(2,1)S(1)} %get-tuple-element.57), channel_id=1, source_target_pairs={{0,24},{1,25},{2,26},{3,27},{4,28},{5,29},{6,30},{7,31},{8,0},{9,1... | collective-permute-start | bytes 3538952 | tf_op jit(solution)/shard_map/ppermute | solution.py:37
  12.1 19.0 %collective-permute-done.1.refs_3_ = bf16[192,3072]{1,0:T(8,128)(2,1)} collective-permute-done((bf16[192,3072]{1,0:T(8,128)(2,1)}, bf16[192,3072]{1,0:T(8,128)(2,1)}, u32[]{:S(2)}, u32[]{:S(2)}) %collective-permute-start.1) | collective-permute-done | bytes 1179680 | tf_op jit(solution)/shard_map/ppermute | solution.py:37
  32.5 4.4 %collective-permute-done.4.refs_6_.refs_8_ = bf16[1536,384]{1,0:T(8,128)(2,1)S(1)} collective-permute-done((bf16[1536,384]{1,0:T(8,128)(2,1)S(1)}, bf16[1536,384]{1,0:T(8,128)(2,1)S(1)}, u32[]{:S(2)}, u32[]{:S(2)}) %collective-permute-start.4) | collective-permute-done | bytes 1179680 | tf_op jit(solution)/shard_map/ppermute | solution.py:37
  38.0 2.6 %collective-permute-done.3.refs_5_.refs_7_ = bf16[1536,384]{1,0:T(8,128)(2,1)} collective-permute-done((bf16[1536,384]{1,0:T(8,128)(2,1)S(1)}, bf16[1536,384]{1,0:T(8,128)(2,1)}, u32[]{:S(2)}, u32[]{:S(2)}) %collective-permute-start.3) | collective-permute-done | bytes 1179680 | tf_op jit(solution)/shard_map/ppermute | solution.py:37
  40.6 2.0 %slice.34 = bf16[96,3072]{1,0:T(8,128)(2,1)} slice(bf16[192,3072]{1,0:T(8,128)(2,1)} %collective-permute-done.1.refs_3_), slice={[0:96], [0:3072]} | slice | bytes 1179648 | tf_op jit(solution)/shard_map/slice | solution.py:382
  42.5 2.0 %collective-permute-start.9 = (bf16[96,3072]{1,0:T(8,128)(2,1)}, bf16[96,3072]{1,0:T(8,128)(2,1)}, u32[]{:S(2)}, u32[]{:S(2)}) collective-permute-start(bf16[96,3072]{1,0:T(8,128)(2,1)} %slice.34), channel_id=1, source_target_pairs={{0,2},{1,3},{2,0},{3,1},{4,6},{5,7},{6,4},{7,5},{8,10},{9,11},{10,... | collective-permute-start | bytes 1769480 | tf_op jit(solution)/shard_map/ppermute | solution.py:37
  44.6 2.0 %slice.35 = bf16[96,3072]{1,0:T(8,128)(2,1)} slice(bf16[192,3072]{1,0:T(8,128)(2,1)} %collective-permute-done.refs_2_), slice={[96:192], [0:3072]} | slice | bytes 1179648 | tf_op jit(solution)/shard_map/slice | solution.py:383
  47.1 10.4 %project.2 = (bf16[3,4,64,384]{3,2,1,0:T(8,128)(2,1)}, bf16[3,4,64,384]{3,2,1,0:T(8,128)(2,1)}) custom-call(bf16[192,3072]{1,0:T(8,128)(2,1)} %bitcast.27, bf16[192,3072]{1,0:T(8,128)(2,1)} %copy-done.7, bf16[192,3072]{1,0:T(8,128)(2,1)} %collective-permute-done.refs_2_, bf16[192,3072]{1,0:T(8,128)(2,1)} %collective-permute-done.1.refs_3_, ...), custom_call_target="tpu_custom_call" | custom-call | flops 3623878656 | bytes 9437184 | tf_op jit(solution)/shard_map/project/pallas_call | solution.py:151
  57.7 4.0 %collective-permute-done.10.refs_3_ = bf16[96,3072]{1,0:T(8,128)(2,1)} collective-permute-done((bf16[96,3072]{1,0:T(8,128)(2,1)}, bf16[96,3072]{1,0:T(8,128)(2,1)}, u32[]{:S(2)}, u32[]{:S(2)}) %collective-permute-start.10) | collective-permute-done | bytes 589856 | tf_op jit(solution)/shard_map/ppermute | solution.py:37
  61.7 2.2 %collective-permute-done.12.refs_5_ = bf16[96,3072]{1,0:T(8,128)(2,1)S(1)} collective-permute-done((bf16[96,3072]{1,0:T(8,128)(2,1)}, bf16[96,3072]{1,0:T(8,128)(2,1)S(1)}, u32[]{:S(2)}, u32[]{:S(2)}) %collective-permute-start.12) | collective-permute-done | bytes 589856 | tf_op jit(solution)/shard_map/ppermute | solution.py:37
  66.1 5.9 %collective-permute-start.6 = (bf16[3,4,64,384]{3,2,1,0:T(8,128)(2,1)}, bf16[3,4,64,384]{3,2,1,0:T(8,128)(2,1)}, u32[]{:S(2)}, u32[]{:S(2)}) collective-permute-start(bf16[3,4,64,384]{3,2,1,0:T(8,128)(2,1)} %get-tuple-element.36), channel_id=1, source_target_pairs={{0,0},{1,16},{2,2},{3,18},{4,4},{5,20},{6,6},{7,22},{8,8},{9,24},{... | collective-permute-start | bytes 1769480 | tf_op jit(solution)/shard_map/ppermute | solution.py:37
  72.0 10.6 %project.3 = (bf16[3,4,64,384]{3,2,1,0:T(8,128)(2,1)}, bf16[3,4,64,384]{3,2,1,0:T(8,128)(2,1)}) custom-call(bf16[192,3072]{1,0:T(8,128)(2,1)} %collective-permute-done.7.refs_0_, bf16[192,3072]{1,0:T(8,128)(2,1)} %collective-permute-done.8.refs_1_, bf16[96,3072]{1,0:T(8,128)(2,1)} %collective-permute-done.9.refs_2_, ...), custom_call_target="tpu_custom_call" | custom-call | flops 3623878656 | bytes 9437184 | tf_op jit(solution)/shard_map/project/pallas_call | solution.py:151
  82.7 2.2 %collective-permute-done.15 = bf16[1,128,3072]{2,1,0:T(8,128)(2,1)} collective-permute-done((bf16[1,128,3072]{2,1,0:T(8,128)(2,1)S(1)}, bf16[1,128,3072]{2,1,0:T(8,128)(2,1)}, u32[]{:S(2)}, u32[]{:S(2)}) %collective-permute-start.15) | collective-permute-done | bytes 786464 | tf_op jit(solution)/shard_map/ppermute | solution.py:37
  84.8 1.9 %collective-permute-start.16 = (bf16[3,4,64,384]{3,2,1,0:T(8,128)(2,1)}, bf16[3,4,64,384]{3,2,1,0:T(8,128)(2,1)S(1)}, u32[]{:S(2)}, u32[]{:S(2)}) collective-permute-start(bf16[3,4,64,384]{3,2,1,0:T(8,128)(2,1)} %get-tuple-element.45), channel_id=1, source_target_pairs={{0,0},{1,16},{2,2},{3,18},{4,4},{5,20},{6,6},{7,22},{8,8},{9,24},{... | collective-permute-start | bytes 1769480 | tf_op jit(solution)/shard_map/ppermute | solution.py:37
  86.7 1.7 collective-permute-start.23
  90.8 1.6 collective-permute-start.20
  92.3 2.4 %collective-permute-start.18 = (bf16[2,3,4,64,256]{4,3,2,1,0:T(8,128)(2,1)S(1)}, bf16[2,3,4,64,256]{4,3,2,1,0:T(8,128)(2,1)}, u32[]{:S(2)}, u32[]{:S(2)}) collective-permute-start(bf16[2,3,4,64,256]{4,3,2,1,0:T(8,128)(2,1)S(1)} %pad_maximum_fusion.2), channel_id=1, source_target_pairs={{0,1},{1,0},{2,3},{3,2},{4,5},{5,4},{6,7},{7,6},{8,9},{9,8},{10,11... | collective-permute-start | bytes 2359304 | tf_op jit(solution)/shard_map/ppermute | solution.py:37
  94.7 8.2 %collective-permute-done.17.f1 = bf16[3,4,64,384]{3,2,1,0:T(8,128)(2,1)S(1)} collective-permute-done((bf16[3,4,64,384]{3,2,1,0:T(8,128)(2,1)}, bf16[3,4,64,384]{3,2,1,0:T(8,128)(2,1)S(1)}, u32[]{:S(2)}, u32[]{:S(2)}) %collective-permute-start.17) | collective-permute-done | bytes 589856 | tf_op jit(solution)/shard_map/ppermute | solution.py:37
  103.8 1.6 collective-permute-start.21
  105.3 2.9 %collective-permute-start.19 = (bf16[2,3,4,64,256]{4,3,2,1,0:T(8,128)(2,1)S(1)}, bf16[2,3,4,64,256]{4,3,2,1,0:T(8,128)(2,1)}, u32[]{:S(2)}, u32[]{:S(2)}) collective-permute-start(bf16[2,3,4,64,256]{4,3,2,1,0:T(8,128)(2,1)S(1)} %pad_maximum_fusion.3), channel_id=1, source_target_pairs={{0,1},{1,0},{2,3},{3,2},{4,5},{5,4},{6,7},{7,6},{8,9},{9,8},{10,11... | collective-permute-start | bytes 2359304 | tf_op jit(solution)/shard_map/ppermute | solution.py:37
  108.9 2.5 %pad_maximum_fusion.1 = bf16[2,128,3072]{2,1,0:T(8,128)(2,1)} fusion(bf16[1,128,3072]{2,1,0:T(8,128)(2,1)S(1)} %collective-permute-done.23, bf16[1,128,3072]{2,1,0:T(8,128)(2,1)} %collective-permute-done.15), kind=kLoop, calls=%fused_computation.1 | loop fusion | flops 786432 | bytes 3145728 | tf_op jit(solution)/shard_map/concatenate | solution.py:417
  111.4 2.1 %collective-permute-start.25 = (bf16[256,3072]{1,0:T(8,128)(2,1)}, bf16[256,3072]{1,0:T(8,128)(2,1)}, u32[]{:S(2)}, u32[]{:S(2)}) collective-permute-start(bf16[256,3072]{1,0:T(8,128)(2,1)} %bitcast.13.refs_1_), channel_id=1, source_target_pairs={{0,24},{1,25},{2,26},{3,27},{4,28},{5,29},{6,30},{7,31},{8,0},{9,1... | collective-permute-start | bytes 4718600 | tf_op jit(solution)/shard_map/ppermute | solution.py:37
  113.5 2.4 %pad_maximum_fusion = bf16[2,128,3072]{2,1,0:T(8,128)(2,1)} fusion(bf16[1,128,3072]{2,1,0:T(8,128)(2,1)} %collective-permute-done.14, bf16[1,128,3072]{2,1,0:T(8,128)(2,1)S(1)} %copy-done.2), kind=kLoop, calls=%fused_computation | loop fusion | flops 786432 | bytes 3145728 | tf_op jit(solution)/shard_map/concatenate | solution.py:416
  116.0 27.0 %attend.1 = (bf16[8,3,64,128]{3,2,1,0:T(8,128)(2,1)}, bf16[8,3,64,128]{3,2,1,0:T(8,128)(2,1)}) custom-call(bf16[3,4,64,384]{3,2,1,0:T(8,128)(2,1)} %collective-permute-done.6.n0, bf16[3,4,64,384]{3,2,1,0:T(8,128)(2,1)} %collective-permute-done.13.n1, bf16[3,4,64,384]{3,2,1,0:T(8,128)(2,1)} %copy-done.3, bf16[3,4,64,384]{3,2,1,0:T(8,128)(2,1)} %copy-done.4, ...), custom_call_target="tpu_custom_call" | custom-call | flops 32000000000 | bytes 6000000 | tf_op jit(solution)/shard_map/attend/pallas_call | solution.py:311
  143.0 4.0 %collective-permute-start.22 = (bf16[8,3,64,128]{3,2,1,0:T(8,128)(2,1)}, bf16[8,3,64,128]{3,2,1,0:T(8,128)(2,1)S(1)}, u32[]{:S(2)}, u32[]{:S(2)}) collective-permute-start(bf16[8,3,64,128]{3,2,1,0:T(8,128)(2,1)} %get-tuple-element.50), channel_id=1, source_target_pairs={{0,1},{1,0},{2,3},{3,2},{4,5},{5,4},{6,7},{7,6},{8,9},{9,8},{10,11... | collective-permute-start | bytes 1179656 | tf_op jit(solution)/shard_map/ppermute | solution.py:37
  148.9 4.6 %collective-permute-done.24.refs_2_ = bf16[256,3072]{1,0:T(8,128)(2,1)} collective-permute-done((bf16[256,3072]{1,0:T(8,128)(2,1)}, bf16[256,3072]{1,0:T(8,128)(2,1)}, u32[]{:S(2)}, u32[]{:S(2)}) %collective-permute-start.24) | collective-permute-done | bytes 1572896 | tf_op jit(solution)/shard_map/ppermute | solution.py:37
  153.5 1.9 %pad_maximum_fusion.4 = bf16[16,3,64,128]{3,2,1,0:T(8,128)(2,1)} fusion(bf16[8,3,64,128]{3,2,1,0:T(8,128)(2,1)S(1)} %collective-permute-done.22, bf16[8,3,64,128]{3,2,1,0:T(8,128)(2,1)} %get-tuple-element.49), kind=kLoop, calls=%fused_computation.6 | loop fusion | flops 393216 | bytes 1572864 | tf_op jit(solution)/shard_map/concatenate | solution.py:424
  155.5 3.6 %all-to-all-start = ((bf16[16,192,128]{2,1,0:T(8,128)(2,1)}), bf16[16,192,128]{2,1,0:T(8,128)(2,1)S(1)}, u32[]{:S(2)}, u32[]{:S(2)}) async-start(bf16[16,192,128]{2,1,0:T(8,128)(2,1)} %bitcast.10), calls=%async_computation | async-start | bytes 1572864 | tf_op jit(solution)/shard_map/all_to_all | solution.py:425
  159.1 15.9 %all-to-all-done = bf16[16,192,128]{2,1,0:T(8,128)(2,1)S(1)} async-done(((bf16[16,192,128]{2,1,0:T(8,128)(2,1)}), bf16[16,192,128]{2,1,0:T(8,128)(2,1)S(1)}, u32[]{:S(2)}, u32[]{:S(2)}) %all-to-all-start) | async-done | bytes 786464 | tf_op jit(solution)/shard_map/all_to_all | solution.py:425
  175.9 8.8 %mix.1 = bf16[192,3072]{1,0:T(8,128)(2,1)} custom-call(bf16[2,8,192,128]{3,2,1,0:T(8,128)(2,1)} %bitcast.21, bf16[256,3072]{1,0:T(8,128)(2,1)} %bitcast.12.refs_0_, bf16[256,3072]{1,0:T(8,128)(2,1)} %bitcast.13.refs_1_, bf16[256,3072]{1,0:T(8,128)(2,1)} %collective-permute-done.24.refs_2_, bf16[256,3072]{1,0:T(8,128)(2,1)} %collective-permute-done.25.refs_3_, ...), custom_call_target="tpu_custom_call" | custom-call | flops 2415919104 | bytes 14000000 | tf_op jit(solution)/shard_map/mix/pallas_call | solution.py:350
  (68 shorter events, 13.4 us)
Async XLA Ops:
  0.0 12.1 %collective-permute-start.2 = (bf16[192,3072]{1,0:T(8,128)(2,1)}, bf16[192,3072]{1,0:T(8,128)(2,1)S(1)}, u32[]{:S(2)}, u32[]{:S(2)}) collective-permute-start(bf16[192,3072]{1,0:T(8,128)(2,1)} %bitcast.24), channel_id=1, source_target_pairs={{0,1},{1,0},{2,3},{3,2},{4,5},{5,4},{6,7},{7,6},{8,9},{9,8},{10,11... | collective-permute-start | bytes 3538952 | tf_op jit(solution)/shard_map/ppermute | solution.py:37
  0.0 31.1 %collective-permute-start.1 = (bf16[192,3072]{1,0:T(8,128)(2,1)}, bf16[192,3072]{1,0:T(8,128)(2,1)}, u32[]{:S(2)}, u32[]{:S(2)}) collective-permute-start(bf16[192,3072]{1,0:T(8,128)(2,1)} %bitcast.25), channel_id=1, source_target_pairs={{0,6},{1,7},{2,4},{3,5},{4,2},{5,3},{6,0},{7,1},{8,14},{9,15},{10,... | collective-permute-start | bytes 3538952 | tf_op jit(solution)/shard_map/ppermute | solution.py:37
  4.1 28.4 %collective-permute-start = (bf16[192,3072]{1,0:T(8,128)(2,1)}, bf16[192,3072]{1,0:T(8,128)(2,1)}, u32[]{:S(2)}, u32[]{:S(2)}) collective-permute-start(bf16[192,3072]{1,0:T(8,128)(2,1)} %bitcast.26), channel_id=1, source_target_pairs={{0,2},{1,3},{2,0},{3,1},{4,6},{5,7},{6,4},{7,5},{8,10},{9,11},{10,... | collective-permute-start | bytes 3538952 | tf_op jit(solution)/shard_map/ppermute | solution.py:37
  4.1 7.9 %collective-permute-start.5 = (s32[1,3072]{1,0:T(1,128)}, s32[1,3072]{1,0:T(1,128)S(1)}, u32[]{:S(2)}, u32[]{:S(2)}) collective-permute-start(s32[1,3072]{1,0:T(1,128)} %param.12), channel_id=1, source_target_pairs={{0,0},{1,16},{2,2},{3,18},{4,4},{5,20},{6,6},{7,22},{8,8},{9,24},{... | collective-permute-start | bytes 36872 | tf_op jit(solution)/shard_map/ppermute | solution.py:37
  7.3 29.6 %collective-permute-start.4 = (bf16[1536,384]{1,0:T(8,128)(2,1)S(1)}, bf16[1536,384]{1,0:T(8,128)(2,1)S(1)}, u32[]{:S(2)}, u32[]{:S(2)}) collective-permute-start(bf16[1536,384]{1,0:T(8,128)(2,1)S(1)} %get-tuple-element.57), channel_id=1, source_target_pairs={{0,24},{1,25},{2,26},{3,27},{4,28},{5,29},{6,30},{7,31},{8,0},{9,1... | collective-permute-start | bytes 3538952 | tf_op jit(solution)/shard_map/ppermute | solution.py:37
  12.1 45.5 %copy-start.10 = (s32[1,3072]{1,0:T(1,128)}, s32[1,3072]{1,0:T(1,128)S(1)}, u32[]{:S(2)}) copy-start(s32[1,3072]{1,0:T(1,128)S(1)} %collective-permute-done.5.refs_5_) | copy-start | bytes 36868
  12.1 28.5 %collective-permute-start.3 = (bf16[1536,384]{1,0:T(8,128)(2,1)S(1)}, bf16[1536,384]{1,0:T(8,128)(2,1)}, u32[]{:S(2)}, u32[]{:S(2)}) collective-permute-start(bf16[1536,384]{1,0:T(8,128)(2,1)S(1)} %get-tuple-element.58), channel_id=1, source_target_pairs={{0,8},{1,9},{2,10},{3,11},{4,12},{5,13},{6,14},{7,15},{8,16},{9,17... | collective-permute-start | bytes 3538952 | tf_op jit(solution)/shard_map/ppermute | solution.py:37
  42.5 15.1 %collective-permute-start.9 = (bf16[96,3072]{1,0:T(8,128)(2,1)}, bf16[96,3072]{1,0:T(8,128)(2,1)}, u32[]{:S(2)}, u32[]{:S(2)}) collective-permute-start(bf16[96,3072]{1,0:T(8,128)(2,1)} %slice.34), channel_id=1, source_target_pairs={{0,2},{1,3},{2,0},{3,1},{4,6},{5,7},{6,4},{7,5},{8,10},{9,11},{10,... | collective-permute-start | bytes 1769480 | tf_op jit(solution)/shard_map/ppermute | solution.py:37
  46.5 15.2 %collective-permute-start.10 = (bf16[96,3072]{1,0:T(8,128)(2,1)}, bf16[96,3072]{1,0:T(8,128)(2,1)}, u32[]{:S(2)}, u32[]{:S(2)}) collective-permute-start(bf16[96,3072]{1,0:T(8,128)(2,1)} %slice.35), channel_id=1, source_target_pairs={{0,6},{1,7},{2,4},{3,5},{4,2},{5,3},{6,0},{7,1},{8,14},{9,15},{10,... | collective-permute-start | bytes 1769480 | tf_op jit(solution)/shard_map/ppermute | solution.py:37
  46.6 19.5 %collective-permute-start.7 = (bf16[192,3072]{1,0:T(8,128)(2,1)}, bf16[192,3072]{1,0:T(8,128)(2,1)}, u32[]{:S(2)}, u32[]{:S(2)}) collective-permute-start(bf16[192,3072]{1,0:T(8,128)(2,1)} %collective-permute-done.refs_2_), channel_id=1, source_target_pairs={{0,1},{1,0},{2,3},{3,2},{4,5},{5,4},{6,7},{7,6},{8,9},{9,8},{10,11... | collective-permute-start | bytes 3538952 | tf_op jit(solution)/shard_map/ppermute | solution.py:37
  46.6 25.4 %collective-permute-start.8 = (bf16[192,3072]{1,0:T(8,128)(2,1)}, bf16[192,3072]{1,0:T(8,128)(2,1)}, u32[]{:S(2)}, u32[]{:S(2)}) collective-permute-start(bf16[192,3072]{1,0:T(8,128)(2,1)} %collective-permute-done.1.refs_3_), channel_id=1, source_target_pairs={{0,1},{1,0},{2,3},{3,2},{4,5},{5,4},{6,7},{7,6},{8,9},{9,8},{10,11... | collective-permute-start | bytes 3538952 | tf_op jit(solution)/shard_map/ppermute | solution.py:37
  57.6 4.1 %collective-permute-start.11 = (bf16[96,3072]{1,0:T(8,128)(2,1)}, bf16[96,3072]{1,0:T(8,128)(2,1)S(1)}, u32[]{:S(2)}, u32[]{:S(2)}) collective-permute-start(bf16[96,3072]{1,0:T(8,128)(2,1)} %collective-permute-done.9.refs_2_), channel_id=1, source_target_pairs={{0,1},{1,0},{2,3},{3,2},{4,5},{5,4},{6,7},{7,6},{8,9},{9,8},{10,11... | collective-permute-start | bytes 1769480 | tf_op jit(solution)/shard_map/ppermute | solution.py:37
  61.7 2.2 %collective-permute-start.12 = (bf16[96,3072]{1,0:T(8,128)(2,1)}, bf16[96,3072]{1,0:T(8,128)(2,1)S(1)}, u32[]{:S(2)}, u32[]{:S(2)}) collective-permute-start(bf16[96,3072]{1,0:T(8,128)(2,1)} %collective-permute-done.10.refs_3_), channel_id=1, source_target_pairs={{0,1},{1,0},{2,3},{3,2},{4,5},{5,4},{6,7},{7,6},{8,9},{9,8},{10,11... | collective-permute-start | bytes 1769480 | tf_op jit(solution)/shard_map/ppermute | solution.py:37
  63.9 20.9 %collective-permute-start.15 = (bf16[1,128,3072]{2,1,0:T(8,128)(2,1)S(1)}, bf16[1,128,3072]{2,1,0:T(8,128)(2,1)}, u32[]{:S(2)}, u32[]{:S(2)}) collective-permute-start(bf16[1,128,3072]{2,1,0:T(8,128)(2,1)S(1)} %copy-done.2), channel_id=1, source_target_pairs={{0,6},{1,7},{2,4},{3,5},{4,2},{5,3},{6,0},{7,1},{8,14},{9,15},{10,... | collective-permute-start | bytes 2359304 | tf_op jit(solution)/shard_map/ppermute | solution.py:37
  64.8 20.0 %collective-permute-start.14 = (bf16[1,128,3072]{2,1,0:T(8,128)(2,1)S(1)}, bf16[1,128,3072]{2,1,0:T(8,128)(2,1)}, u32[]{:S(2)}, u32[]{:S(2)}) collective-permute-start(bf16[1,128,3072]{2,1,0:T(8,128)(2,1)S(1)} %copy-done.2), channel_id=1, source_target_pairs={{0,2},{1,3},{2,0},{3,1},{4,6},{5,7},{6,4},{7,5},{8,10},{9,11},{10,... | collective-permute-start | bytes 2359304 | tf_op jit(solution)/shard_map/ppermute | solution.py:37
  64.8 21.9 %collective-permute-start.13 = (bf16[3,4,64,384]{3,2,1,0:T(8,128)(2,1)}, bf16[3,4,64,384]{3,2,1,0:T(8,128)(2,1)}, u32[]{:S(2)}, u32[]{:S(2)}) collective-permute-start(bf16[3,4,64,384]{3,2,1,0:T(8,128)(2,1)} %get-tuple-element.41), channel_id=1, source_target_pairs={{0,8},{1,24},{2,10},{3,26},{4,12},{5,28},{6,14},{7,30},{8,0},{9,16... | collective-permute-start | bytes 1769480 | tf_op jit(solution)/shard_map/ppermute | solution.py:37
  66.1 20.6 %collective-permute-start.6 = (bf16[3,4,64,384]{3,2,1,0:T(8,128)(2,1)}, bf16[3,4,64,384]{3,2,1,0:T(8,128)(2,1)}, u32[]{:S(2)}, u32[]{:S(2)}) collective-permute-start(bf16[3,4,64,384]{3,2,1,0:T(8,128)(2,1)} %get-tuple-element.36), channel_id=1, source_target_pairs={{0,0},{1,16},{2,2},{3,18},{4,4},{5,20},{6,6},{7,22},{8,8},{9,24},{... | collective-permute-start | bytes 1769480 | tf_op jit(solution)/shard_map/ppermute | solution.py:37
  84.8 9.8 %collective-permute-start.16 = (bf16[3,4,64,384]{3,2,1,0:T(8,128)(2,1)}, bf16[3,4,64,384]{3,2,1,0:T(8,128)(2,1)S(1)}, u32[]{:S(2)}, u32[]{:S(2)}) collective-permute-start(bf16[3,4,64,384]{3,2,1,0:T(8,128)(2,1)} %get-tuple-element.45), channel_id=1, source_target_pairs={{0,0},{1,16},{2,2},{3,18},{4,4},{5,20},{6,6},{7,22},{8,8},{9,24},{... | collective-permute-start | bytes 1769480 | tf_op jit(solution)/shard_map/ppermute | solution.py:37
  86.7 22.2 %collective-permute-start.23 = (bf16[1,128,3072]{2,1,0:T(8,128)(2,1)S(1)}, bf16[1,128,3072]{2,1,0:T(8,128)(2,1)S(1)}, u32[]{:S(2)}, u32[]{:S(2)}) collective-permute-start(bf16[1,128,3072]{2,1,0:T(8,128)(2,1)S(1)} %copy-done.2), channel_id=1, source_target_pairs={{0,4},{1,5},{2,6},{3,7},{4,0},{5,1},{6,2},{7,3},{8,12},{9,13},{10,... | collective-permute-start | bytes 2359304 | tf_op jit(solution)/shard_map/ppermute | solution.py:37
  88.5 14.4 %collective-permute-start.17 = (bf16[3,4,64,384]{3,2,1,0:T(8,128)(2,1)}, bf16[3,4,64,384]{3,2,1,0:T(8,128)(2,1)S(1)}, u32[]{:S(2)}, u32[]{:S(2)}) collective-permute-start(bf16[3,4,64,384]{3,2,1,0:T(8,128)(2,1)} %get-tuple-element.47), channel_id=1, source_target_pairs={{0,8},{1,24},{2,10},{3,26},{4,12},{5,28},{6,14},{7,30},{8,0},{9,16... | collective-permute-start | bytes 1769480 | tf_op jit(solution)/shard_map/ppermute | solution.py:37
  90.8 25.2 %collective-permute-start.20 = (bf16[2,3,4,64,256]{4,3,2,1,0:T(8,128)(2,1)S(1)}, bf16[2,3,4,64,256]{4,3,2,1,0:T(8,128)(2,1)}, u32[]{:S(2)}, u32[]{:S(2)}) collective-permute-start(bf16[2,3,4,64,256]{4,3,2,1,0:T(8,128)(2,1)S(1)} %pad_maximum_fusion.2), channel_id=1, source_target_pairs={{1,32},{3,34},{5,36},{7,38},{9,40},{11,42},{13,44},{15,46},{17,48}... | collective-permute-start | bytes 2359304 | tf_op jit(solution)/shard_map/ppermute | solution.py:37
  92.3 23.6 %collective-permute-start.18 = (bf16[2,3,4,64,256]{4,3,2,1,0:T(8,128)(2,1)S(1)}, bf16[2,3,4,64,256]{4,3,2,1,0:T(8,128)(2,1)}, u32[]{:S(2)}, u32[]{:S(2)}) collective-permute-start(bf16[2,3,4,64,256]{4,3,2,1,0:T(8,128)(2,1)S(1)} %pad_maximum_fusion.2), channel_id=1, source_target_pairs={{0,1},{1,0},{2,3},{3,2},{4,5},{5,4},{6,7},{7,6},{8,9},{9,8},{10,11... | collective-permute-start | bytes 2359304 | tf_op jit(solution)/shard_map/ppermute | solution.py:37
  103.8 12.2 %collective-permute-start.21 = (bf16[2,3,4,64,256]{4,3,2,1,0:T(8,128)(2,1)S(1)}, bf16[2,3,4,64,256]{4,3,2,1,0:T(8,128)(2,1)}, u32[]{:S(2)}, u32[]{:S(2)}) collective-permute-start(bf16[2,3,4,64,256]{4,3,2,1,0:T(8,128)(2,1)S(1)} %pad_maximum_fusion.3), channel_id=1, source_target_pairs={{1,32},{3,34},{5,36},{7,38},{9,40},{11,42},{13,44},{15,46},{17,48}... | collective-permute-start | bytes 2359304 | tf_op jit(solution)/shard_map/ppermute | solution.py:37
  105.3 10.7 %collective-permute-start.19 = (bf16[2,3,4,64,256]{4,3,2,1,0:T(8,128)(2,1)S(1)}, bf16[2,3,4,64,256]{4,3,2,1,0:T(8,128)(2,1)}, u32[]{:S(2)}, u32[]{:S(2)}) collective-permute-start(bf16[2,3,4,64,256]{4,3,2,1,0:T(8,128)(2,1)S(1)} %pad_maximum_fusion.3), channel_id=1, source_target_pairs={{0,1},{1,0},{2,3},{3,2},{4,5},{5,4},{6,7},{7,6},{8,9},{9,8},{10,11... | collective-permute-start | bytes 2359304 | tf_op jit(solution)/shard_map/ppermute | solution.py:37
  111.4 37.2 %collective-permute-start.25 = (bf16[256,3072]{1,0:T(8,128)(2,1)}, bf16[256,3072]{1,0:T(8,128)(2,1)}, u32[]{:S(2)}, u32[]{:S(2)}) collective-permute-start(bf16[256,3072]{1,0:T(8,128)(2,1)} %bitcast.13.refs_1_), channel_id=1, source_target_pairs={{0,24},{1,25},{2,26},{3,27},{4,28},{5,29},{6,30},{7,31},{8,0},{9,1... | collective-permute-start | bytes 4718600 | tf_op jit(solution)/shard_map/ppermute | solution.py:37
  116.0 37.6 %collective-permute-start.24 = (bf16[256,3072]{1,0:T(8,128)(2,1)}, bf16[256,3072]{1,0:T(8,128)(2,1)}, u32[]{:S(2)}, u32[]{:S(2)}) collective-permute-start(bf16[256,3072]{1,0:T(8,128)(2,1)} %bitcast.12.refs_0_), channel_id=1, source_target_pairs={{0,8},{1,9},{2,10},{3,11},{4,12},{5,13},{6,14},{7,15},{8,16},{9,17... | collective-permute-start | bytes 4718600 | tf_op jit(solution)/shard_map/ppermute | solution.py:37
  143.0 5.6 %collective-permute-start.22 = (bf16[8,3,64,128]{3,2,1,0:T(8,128)(2,1)}, bf16[8,3,64,128]{3,2,1,0:T(8,128)(2,1)S(1)}, u32[]{:S(2)}, u32[]{:S(2)}) collective-permute-start(bf16[8,3,64,128]{3,2,1,0:T(8,128)(2,1)} %get-tuple-element.50), channel_id=1, source_target_pairs={{0,1},{1,0},{2,3},{3,2},{4,5},{5,4},{6,7},{7,6},{8,9},{9,8},{10,11... | collective-permute-start | bytes 1179656 | tf_op jit(solution)/shard_map/ppermute | solution.py:37
  147.0 12.1 %collective-permute-start.27 = (bf16[256,3072]{1,0:T(8,128)(2,1)}, bf16[256,3072]{1,0:T(8,128)(2,1)S(1)}, u32[]{:S(2)}, u32[]{:S(2)}) collective-permute-start(bf16[256,3072]{1,0:T(8,128)(2,1)} %bitcast.13.refs_1_), channel_id=1, source_target_pairs={{0,1},{1,0},{2,3},{3,2},{4,5},{5,4},{6,7},{7,6},{8,9},{9,8},{10,11... | collective-permute-start | bytes 4718600 | tf_op jit(solution)/shard_map/ppermute | solution.py:37
  147.1 12.1 %collective-permute-start.26 = (bf16[256,3072]{1,0:T(8,128)(2,1)}, bf16[256,3072]{1,0:T(8,128)(2,1)}, u32[]{:S(2)}, u32[]{:S(2)}) collective-permute-start(bf16[256,3072]{1,0:T(8,128)(2,1)} %bitcast.12.refs_0_), channel_id=1, source_target_pairs={{0,1},{1,0},{2,3},{3,2},{4,5},{5,4},{6,7},{7,6},{8,9},{9,8},{10,11... | collective-permute-start | bytes 4718600 | tf_op jit(solution)/shard_map/ppermute | solution.py:37
  148.5 26.5 %collective-permute-start.29 = (bf16[256,3072]{1,0:T(8,128)(2,1)}, bf16[256,3072]{1,0:T(8,128)(2,1)}, u32[]{:S(2)}, u32[]{:S(2)}) collective-permute-start(bf16[256,3072]{1,0:T(8,128)(2,1)} %collective-permute-done.25.refs_3_), channel_id=1, source_target_pairs={{0,1},{1,0},{2,3},{3,2},{4,5},{5,4},{6,7},{7,6},{8,9},{9,8},{10,11... | collective-permute-start | bytes 4718600 | tf_op jit(solution)/shard_map/ppermute | solution.py:37
  153.5 21.5 %collective-permute-start.28 = (bf16[256,3072]{1,0:T(8,128)(2,1)}, bf16[256,3072]{1,0:T(8,128)(2,1)}, u32[]{:S(2)}, u32[]{:S(2)}) collective-permute-start(bf16[256,3072]{1,0:T(8,128)(2,1)} %collective-permute-done.24.refs_2_), channel_id=1, source_target_pairs={{0,1},{1,0},{2,3},{3,2},{4,5},{5,4},{6,7},{7,6},{8,9},{9,8},{10,11... | collective-permute-start | bytes 4718600 | tf_op jit(solution)/shard_map/ppermute | solution.py:37
  155.5 19.6 %all-to-all-start = ((bf16[16,192,128]{2,1,0:T(8,128)(2,1)}), bf16[16,192,128]{2,1,0:T(8,128)(2,1)S(1)}, u32[]{:S(2)}, u32[]{:S(2)}) async-start(bf16[16,192,128]{2,1,0:T(8,128)(2,1)} %bitcast.10), calls=%async_computation | async-start | bytes 1572864 | tf_op jit(solution)/shard_map/all_to_all | solution.py:425
  (10 other events, 99.3 us)

commit v5 on v4

--- a/solution.py
+++ b/solution.py
@@ -13,7 +13,7 @@
 WIN = 6
 AXES = ("x", "yh", "yl", "z", "c")
 SIZES = (4, 2, 2, 4, 2)
-VMEM = 63 * 1024 * 1024
+VMEM = 40 * 1024 * 1024
 MIXERS = [
     [((x * 4 + (yh ^ c) * 2 + yl) * 4 + z) * 2 + c for yh in range(2) for yl in range(2) for z in range(4)]
     for x in range(4)

time: 186 us -> 172 us (0.925)
  local copies, waits for them, and re-layouts: 10.9 us -> 2.35 us
  Pallas kernels: 56.8 us -> 48.8 us
  waiting for transfers between devices: 65.7 us -> 70.7 us
  other arithmetic: 6.99 us -> 3.22 us
  starting transfers between devices: 44.2 us -> 46.3 us
    ppermute x30, waiting for transfers between devices: 49.7 us -> 57 us  [move(): return lax.ppermute(value, AXES, pairs)]
    pallas_call x2, Pallas kernels: 21.1 us -> 15 us  [project(): pl.pallas_call(body, out_shape=[jax.ShapeDtypeStruct((3, 4, 64, 384), jnp...]
    unnamed x23 -> x35, local copies, waits for them, and re-layouts: 3.86 us -> 0.17 us
    concatenate x1, other arithmetic: 2.46 us -> 0.15 us  [per_device(): w_two = jnp.concatenate([w_rear, w_far]).reshape(2 * HD, D)]
    concatenate x1, other arithmetic: 2.44 us -> 0.15 us  [per_device(): w_one = jnp.concatenate([w_own, w_near]).reshape(2 * HD, D)]
    all_to_all x1, waiting for transfers between devices: 15.9 us -> 13.7 us  [per_device(): lax.all_to_all(both.reshape(16, 192, HD), AXES, 0, 0, axis_index_groups=M...]
    slice x1, local copies, waits for them, and re-layouts: 1.97 us -> 0.04 us  [per_device(): far_b = move(near[96:], across(3))]
    slice x1, local copies, waits for them, and re-layouts: 1.96 us -> 0.04 us  [per_device(): far_a = move(rear[:96], across(1))]
  transfers between devices with their start and end apart: 31 -> 31, of which waited for: 11 -> 13; matrix products, arithmetic and copies ran while one was open for 7% -> 3% of each run, Pallas kernels for 26% -> 24%
where the time goes in v5:
time: 172 us
  waiting for transfers between devices  70.7 us (41%)
  Pallas kernels  48.8 us (28%)
  starting transfers between devices  46.3 us (27%)
  other arithmetic  3.22 us (2%)
  local copies, waits for them, and re-layouts  2.35 us (1%)
    ppermute x30, waiting for transfers between devices, move(): return lax.ppermute(value, AXES, pairs)  57 us
    ppermute x30, starting transfers between devices, move(): return lax.ppermute(value, AXES, pairs)  42 us
    pallas_call x1, Pallas kernels, attend(): pl.pallas_call(body, out_shape=[jax.ShapeDtypeStruct((8, 3, 64, HD), jnp....  25.8 us
    pallas_call x2, Pallas kernels, project(): pl.pallas_call(body, out_shape=[jax.ShapeDtypeStruct((3, 4, 64, 384), jnp...  15 us
    all_to_all x1, waiting for transfers between devices, per_device(): lax.all_to_all(both.reshape(16, 192, HD), AXES, 0, 0, axis_index_groups=M...  13.7 us
    pallas_call x1, Pallas kernels, mix(): pl.pallas_call(mix_body, out_shape=jax.ShapeDtypeStruct((192, D), jnp.bfl...  7.95 us
    all_to_all x1, starting transfers between devices, per_device(): lax.all_to_all(both.reshape(16, 192, HD), AXES, 0, 0, axis_index_groups=M...  4.29 us
  transfers between devices with their start and end apart: 31, of which 13 were waited for; matrix products, arithmetic and copies ran while one was open for 3% of the time, Pallas kernels for 24%

profile of v5, /device:TPU:0, one launch (start us, length us, event | category | flops | bytes accessed | tf_op | source)
XLA Modules:
  0.0 171.7 jit_solution(8417475958144714367)
XLA Ops:
  0.0 4.1 %collective-permute-start.1 = (bf16[192,3072]{1,0:T(8,128)(2,1)}, bf16[192,3072]{1,0:T(8,128)(2,1)S(1)}, u32[]{:S(2)}, u32[]{:S(2)}) collective-permute-start(bf16[192,3072]{1,0:T(8,128)(2,1)} %bitcast.30), channel_id=1, source_target_pairs={{0,6},{1,7},{2,4},{3,5},{4,2},{5,3},{6,0},{7,1},{8,14},{9,15},{10,... | collective-permute-start | bytes 3538952 | tf_op jit(solution)/shard_map/ppermute | solution.py:37
  4.1 1.4 collective-permute-start.5
  5.5 2.0 %slice_bitcast_fusion = (bf16[1536,384]{1,0:T(8,128)(2,1)S(1)}, bf16[1536,384]{1,0:T(8,128)(2,1)S(1)}) fusion(bf16[3072,1,384]{2,0,1:T(8,128)(2,1)} %param.8), kind=kLoop, calls=%fused_computation.2 | loop fusion | bytes 4718592 | tf_op jit(solution)/shard_map/slice | solution.py:376
  7.5 4.7 %collective-permute-start.4 = (bf16[1536,384]{1,0:T(8,128)(2,1)S(1)}, bf16[1536,384]{1,0:T(8,128)(2,1)S(1)}, u32[]{:S(2)}, u32[]{:S(2)}) collective-permute-start(bf16[1536,384]{1,0:T(8,128)(2,1)S(1)} %get-tuple-element.57), channel_id=1, source_target_pairs={{0,24},{1,25},{2,26},{3,27},{4,28},{5,29},{6,30},{7,31},{8,0},{9,1... | collective-permute-start | bytes 3538952 | tf_op jit(solution)/shard_map/ppermute | solution.py:37
  12.2 18.8 %collective-permute-done.1.refs_3_ = bf16[192,3072]{1,0:T(8,128)(2,1)S(1)} collective-permute-done((bf16[192,3072]{1,0:T(8,128)(2,1)}, bf16[192,3072]{1,0:T(8,128)(2,1)S(1)}, u32[]{:S(2)}, u32[]{:S(2)}) %collective-permute-start.1) | collective-permute-done | bytes 1179680 | tf_op jit(solution)/shard_map/ppermute | solution.py:37
  31.0 1.5 collective-permute-done.refs_2_
  32.4 4.7 %collective-permute-done.4.refs_6_.refs_8_ = bf16[1536,384]{1,0:T(8,128)(2,1)S(1)} collective-permute-done((bf16[1536,384]{1,0:T(8,128)(2,1)S(1)}, bf16[1536,384]{1,0:T(8,128)(2,1)S(1)}, u32[]{:S(2)}, u32[]{:S(2)}) %collective-permute-start.4) | collective-permute-done | bytes 1179680 | tf_op jit(solution)/shard_map/ppermute | solution.py:37
  37.1 3.5 %collective-permute-done.3.refs_5_.refs_7_ = bf16[1536,384]{1,0:T(8,128)(2,1)S(1)} collective-permute-done((bf16[1536,384]{1,0:T(8,128)(2,1)S(1)}, bf16[1536,384]{1,0:T(8,128)(2,1)S(1)}, u32[]{:S(2)}, u32[]{:S(2)}) %collective-permute-start.3) | collective-permute-done | bytes 1179680 | tf_op jit(solution)/shard_map/ppermute | solution.py:37
  40.6 2.1 %collective-permute-start.9 = (bf16[96,3072]{1,0:T(8,128)(2,1)S(1)}, bf16[96,3072]{1,0:T(8,128)(2,1)S(1)}, u32[]{:S(2)}, u32[]{:S(2)}) collective-permute-start(bf16[96,3072]{1,0:T(8,128)(2,1)S(1)} %slice.34), channel_id=1, source_target_pairs={{0,2},{1,3},{2,0},{3,1},{4,6},{5,7},{6,4},{7,5},{8,10},{9,11},{10,... | collective-permute-start | bytes 1769480 | tf_op jit(solution)/shard_map/ppermute | solution.py:37
  43.5 7.5 %project.2 = (bf16[3,4,64,384]{3,2,1,0:T(8,128)(2,1)S(1)}, bf16[3,4,64,384]{3,2,1,0:T(8,128)(2,1)S(1)}) custom-call(bf16[192,3072]{1,0:T(8,128)(2,1)S(1)} %bitcast.32, bf16[192,3072]{1,0:T(8,128)(2,1)S(1)} %collective-permute-done.2.refs_1_, bf16[192,3072]{1,0:T(8,128)(2,1)S(1)} %collective-permute-done.refs_2_, ...), custom_call_target="tpu_custom_call" | custom-call | flops 3623878656 | bytes 9437184 | tf_op jit(solution)/shard_map/project/pallas_call | solution.py:151
  51.0 4.0 %collective-permute-done.9.refs_2_ = bf16[96,3072]{1,0:T(8,128)(2,1)S(1)} collective-permute-done((bf16[96,3072]{1,0:T(8,128)(2,1)S(1)}, bf16[96,3072]{1,0:T(8,128)(2,1)S(1)}, u32[]{:S(2)}, u32[]{:S(2)}) %collective-permute-start.9) | collective-permute-done | bytes 589856 | tf_op jit(solution)/shard_map/ppermute | solution.py:37
  54.9 2.8 %collective-permute-done.10.refs_3_ = bf16[96,3072]{1,0:T(8,128)(2,1)S(1)} collective-permute-done((bf16[96,3072]{1,0:T(8,128)(2,1)S(1)}, bf16[96,3072]{1,0:T(8,128)(2,1)S(1)}, u32[]{:S(2)}, u32[]{:S(2)}) %collective-permute-start.10) | collective-permute-done | bytes 589856 | tf_op jit(solution)/shard_map/ppermute | solution.py:37
  57.7 2.0 %collective-permute-done.12.refs_5_ = bf16[96,3072]{1,0:T(8,128)(2,1)S(1)} collective-permute-done((bf16[96,3072]{1,0:T(8,128)(2,1)S(1)}, bf16[96,3072]{1,0:T(8,128)(2,1)S(1)}, u32[]{:S(2)}, u32[]{:S(2)}) %collective-permute-start.12) | collective-permute-done | bytes 589856 | tf_op jit(solution)/shard_map/ppermute | solution.py:37
  60.0 1.5 collective-permute-start.13
  62.4 7.5 %project.3 = (bf16[3,4,64,384]{3,2,1,0:T(8,128)(2,1)S(1)}, bf16[3,4,64,384]{3,2,1,0:T(8,128)(2,1)S(1)}) custom-call(bf16[192,3072]{1,0:T(8,128)(2,1)S(1)} %collective-permute-done.7.refs_0_, bf16[192,3072]{1,0:T(8,128)(2,1)S(1)} %collective-permute-done.8.refs_1_, bf16[96,3072]{1,0:T(8,128)(2,1)S(1)} %collective-permute-done.9.refs_2_, ...), custom_call_target="tpu_custom_call" | custom-call | flops 3623878656 | bytes 9437184 | tf_op jit(solution)/shard_map/project/pallas_call | solution.py:151
  70.0 10.5 %collective-permute-done.15 = bf16[1,128,3072]{2,1,0:T(8,128)(2,1)S(1)} collective-permute-done((bf16[1,128,3072]{2,1,0:T(8,128)(2,1)S(1)}, bf16[1,128,3072]{2,1,0:T(8,128)(2,1)S(1)}, u32[]{:S(2)}, u32[]{:S(2)}) %collective-permute-start.15) | collective-permute-done | bytes 786464 | tf_op jit(solution)/shard_map/ppermute | solution.py:37
  81.3 1.5 collective-permute-start.23
  82.8 1.3 collective-permute-start.17
  84.2 1.0 pad_maximum_fusion.2
  85.2 1.6 collective-permute-start.20
  86.7 3.4 %collective-permute-start.18 = (bf16[2,3,4,64,256]{4,3,2,1,0:T(8,128)(2,1)}, bf16[2,3,4,64,256]{4,3,2,1,0:T(8,128)(2,1)}, u32[]{:S(2)}, u32[]{:S(2)}) collective-permute-start(bf16[2,3,4,64,256]{4,3,2,1,0:T(8,128)(2,1)} %pad_maximum_fusion.2), channel_id=1, source_target_pairs={{0,1},{1,0},{2,3},{3,2},{4,5},{5,4},{6,7},{7,6},{8,9},{9,8},{10,11... | collective-permute-start | bytes 2359304 | tf_op jit(solution)/shard_map/ppermute | solution.py:37
  90.1 7.2 %collective-permute-done.17.f1 = bf16[3,4,64,384]{3,2,1,0:T(8,128)(2,1)S(1)} collective-permute-done((bf16[3,4,64,384]{3,2,1,0:T(8,128)(2,1)S(1)}, bf16[3,4,64,384]{3,2,1,0:T(8,128)(2,1)S(1)}, u32[]{:S(2)}, u32[]{:S(2)}) %collective-permute-start.17) | collective-permute-done | bytes 589856 | tf_op jit(solution)/shard_map/ppermute | solution.py:37
  97.3 1.0 pad_maximum_fusion.3
  98.4 1.5 collective-permute-start.21
  99.9 4.0 %collective-permute-start.19 = (bf16[2,3,4,64,256]{4,3,2,1,0:T(8,128)(2,1)}, bf16[2,3,4,64,256]{4,3,2,1,0:T(8,128)(2,1)}, u32[]{:S(2)}, u32[]{:S(2)}) collective-permute-start(bf16[2,3,4,64,256]{4,3,2,1,0:T(8,128)(2,1)} %pad_maximum_fusion.3), channel_id=1, source_target_pairs={{0,1},{1,0},{2,3},{3,2},{4,5},{5,4},{6,7},{7,6},{8,9},{9,8},{10,11... | collective-permute-start | bytes 2359304 | tf_op jit(solution)/shard_map/ppermute | solution.py:37
  104.2 1.8 %collective-permute-start.25 = (bf16[256,3072]{1,0:T(8,128)(2,1)S(1)}, bf16[256,3072]{1,0:T(8,128)(2,1)}, u32[]{:S(2)}, u32[]{:S(2)}) collective-permute-start(bf16[256,3072]{1,0:T(8,128)(2,1)S(1)} %bitcast.21), channel_id=1, source_target_pairs={{0,24},{1,25},{2,26},{3,27},{4,28},{5,29},{6,30},{7,31},{8,0},{9,1... | collective-permute-start | bytes 4718600 | tf_op jit(solution)/shard_map/ppermute | solution.py:37
  106.6 25.8 %attend.1 = (bf16[8,3,64,128]{3,2,1,0:T(8,128)(2,1)S(1)}, bf16[8,3,64,128]{3,2,1,0:T(8,128)(2,1)S(1)}) custom-call(bf16[3,4,64,384]{3,2,1,0:T(8,128)(2,1)S(1)} %copy-done.8, bf16[3,4,64,384]{3,2,1,0:T(8,128)(2,1)S(1)} %copy-done.6, bf16[3,4,64,384]{3,2,1,0:T(8,128)(2,1)S(1)} %copy-done.2, bf16[3,4,64,384]{3,2,1,0:T(8,128)(2,1)S(1)} %copy-done.4, ...), custom_call_target="tpu_custom_call" | custom-call | flops 32000000000 | bytes 6000000 | tf_op jit(solution)/shard_map/attend/pallas_call | solution.py:311
  132.4 9.3 %collective-permute-start.22 = (bf16[8,3,64,128]{3,2,1,0:T(8,128)(2,1)S(1)}, bf16[8,3,64,128]{3,2,1,0:T(8,128)(2,1)S(1)}, u32[]{:S(2)}, u32[]{:S(2)}) collective-permute-start(bf16[8,3,64,128]{3,2,1,0:T(8,128)(2,1)S(1)} %get-tuple-element.50), channel_id=1, source_target_pairs={{0,1},{1,0},{2,3},{3,2},{4,5},{5,4},{6,7},{7,6},{8,9},{9,8},{10,11... | collective-permute-start | bytes 1179656 | tf_op jit(solution)/shard_map/ppermute | solution.py:37
  144.6 4.3 %all-to-all-start = ((bf16[16,192,128]{2,1,0:T(8,128)(2,1)}), bf16[16,192,128]{2,1,0:T(8,128)(2,1)}, u32[]{:S(2)}, u32[]{:S(2)}) async-start(bf16[16,192,128]{2,1,0:T(8,128)(2,1)} %bitcast.37), calls=%async_computation | async-start | bytes 1572864 | tf_op jit(solution)/shard_map/all_to_all | solution.py:425
  148.9 1.1 collective-permute-done.26.refs_4_
  150.0 13.7 %all-to-all-done = bf16[16,192,128]{2,1,0:T(8,128)(2,1)} async-done(((bf16[16,192,128]{2,1,0:T(8,128)(2,1)}), bf16[16,192,128]{2,1,0:T(8,128)(2,1)}, u32[]{:S(2)}, u32[]{:S(2)}) %all-to-all-start) | async-done | bytes 786464 | tf_op jit(solution)/shard_map/all_to_all | solution.py:425
  163.7 7.9 %mix.1 = bf16[192,3072]{1,0:T(8,128)(2,1)} custom-call(bf16[2,8,192,128]{3,2,1,0:T(8,128)(2,1)} %bitcast.11.attn, bf16[256,3072]{1,0:T(8,128)(2,1)S(1)} %bitcast.26, bf16[256,3072]{1,0:T(8,128)(2,1)S(1)} %bitcast.23, bf16[256,3072]{1,0:T(8,128)(2,1)} %collective-permute-done.24.refs_2_, bf16[256,3072]{1,0:T(8,128)(2,1)} %collective-permute-done.25.refs_3_, ...), custom_call_target="tpu_custom_call" | custom-call | flops 2415919104 | bytes 14000000 | tf_op jit(solution)/shard_map/mix/pallas_call | solution.py:350
  (80 shorter events, 6.4 us)
Async XLA Ops:
  0.0 12.2 %collective-permute-start.2 = (bf16[192,3072]{1,0:T(8,128)(2,1)}, bf16[192,3072]{1,0:T(8,128)(2,1)S(1)}, u32[]{:S(2)}, u32[]{:S(2)}) collective-permute-start(bf16[192,3072]{1,0:T(8,128)(2,1)} %bitcast.29), channel_id=1, source_target_pairs={{0,1},{1,0},{2,3},{3,2},{4,5},{5,4},{6,7},{7,6},{8,9},{9,8},{10,11... | collective-permute-start | bytes 3538952 | tf_op jit(solution)/shard_map/ppermute | solution.py:37
  0.0 31.0 %collective-permute-start.1 = (bf16[192,3072]{1,0:T(8,128)(2,1)}, bf16[192,3072]{1,0:T(8,128)(2,1)S(1)}, u32[]{:S(2)}, u32[]{:S(2)}) collective-permute-start(bf16[192,3072]{1,0:T(8,128)(2,1)} %bitcast.30), channel_id=1, source_target_pairs={{0,6},{1,7},{2,4},{3,5},{4,2},{5,3},{6,0},{7,1},{8,14},{9,15},{10,... | collective-permute-start | bytes 3538952 | tf_op jit(solution)/shard_map/ppermute | solution.py:37
  4.1 28.3 %collective-permute-start = (bf16[192,3072]{1,0:T(8,128)(2,1)}, bf16[192,3072]{1,0:T(8,128)(2,1)S(1)}, u32[]{:S(2)}, u32[]{:S(2)}) collective-permute-start(bf16[192,3072]{1,0:T(8,128)(2,1)} %bitcast.31), channel_id=1, source_target_pairs={{0,2},{1,3},{2,0},{3,1},{4,6},{5,7},{6,4},{7,5},{8,10},{9,11},{10,... | collective-permute-start | bytes 3538952 | tf_op jit(solution)/shard_map/ppermute | solution.py:37
  4.1 8.1 %collective-permute-start.5 = (s32[1,3072]{1,0:T(1,128)}, s32[1,3072]{1,0:T(1,128)S(1)}, u32[]{:S(2)}, u32[]{:S(2)}) collective-permute-start(s32[1,3072]{1,0:T(1,128)} %param.12), channel_id=1, source_target_pairs={{0,0},{1,16},{2,2},{3,18},{4,4},{5,20},{6,6},{7,22},{8,8},{9,24},{... | collective-permute-start | bytes 36872 | tf_op jit(solution)/shard_map/ppermute | solution.py:37
  5.5 38.0 %copy-start.9 = (bf16[4,2,24,3072]{3,2,1,0:T(8,128)(2,1)S(1)}, bf16[4,2,24,3072]{3,2,1,0:T(8,128)(2,1)}, u32[]{:S(2)}) copy-start(bf16[4,2,24,3072]{3,2,1,0:T(8,128)(2,1)} %param.7) | copy-start | bytes 3538948
  7.5 29.6 %collective-permute-start.4 = (bf16[1536,384]{1,0:T(8,128)(2,1)S(1)}, bf16[1536,384]{1,0:T(8,128)(2,1)S(1)}, u32[]{:S(2)}, u32[]{:S(2)}) collective-permute-start(bf16[1536,384]{1,0:T(8,128)(2,1)S(1)} %get-tuple-element.57), channel_id=1, source_target_pairs={{0,24},{1,25},{2,26},{3,27},{4,28},{5,29},{6,30},{7,31},{8,0},{9,1... | collective-permute-start | bytes 3538952 | tf_op jit(solution)/shard_map/ppermute | solution.py:37
  12.2 28.4 %collective-permute-start.3 = (bf16[1536,384]{1,0:T(8,128)(2,1)S(1)}, bf16[1536,384]{1,0:T(8,128)(2,1)S(1)}, u32[]{:S(2)}, u32[]{:S(2)}) collective-permute-start(bf16[1536,384]{1,0:T(8,128)(2,1)S(1)} %get-tuple-element.58), channel_id=1, source_target_pairs={{0,8},{1,9},{2,10},{3,11},{4,12},{5,13},{6,14},{7,15},{8,16},{9,17... | collective-permute-start | bytes 3538952 | tf_op jit(solution)/shard_map/ppermute | solution.py:37
  40.6 14.3 %collective-permute-start.9 = (bf16[96,3072]{1,0:T(8,128)(2,1)S(1)}, bf16[96,3072]{1,0:T(8,128)(2,1)S(1)}, u32[]{:S(2)}, u32[]{:S(2)}) collective-permute-start(bf16[96,3072]{1,0:T(8,128)(2,1)S(1)} %slice.34), channel_id=1, source_target_pairs={{0,2},{1,3},{2,0},{3,1},{4,6},{5,7},{6,4},{7,5},{8,10},{9,11},{10,... | collective-permute-start | bytes 1769480 | tf_op jit(solution)/shard_map/ppermute | solution.py:37
  42.8 14.9 %collective-permute-start.10 = (bf16[96,3072]{1,0:T(8,128)(2,1)S(1)}, bf16[96,3072]{1,0:T(8,128)(2,1)S(1)}, u32[]{:S(2)}, u32[]{:S(2)}) collective-permute-start(bf16[96,3072]{1,0:T(8,128)(2,1)S(1)} %slice.35), channel_id=1, source_target_pairs={{0,6},{1,7},{2,4},{3,5},{4,2},{5,3},{6,0},{7,1},{8,14},{9,15},{10,... | collective-permute-start | bytes 1769480 | tf_op jit(solution)/shard_map/ppermute | solution.py:37
  43.0 18.6 %collective-permute-start.7 = (bf16[192,3072]{1,0:T(8,128)(2,1)S(1)}, bf16[192,3072]{1,0:T(8,128)(2,1)S(1)}, u32[]{:S(2)}, u32[]{:S(2)}) collective-permute-start(bf16[192,3072]{1,0:T(8,128)(2,1)S(1)} %collective-permute-done.refs_2_), channel_id=1, source_target_pairs={{0,1},{1,0},{2,3},{3,2},{4,5},{5,4},{6,7},{7,6},{8,9},{9,8},{10,11... | collective-permute-start | bytes 3538952 | tf_op jit(solution)/shard_map/ppermute | solution.py:37
  43.0 19.5 %collective-permute-start.8 = (bf16[192,3072]{1,0:T(8,128)(2,1)S(1)}, bf16[192,3072]{1,0:T(8,128)(2,1)S(1)}, u32[]{:S(2)}, u32[]{:S(2)}) collective-permute-start(bf16[192,3072]{1,0:T(8,128)(2,1)S(1)} %collective-permute-done.1.refs_3_), channel_id=1, source_target_pairs={{0,1},{1,0},{2,3},{3,2},{4,5},{5,4},{6,7},{7,6},{8,9},{9,8},{10,11... | collective-permute-start | bytes 3538952 | tf_op jit(solution)/shard_map/ppermute | solution.py:37
  54.9 2.8 %collective-permute-start.11 = (bf16[96,3072]{1,0:T(8,128)(2,1)S(1)}, bf16[96,3072]{1,0:T(8,128)(2,1)S(1)}, u32[]{:S(2)}, u32[]{:S(2)}) collective-permute-start(bf16[96,3072]{1,0:T(8,128)(2,1)S(1)} %collective-permute-done.9.refs_2_), channel_id=1, source_target_pairs={{0,1},{1,0},{2,3},{3,2},{4,5},{5,4},{6,7},{7,6},{8,9},{9,8},{10,11... | collective-permute-start | bytes 1769480 | tf_op jit(solution)/shard_map/ppermute | solution.py:37
  57.7 2.0 %collective-permute-start.12 = (bf16[96,3072]{1,0:T(8,128)(2,1)S(1)}, bf16[96,3072]{1,0:T(8,128)(2,1)S(1)}, u32[]{:S(2)}, u32[]{:S(2)}) collective-permute-start(bf16[96,3072]{1,0:T(8,128)(2,1)S(1)} %collective-permute-done.10.refs_3_), channel_id=1, source_target_pairs={{0,1},{1,0},{2,3},{3,2},{4,5},{5,4},{6,7},{7,6},{8,9},{9,8},{10,11... | collective-permute-start | bytes 1769480 | tf_op jit(solution)/shard_map/ppermute | solution.py:37
  59.7 20.8 %collective-permute-start.15 = (bf16[1,128,3072]{2,1,0:T(8,128)(2,1)S(1)}, bf16[1,128,3072]{2,1,0:T(8,128)(2,1)S(1)}, u32[]{:S(2)}, u32[]{:S(2)}) collective-permute-start(bf16[1,128,3072]{2,1,0:T(8,128)(2,1)S(1)} %copy-done.12), channel_id=1, source_target_pairs={{0,6},{1,7},{2,4},{3,5},{4,2},{5,3},{6,0},{7,1},{8,14},{9,15},{10,... | collective-permute-start | bytes 2359304 | tf_op jit(solution)/shard_map/ppermute | solution.py:37
  60.0 20.5 %collective-permute-start.14 = (bf16[1,128,3072]{2,1,0:T(8,128)(2,1)S(1)}, bf16[1,128,3072]{2,1,0:T(8,128)(2,1)S(1)}, u32[]{:S(2)}, u32[]{:S(2)}) collective-permute-start(bf16[1,128,3072]{2,1,0:T(8,128)(2,1)S(1)} %copy-done.12), channel_id=1, source_target_pairs={{0,2},{1,3},{2,0},{3,1},{4,6},{5,7},{6,4},{7,5},{8,10},{9,11},{10,... | collective-permute-start | bytes 2359304 | tf_op jit(solution)/shard_map/ppermute | solution.py:37
  60.0 21.2 %collective-permute-start.13 = (bf16[3,4,64,384]{3,2,1,0:T(8,128)(2,1)S(1)}, bf16[3,4,64,384]{3,2,1,0:T(8,128)(2,1)S(1)}, u32[]{:S(2)}, u32[]{:S(2)}) collective-permute-start(bf16[3,4,64,384]{3,2,1,0:T(8,128)(2,1)S(1)} %get-tuple-element.41), channel_id=1, source_target_pairs={{0,8},{1,24},{2,10},{3,26},{4,12},{5,28},{6,14},{7,30},{8,0},{9,16... | collective-permute-start | bytes 1769480 | tf_op jit(solution)/shard_map/ppermute | solution.py:37
  61.6 19.7 %collective-permute-start.6 = (bf16[3,4,64,384]{3,2,1,0:T(8,128)(2,1)S(1)}, bf16[3,4,64,384]{3,2,1,0:T(8,128)(2,1)S(1)}, u32[]{:S(2)}, u32[]{:S(2)}) collective-permute-start(bf16[3,4,64,384]{3,2,1,0:T(8,128)(2,1)S(1)} %get-tuple-element.36), channel_id=1, source_target_pairs={{0,0},{1,16},{2,2},{3,18},{4,4},{5,20},{6,6},{7,22},{8,8},{9,24},{... | collective-permute-start | bytes 1769480 | tf_op jit(solution)/shard_map/ppermute | solution.py:37
  80.5 9.6 %collective-permute-start.16 = (bf16[3,4,64,384]{3,2,1,0:T(8,128)(2,1)S(1)}, bf16[3,4,64,384]{3,2,1,0:T(8,128)(2,1)S(1)}, u32[]{:S(2)}, u32[]{:S(2)}) collective-permute-start(bf16[3,4,64,384]{3,2,1,0:T(8,128)(2,1)S(1)} %get-tuple-element.45), channel_id=1, source_target_pairs={{0,0},{1,16},{2,2},{3,18},{4,4},{5,20},{6,6},{7,22},{8,8},{9,24},{... | collective-permute-start | bytes 1769480 | tf_op jit(solution)/shard_map/ppermute | solution.py:37
  81.3 22.7 %collective-permute-start.23 = (bf16[1,128,3072]{2,1,0:T(8,128)(2,1)S(1)}, bf16[1,128,3072]{2,1,0:T(8,128)(2,1)S(1)}, u32[]{:S(2)}, u32[]{:S(2)}) collective-permute-start(bf16[1,128,3072]{2,1,0:T(8,128)(2,1)S(1)} %copy-done.12), channel_id=1, source_target_pairs={{0,4},{1,5},{2,6},{3,7},{4,0},{5,1},{6,2},{7,3},{8,12},{9,13},{10,... | collective-permute-start | bytes 2359304 | tf_op jit(solution)/shard_map/ppermute | solution.py:37
  82.8 14.5 %collective-permute-start.17 = (bf16[3,4,64,384]{3,2,1,0:T(8,128)(2,1)S(1)}, bf16[3,4,64,384]{3,2,1,0:T(8,128)(2,1)S(1)}, u32[]{:S(2)}, u32[]{:S(2)}) collective-permute-start(bf16[3,4,64,384]{3,2,1,0:T(8,128)(2,1)S(1)} %get-tuple-element.47), channel_id=1, source_target_pairs={{0,8},{1,24},{2,10},{3,26},{4,12},{5,28},{6,14},{7,30},{8,0},{9,16... | collective-permute-start | bytes 1769480 | tf_op jit(solution)/shard_map/ppermute | solution.py:37
  85.2 21.0 %collective-permute-start.20 = (bf16[2,3,4,64,256]{4,3,2,1,0:T(8,128)(2,1)}, bf16[2,3,4,64,256]{4,3,2,1,0:T(8,128)(2,1)}, u32[]{:S(2)}, u32[]{:S(2)}) collective-permute-start(bf16[2,3,4,64,256]{4,3,2,1,0:T(8,128)(2,1)} %pad_maximum_fusion.2), channel_id=1, source_target_pairs={{1,32},{3,34},{5,36},{7,38},{9,40},{11,42},{13,44},{15,46},{17,48}... | collective-permute-start | bytes 2359304 | tf_op jit(solution)/shard_map/ppermute | solution.py:37
  86.7 19.8 %collective-permute-start.18 = (bf16[2,3,4,64,256]{4,3,2,1,0:T(8,128)(2,1)}, bf16[2,3,4,64,256]{4,3,2,1,0:T(8,128)(2,1)}, u32[]{:S(2)}, u32[]{:S(2)}) collective-permute-start(bf16[2,3,4,64,256]{4,3,2,1,0:T(8,128)(2,1)} %pad_maximum_fusion.2), channel_id=1, source_target_pairs={{0,1},{1,0},{2,3},{3,2},{4,5},{5,4},{6,7},{7,6},{8,9},{9,8},{10,11... | collective-permute-start | bytes 2359304 | tf_op jit(solution)/shard_map/ppermute | solution.py:37
  98.4 8.2 %collective-permute-start.21 = (bf16[2,3,4,64,256]{4,3,2,1,0:T(8,128)(2,1)}, bf16[2,3,4,64,256]{4,3,2,1,0:T(8,128)(2,1)}, u32[]{:S(2)}, u32[]{:S(2)}) collective-permute-start(bf16[2,3,4,64,256]{4,3,2,1,0:T(8,128)(2,1)} %pad_maximum_fusion.3), channel_id=1, source_target_pairs={{1,32},{3,34},{5,36},{7,38},{9,40},{11,42},{13,44},{15,46},{17,48}... | collective-permute-start | bytes 2359304 | tf_op jit(solution)/shard_map/ppermute | solution.py:37
  99.9 6.6 %collective-permute-start.19 = (bf16[2,3,4,64,256]{4,3,2,1,0:T(8,128)(2,1)}, bf16[2,3,4,64,256]{4,3,2,1,0:T(8,128)(2,1)}, u32[]{:S(2)}, u32[]{:S(2)}) collective-permute-start(bf16[2,3,4,64,256]{4,3,2,1,0:T(8,128)(2,1)} %pad_maximum_fusion.3), channel_id=1, source_target_pairs={{0,1},{1,0},{2,3},{3,2},{4,5},{5,4},{6,7},{7,6},{8,9},{9,8},{10,11... | collective-permute-start | bytes 2359304 | tf_op jit(solution)/shard_map/ppermute | solution.py:37
  104.2 38.9 %collective-permute-start.25 = (bf16[256,3072]{1,0:T(8,128)(2,1)S(1)}, bf16[256,3072]{1,0:T(8,128)(2,1)}, u32[]{:S(2)}, u32[]{:S(2)}) collective-permute-start(bf16[256,3072]{1,0:T(8,128)(2,1)S(1)} %bitcast.21), channel_id=1, source_target_pairs={{0,24},{1,25},{2,26},{3,27},{4,28},{5,29},{6,30},{7,31},{8,0},{9,1... | collective-permute-start | bytes 4718600 | tf_op jit(solution)/shard_map/ppermute | solution.py:37
  106.2 37.4 %collective-permute-start.24 = (bf16[256,3072]{1,0:T(8,128)(2,1)S(1)}, bf16[256,3072]{1,0:T(8,128)(2,1)}, u32[]{:S(2)}, u32[]{:S(2)}) collective-permute-start(bf16[256,3072]{1,0:T(8,128)(2,1)S(1)} %bitcast.24), channel_id=1, source_target_pairs={{0,8},{1,9},{2,10},{3,11},{4,12},{5,13},{6,14},{7,15},{8,16},{9,17... | collective-permute-start | bytes 4718600 | tf_op jit(solution)/shard_map/ppermute | solution.py:37
  132.4 10.7 %collective-permute-start.22 = (bf16[8,3,64,128]{3,2,1,0:T(8,128)(2,1)S(1)}, bf16[8,3,64,128]{3,2,1,0:T(8,128)(2,1)S(1)}, u32[]{:S(2)}, u32[]{:S(2)}) collective-permute-start(bf16[8,3,64,128]{3,2,1,0:T(8,128)(2,1)S(1)} %get-tuple-element.50), channel_id=1, source_target_pairs={{0,1},{1,0},{2,3},{3,2},{4,5},{5,4},{6,7},{7,6},{8,9},{9,8},{10,11... | collective-permute-start | bytes 1179656 | tf_op jit(solution)/shard_map/ppermute | solution.py:37
  141.7 7.1 %collective-permute-start.27 = (bf16[256,3072]{1,0:T(8,128)(2,1)S(1)}, bf16[256,3072]{1,0:T(8,128)(2,1)}, u32[]{:S(2)}, u32[]{:S(2)}) collective-permute-start(bf16[256,3072]{1,0:T(8,128)(2,1)S(1)} %bitcast.22), channel_id=1, source_target_pairs={{0,1},{1,0},{2,3},{3,2},{4,5},{5,4},{6,7},{7,6},{8,9},{9,8},{10,11... | collective-permute-start | bytes 4718600 | tf_op jit(solution)/shard_map/ppermute | solution.py:37
  141.8 8.1 %collective-permute-start.26 = (bf16[256,3072]{1,0:T(8,128)(2,1)S(1)}, bf16[256,3072]{1,0:T(8,128)(2,1)}, u32[]{:S(2)}, u32[]{:S(2)}) collective-permute-start(bf16[256,3072]{1,0:T(8,128)(2,1)S(1)} %bitcast.25), channel_id=1, source_target_pairs={{0,1},{1,0},{2,3},{3,2},{4,5},{5,4},{6,7},{7,6},{8,9},{9,8},{10,11... | collective-permute-start | bytes 4718600 | tf_op jit(solution)/shard_map/ppermute | solution.py:37
  143.1 20.6 %collective-permute-start.29 = (bf16[256,3072]{1,0:T(8,128)(2,1)}, bf16[256,3072]{1,0:T(8,128)(2,1)}, u32[]{:S(2)}, u32[]{:S(2)}) collective-permute-start(bf16[256,3072]{1,0:T(8,128)(2,1)} %collective-permute-done.25.refs_3_), channel_id=1, source_target_pairs={{0,1},{1,0},{2,3},{3,2},{4,5},{5,4},{6,7},{7,6},{8,9},{9,8},{10,11... | collective-permute-start | bytes 4718600 | tf_op jit(solution)/shard_map/ppermute | solution.py:37
  143.6 20.1 %collective-permute-start.28 = (bf16[256,3072]{1,0:T(8,128)(2,1)}, bf16[256,3072]{1,0:T(8,128)(2,1)}, u32[]{:S(2)}, u32[]{:S(2)}) collective-permute-start(bf16[256,3072]{1,0:T(8,128)(2,1)} %collective-permute-done.24.refs_2_), channel_id=1, source_target_pairs={{0,1},{1,0},{2,3},{3,2},{4,5},{5,4},{6,7},{7,6},{8,9},{9,8},{10,11... | collective-permute-start | bytes 4718600 | tf_op jit(solution)/shard_map/ppermute | solution.py:37
  144.6 19.2 %all-to-all-start = ((bf16[16,192,128]{2,1,0:T(8,128)(2,1)}), bf16[16,192,128]{2,1,0:T(8,128)(2,1)}, u32[]{:S(2)}, u32[]{:S(2)}) async-start(bf16[16,192,128]{2,1,0:T(8,128)(2,1)} %bitcast.37), calls=%async_computation | async-start | bytes 1572864 | tf_op jit(solution)/shard_map/all_to_all | solution.py:425
  (16 other events, 179.9 us)
